TPU v7x, 32 devices: a whole 2x2x4 slice. The times are simulated.
32 devices in a mesh: dp: 8 (over z, y), ctx: 4 (over x, core).
Axes of the slice: x: 2, y: 2, z: 4, core: 2. Of those that a mesh axis runs over, the one named last changes fastest.
Arguments:
- layer_input: float32 [8, 512, 1024], P('dp', 'ctx'), may hold values from -6 to 6
- segment_ids: int32 [8, 512], P('dp'), may hold values from 0 to 2, never falling along the last dimension, each value on 1 to 384 neighbouring positions
- ln1_gain: float32 [1024], replicated, may hold values from 0.1 to 1.9
- ln1_bias: float32 [1024], replicated, may hold values from -3 to 3
- w_qkv: bfloat16 [1024, 3072], P('dp', 'ctx')
- qv_bias: float32 [2048], replicated, may hold values from -3 to 3
- w_out: bfloat16 [1024, 1024], P('dp', 'ctx'), may hold values from -0.75 to 0.75
- out_bias: float32 [1024], replicated, may hold values from -3 to 3
- ln2_gain: float32 [1024], replicated, may hold values from 0.1 to 1.9
- ln2_bias: float32 [1024], replicated, may hold values from -3 to 3
- w_up: bfloat16 [1024, 4096], P('dp', 'ctx'), may hold values from -0.1875 to 0.1875
- up_bias: float32 [4096], replicated, may hold values from -3 to 3
- w_down: bfloat16 [4096, 1024], P('dp', 'ctx'), may hold values from -0.09375 to 0.09375
- down_bias: float32 [1024], replicated, may hold values from -3 to 3
- cotangent: float32 [8, 512, 1024], P('dp', 'ctx'), may hold values from -6 to 6
Outputs:
- result: float32 [8, 512, 1024], P('dp', 'ctx')
- input_grad: float32 [8, 512, 1024], P('dp', 'ctx')
- ln1_gain_grad: float32 [1024], replicated
- ln1_bias_grad: float32 [1024], replicated
- w_qkv_grad: float32 [1024, 3072], P('dp', 'ctx')
- qv_bias_grad: float32 [2048], replicated
- w_out_grad: float32 [1024, 1024], P('dp', 'ctx')
- out_bias_grad: float32 [1024], replicated
- ln2_gain_grad: float32 [1024], replicated
- ln2_bias_grad: float32 [1024], replicated
- w_up_grad: float32 [1024, 4096], P('dp', 'ctx')
- up_bias_grad: float32 [4096], replicated
- w_down_grad: float32 [4096, 1024], P('dp', 'ctx')
- down_bias_grad: float32 [1024], replicated
Inputs may be any that keep to these rules, and one draw needn't show every extreme that they name: `segment_ids`: segment ids never fall along a sequence; every document holds 1 to 384 tokens and one of each sequence holds exactly that many.
All inputs are finite; a program needn't handle non-finite values.
Results may differ from a plain program's by a relative error of at most 0.017.
Values may be sent and summed in bfloat16 or wider, within the bound.
No kernel may reach another device: no remote copies, remote signals or barrier semaphores. Data moves between devices by JAX's collectives and lax.ppermute only.
A program may use at most 192 MiB of HBM per device.

v0:
```python
import math

import jax
import jax.numpy as jnp
from jax import lax
from jax.experimental import pallas as pl
from jax.experimental.pallas import tpu as pltpu
from jax.sharding import PartitionSpec as P

HEADS = 16
HEAD_DIM = 64

epsilon = 1e-05
gelu_scale = 0.7978845608028654
cubic_term = 0.044715
neg_large = -1e30
BF = jnp.bfloat16
F32 = jnp.float32


def layer_norm(values, gain, offset):
    center = jnp.mean(values, axis=-1, keepdims=True)
    centered = values - center
    variance = jnp.mean(centered * centered, axis=-1, keepdims=True)
    inv_std = lax.rsqrt(variance + epsilon)
    normed = centered * inv_std
    return (normed * gain + offset, normed, inv_std)


def norm_backward(upstream, normed, inv_std, gain):
    scaled = upstream * gain
    return inv_std * (
        scaled
        - jnp.mean(scaled, axis=-1, keepdims=True)
        - normed * jnp.mean(scaled * normed, axis=-1, keepdims=True)
    )


def gelu_both(values):
    square = values * values
    tangent = jnp.tanh(gelu_scale * (values + cubic_term * values * square))
    forward = 0.5 * values * (1.0 + tangent)
    slope = 0.5 * (1.0 + tangent) + 0.5 * values * (1.0 - tangent * tangent) * gelu_scale * (
        1.0 + 3.0 * cubic_term * square
    )
    return forward, slope


def dot(a, b):
    return jnp.dot(a, b, preferred_element_type=F32)


def dot_nt(a, b):
    return lax.dot_general(a, b, (((1,), (1,)), ((), ())), preferred_element_type=F32)


def dot_tn(a, b):
    return lax.dot_general(a, b, (((0,), (0,)), ((), ())), preferred_element_type=F32)


def pick(stack, index):
    return lax.dynamic_index_in_dim(stack, index, 0, keepdims=False)


def ctx_bits(count):
    bits = []
    bit = count // 2
    while bit:
        bits.append(bit)
        bit //= 2
    return bits


def ctx_order(count):
    order = [0]
    for bit in ctx_bits(count):
        order = order + [r | bit for r in order]
    return order


def ctx_swap(x, bit):
    count = lax.axis_size("ctx")
    return lax.ppermute(x, "ctx", [(i, i ^ bit) for i in range(count)])


def gather_step(pieces, bit):
    return pieces + [ctx_swap(p, bit) for p in pieces]


def ctx_gather(x):
    pieces = [x]
    for bit in ctx_bits(lax.axis_size("ctx")):
        pieces = gather_step(pieces, bit)
    return jnp.concatenate(pieces, axis=0)


def ctx_scatter(x):
    for bit in reversed(ctx_bits(lax.axis_size("ctx"))):
        half = x.shape[0] // 2
        x = x[:half] + ctx_swap(x[half:].astype(BF), bit).astype(F32)
    return x


def exchange_step(pieces, bit):
    pieces = list(pieces)
    slots = [r for r in range(len(pieces)) if r & bit]
    got = ctx_swap(jnp.stack([pieces[r] for r in slots]), bit)
    for i, r in enumerate(slots):
        pieces[r] = got[i]
    return pieces


def ctx_exchange(pieces):
    for bit in ctx_bits(lax.axis_size("ctx")):
        pieces = exchange_step(pieces, bit)
    return pieces


def trade(near, far):
    count = 2 * near.shape[0]
    if count == 4:
        got = ctx_swap(far, 2)
        return [(near, 0), (ctx_swap(near, 1), 1), (got, 0), (ctx_swap(got, 1), 1)]
    pieces = ctx_exchange([*near, *far])
    return [(piece[None], 0) for piece in pieces]


def put_piece(near_ref, far_ref, r, value):
    half = near_ref.shape[0]
    (near_ref if r < half else far_ref)[r % half] = value


def put_piece_at(near_ref, far_ref, slot, value):
    half = near_ref.shape[0]

    @pl.when(slot < half)
    def _():
        near_ref[slot] = value

    @pl.when(slot >= half)
    def _():
        far_ref[slot - half] = value


def piece_shapes(ctx, rows, width):
    return [((ctx // 2, rows, width), BF)] * 2


def owned(ids, pieces, k):
    value = pieces[0]
    for r in range(1, len(pieces)):
        value = jnp.where(ids[0] == (k ^ r), pieces[r], value)
    return value


def by_owner(pieces, me, axis):
    stack = jnp.stack(pieces)
    return jnp.concatenate([pick(stack, me ^ k) for k in range(len(pieces))], axis=axis)


def dp_shape(count):
    z_count = 4 if count % 4 == 0 else count
    return z_count, count // z_count


def ring_z(x):
    count = lax.axis_size("dp")
    _, y_count = dp_shape(count)
    return lax.ppermute(x, "dp", [(i, (i + y_count) % count) for i in range(count)])


def ring_y(x):
    count = lax.axis_size("dp")
    _, y_count = dp_shape(count)
    return lax.ppermute(
        x, "dp", [(i, i // y_count * y_count + (i + 1) % y_count) for i in range(count)]
    )


def along_y(x):
    row = [x]
    for _ in range(dp_shape(lax.axis_size("dp"))[1] - 1):
        row.append(ring_y(row[-1]))
    return row


def dp_places(reverse=False):
    count = lax.axis_size("dp")
    z_count, y_count = dp_shape(count)
    me = lax.axis_index("dp")
    z, y = me // y_count, me % y_count
    places = []
    for s in range(z_count):
        for t in range(y_count):
            places.append((z + z_count - s) % z_count * y_count + (y + y_count - t) % y_count)
    return places


def after(x, *earlier):
    return lax.optimization_barrier((x, *earlier))[0]


def call(kernel, outs, args, scalars=1, scratch=(), work=0, earlier=(), far=()):
    used = len(args)
    sizes = [(x.shape, x.dtype) for x in args] + list(outs) + [(x.shape, x.dtype) for x in scratch]
    held = sum(math.prod(shape) * jnp.dtype(dtype).itemsize for shape, dtype in sizes)
    limit = held * 5 // 4 + work + 4 * 2**20
    first_out = used + len(earlier)
    fetched = [pltpu.VMEM(args[i].shape, args[i].dtype) for i in far]
    if far:
        fetched.append(pltpu.SemaphoreType.DMA((len(far),)))

    def body(*refs):
        ins, rest = list(refs[:used]), refs[first_out:]
        if far:
            rest, buffers, sem = rest[: -len(far) - 1], rest[-len(far) - 1 : -1], rest[-1]
            copies = [
                pltpu.make_async_copy(ins[i], buffer, sem.at[j])
                for j, (i, buffer) in enumerate(zip(far, buffers))
            ]
            for copy in copies:
                copy.start()
            for copy in copies:
                copy.wait()
            for i, buffer in zip(far, buffers):
                ins[i] = buffer
        kernel(*ins, *rest)

    def space(i):
        if i in far:
            return pltpu.HBM
        return pltpu.SMEM if i < scalars else pl.ANY if i >= used else pltpu.VMEM

    return pl.pallas_call(
        body,
        out_shape=[jax.ShapeDtypeStruct(shape, dtype) for shape, dtype in outs],
        in_specs=[pl.BlockSpec(memory_space=space(i)) for i in range(first_out)],
        out_specs=[pl.BlockSpec(memory_space=pltpu.VMEM)] * len(outs),
        scratch_shapes=[*scratch, *fetched],
        compiler_params=pltpu.CompilerParams(vmem_limit_bytes=limit),
    )(*args, *earlier)


def assemble(full, blocks, places, cuts):
    count, held = len(blocks), len(cuts)
    shapes = [cut(jnp.zeros(blocks[0].shape, BF)).shape for cut in cuts]
    total = lax.axis_size("dp")

    def kernel(place_ref, *refs):
        outs = refs[-held:]
        for i in range(count):
            for out_ref, cut, (rows, _) in zip(outs, cuts, shapes):
                at = pl.multiple_of(place_ref[i] * rows, rows)
                out_ref[pl.ds(at, rows), :] = cut(refs[i])

    return pl.pallas_call(
        kernel,
        out_shape=[jax.ShapeDtypeStruct((total * rows, width), BF) for rows, width in shapes],
        in_specs=[pl.BlockSpec(memory_space=pltpu.SMEM)]
        + [pl.BlockSpec(memory_space=pltpu.VMEM)] * (count + (held if full else 0)),
        out_specs=[pl.BlockSpec(memory_space=pltpu.VMEM)] * held,
        input_output_aliases={1 + count + j: j for j in range(held)} if full else {},
        compiler_params=pltpu.CompilerParams(
            vmem_limit_bytes=4 * 2**20 + 6 * sum(total * rows * width for rows, width in shapes)
        ),
    )(jnp.stack(places).astype(jnp.int32), *blocks, *(full or []))


def dp_bits():
    bits = []
    bit = 1
    while bit < lax.axis_size("dp"):
        bits.append(bit)
        bit *= 2
    return bits


def slot_order(bits):
    order = [0]
    for bit in reversed(bits):
        order = order + [r | bit for r in order]
    return order


def grad_blocks(ids, left_ref, right, keep_ref, *send_refs):
    half, rows = keep_ref.shape[:2]
    bits = []
    while 2 ** len(bits) < 2 * half:
        bits.append(2 ** len(bits))
    ranges = [(keep_ref, 0)]
    for ref in send_refs[::-1]:
        ranges.append((ref, ranges[-1][1] + ranges[-1][0].shape[0]))
    for k in range(2 * half):
        block = dot_tn(left_ref[:, k * rows : (k + 1) * rows], right).astype(BF)
        name = jnp.bitwise_xor(ids[1], k)
        slot = 0
        for i, bit in enumerate(bits):
            slot = slot + lax.div(jnp.bitwise_and(name, bit), bit) * (half >> i)
        for ref, first in ranges:

            @pl.when((slot >= first) & (slot < first + ref.shape[0]))
            def _():
                ref[slot - first] = block


def block_shapes(dps, rows, width, parts):
    half = dps // 2
    counts = [half] + ([half] if parts == 1 else [half - half // 2, half // 2])
    return [((n, rows, width), BF) for n in counts]


def dp_swap(x, bit):
    count = lax.axis_size("dp")
    return lax.ppermute(x, "dp", [(i, i ^ bit) for i in range(count)])


def combine(terms, start, count, outs, write, earlier=()):

    def kernel(ids, *refs):
        for i in range(count):
            total = refs[0][start - terms[0][1] + i].astype(F32)
            for ref, (_, first) in zip(refs[1 : len(terms)], terms[1:]):
                total = total + ref[start - first + i].astype(F32)
            write(ids, i, total, refs[len(terms) :])

    ids = lax.axis_index("ctx").astype(jnp.int32)[None]
    return call(kernel, outs, [ids] + [array for array, _ in terms], earlier=earlier)


class Reduction:

    def __init__(self, blocks):
        keep, *sends = blocks
        self.bits = dp_bits()
        self.size = keep.shape[0]
        bit = self.bits.pop(0)
        got = [dp_swap(send, bit) for send in sends]
        self.first = [(keep, 0), (got[0], self.size - got[0].shape[0])]
        self.terms = [(keep, 0), (got[-1], 0)]

    def step(self, *earlier):
        self.size //= 2
        terms, self.first = self.first or self.terms, None

        def write(ids, i, block, refs):
            refs[0][i] = block.astype(BF)

        shape = (self.size,) + terms[0][0].shape[1:]
        (send,) = combine(terms, self.size, self.size, [(shape, BF)], write, earlier)
        self.terms.append((dp_swap(send, self.bits.pop(0)), 0))
        return send

    def result(self, outs, write, *earlier):
        return combine(self.terms, 0, 1, outs, write, earlier)


def sync(reductions, *values):
    held = [([a for a, _ in r.first or []], [a for a, _ in r.terms]) for r in reductions]
    held, values = lax.optimization_barrier((held, values))
    for r, (first, terms) in zip(reductions, held):
        if r.first:
            r.first = [(a, at) for a, (_, at) in zip(first, r.first)]
        r.terms = [(a, at) for a, (_, at) in zip(terms, r.terms)]
    return values


def unit_pieces(w_up, w_down, c, sub, unit):
    ctx, dps = lax.axis_size("ctx"), lax.axis_size("dp")
    down_view = w_down.reshape(ctx, sub, unit)
    up_view = jnp.moveaxis(w_up.reshape(w_up.shape[0], dps // ctx, ctx, sub), 2, 0).reshape(
        ctx, sub, unit
    )
    return [jnp.stack([pick(up_view, c ^ r), pick(down_view, c ^ r)]) for r in range(ctx)]


def join_units(pieces, c, up_rows):
    unit_up = by_owner([p[0].reshape(up_rows, -1) for p in pieces], c, 1)
    unit_down = by_owner([p[1] for p in pieces], c, 1)
    return jnp.stack([unit_up.reshape(unit_down.shape), unit_down])


def store_block(ids, i, block, refs):
    refs[0][...] = block


def column_pieces(ctx):

    def write(ids, i, block, refs):
        part = block.shape[1] // ctx
        for k in range(ctx):
            value = block[:, k * part : (k + 1) * part].astype(BF)
            put_piece_at(*refs, jnp.bitwise_xor(ids[0], k), value)

    return write


def kind_pieces(ctx):

    def write(ids, i, block, refs):
        part = block.shape[1] // 3
        for j in range(3):
            kind = lax.rem((j + 3 * ctx - ids[0]) * ctx, 3)
            value = block[:, :part]
            for k in range(1, 3):
                value = jnp.where(kind == k, block[:, k * part : (k + 1) * part], value)
            refs[j][...] = value.astype(BF)

    return write


def units_home(ids, up_pieces, down_pieces, up_shape, down_shape, sub, earlier=()):
    ctx = len(up_pieces)

    def kernel(ids, *refs):
        up_ref, down_ref = refs[2 * ctx :]
        ups = [ref[i] for ref, (_, i) in zip(refs, up_pieces)]
        downs = [ref[i] for ref, (_, i) in zip(refs[ctx:], down_pieces)]
        for k in range(ctx):
            down_ref[k * sub : (k + 1) * sub, :] = owned(ids, downs, k).astype(F32)
            value = owned(ids, ups, k).astype(F32)
            for i in range(value.shape[1] // sub):
                at = (i * ctx + k) * sub
                up_ref[:, at : at + sub] = value[:, i * sub : (i + 1) * sub]

    return call(
        kernel,
        [(up_shape, F32), (down_shape, F32)],
        [ids] + [array for array, _ in up_pieces + down_pieces],
        earlier=earlier,
    )


def add_result(middle, keep, got, bias, earlier=()):

    def kernel(ids, middle_ref, keep_ref, got_ref, bias_ref, out_ref):
        out_ref[...] = middle_ref[...] + keep_ref[...] + got_ref[...].astype(F32) + bias_ref[...]

    return call(
        kernel,
        [(middle.shape, F32)],
        [jnp.zeros((1,), jnp.int32), middle, keep, got, bias[None]],
        earlier=earlier,
    )[0]


def ctx_sum(x):
    for bit in reversed(ctx_bits(lax.axis_size("ctx"))):
        x = x + ctx_swap(x, bit)
    return x


def score_tile(q, k, slope, gap):
    return dot_nt(q, k) * (1.0 / math.sqrt(HEAD_DIM)) - slope * gap


def pair_gaps(pos_q, pos_k, seg_q, seg_k):
    allowed = (pos_k <= pos_q) & (seg_k == seg_q)
    return jnp.where(allowed, pos_q - pos_k, jnp.inf)


def attention_forward(ids, slopes, ln1_parts, full_qkv, qv_rows, tokens_col, tokens_row, unit):
    rows, width = ln1_parts[0].shape
    seq = rows * len(ln1_parts)
    tile = min(seq, 512)
    heads = unit // HEAD_DIM
    ctx = qv_rows.shape[0] // 2

    order = ctx_order(ctx)

    def kernel(ids, slopes, w_ref, bias_ref, col_ref, row_ref, *refs):
        x_ref, qkv_ref, attn_ref, lse_ref, near_ref, far_ref = refs[ctx:]
        for i in range(ctx):
            x_ref[i * rows : (i + 1) * rows, :] = refs[i][...]
        q_bias = bias_ref[pl.ds(ids[0], 1), :]
        v_bias = bias_ref[pl.ds(ctx + ids[0], 1), :]
        x = x_ref[...]
        qkv_ref[:, :unit] = (dot(x, w_ref[:, :unit]) + q_bias).astype(BF)
        qkv_ref[:, unit : 2 * unit] = dot(x, w_ref[:, unit : 2 * unit]).astype(BF)
        qkv_ref[:, 2 * unit :] = (dot(x, w_ref[:, 2 * unit :]) + v_bias).astype(BF)
        for lo in range(0, seq, tile):
            at = slice(lo, lo + tile)
            gap = pair_gaps(
                col_ref[at, 0:1], row_ref[0:1, :], col_ref[at, 1:2], row_ref[1:2, :]
            )
            for h in range(heads):
                cols = [slice(j * unit + h * HEAD_DIM, j * unit + (h + 1) * HEAD_DIM) for j in range(3)]
                scores = score_tile(qkv_ref[at, cols[0]], qkv_ref[:, cols[1]], slopes[h], gap)
                row_max = jnp.max(scores, axis=-1, keepdims=True)
                probs = jnp.exp(scores - row_max)
                row_sum = jnp.sum(probs, axis=-1, keepdims=True)
                out = dot(probs.astype(BF), qkv_ref[:, cols[2]]) / row_sum
                attn_ref[at, cols[0]] = out.astype(BF)
                lse_ref[at, h : h + 1] = row_max + jnp.log(row_sum)
        for i, r in enumerate(order):
            put_piece(near_ref, far_ref, r, attn_ref[i * rows : (i + 1) * rows, :])

    return call(
        kernel,
        [((seq, width), BF), ((seq, 3 * unit), BF), ((seq, unit), BF), ((seq, heads), F32)]
        + piece_shapes(ctx, rows, unit),
        [ids, slopes, full_qkv, qv_rows, tokens_col, tokens_row, *ln1_parts],
        scalars=2,
        work=20 * tile * seq,
    )


def attention_backward(
    ids, slopes, ln1_all, qkv, attn, pieces, lse, tokens_col, tokens_row, unit, dps, earlier=()
):
    seq, width = ln1_all.shape
    ctx = len(pieces)
    order = ctx_order(ctx)
    rows = seq // ctx
    tile = min(seq, 512)
    heads = unit // HEAD_DIM
    inv_root = 1.0 / math.sqrt(HEAD_DIM)

    def kernel(ids, slopes, x_ref, qkv_ref, attn_ref, lse_ref, col_ref, row_ref, *refs):
        out_ref, sum_ref, *block_refs, total_ref, grad_ref = refs[ctx:]
        for i, r in enumerate(order):
            grad_ref[i * rows : (i + 1) * rows, :] = refs[r][pieces[r][1]]
        for lo in range(0, seq, tile):
            at = slice(lo, lo + tile)
            gap = pair_gaps(
                col_ref[at, 0:1], row_ref[0:1, :], col_ref[at, 1:2], row_ref[1:2, :]
            )
            for h in range(heads):
                cols = [slice(j * unit + h * HEAD_DIM, j * unit + (h + 1) * HEAD_DIM) for j in range(3)]
                q, k, v = qkv_ref[at, cols[0]], qkv_ref[:, cols[1]], qkv_ref[:, cols[2]]
                do = grad_ref[at, cols[0]]
                delta = jnp.sum(
                    do.astype(F32) * attn_ref[at, cols[0]].astype(F32), axis=-1, keepdims=True
                )
                probs = jnp.exp(score_tile(q, k, slopes[h], gap) - lse_ref[at, h : h + 1])
                score_bf = (probs * (dot_nt(do, v) - delta)).astype(BF)
                total_ref[at, cols[0]] = inv_root * dot(score_bf, k)
                dk = inv_root * dot_tn(score_bf, q)
                dv = dot_tn(probs.astype(BF), do)
                if lo:
                    dk = dk + total_ref[:, cols[1]]
                    dv = dv + total_ref[:, cols[2]]
                total_ref[:, cols[1]] = dk
                total_ref[:, cols[2]] = dv
        total = total_ref[...]
        out_ref[...] = total.astype(BF)
        sum_ref[...] = jnp.sum(total, axis=0, keepdims=True)
        grad_blocks(ids, x_ref, out_ref[...], *block_refs)

    return call(
        kernel,
        [((seq, 3 * unit), BF), ((1, 3 * unit), F32)] + block_shapes(dps, width // dps, 3 * unit, 1),
        [ids, slopes, ln1_all, qkv, attn, lse, tokens_col, tokens_row]
        + [array for array, _ in pieces],
        scalars=2,
        work=28 * tile * seq,
        scratch=[pltpu.VMEM((seq, 3 * unit), F32), pltpu.VMEM((seq, unit), BF)],
        earlier=earlier,
    )


def split_halves(value, keep_ref, send_ref):
    half = keep_ref.shape[0]
    keep_ref[...] = value[:half]
    send_ref[...] = value[half:].astype(BF)


def input_terms(ids, x, weight, normed_parts, qkv_sums, sums2, up_sums, sub):
    rows, width = x.shape[0], weight.shape[0]
    ctx = len(normed_parts)
    unit = width // ctx
    part = rows // ctx
    units = up_sums.shape[1]
    small_rows = 8 + units * ctx // width

    def kernel(ids, x_ref, w_ref, qkv_ref, sums_ref, up_ref, *refs):
        normed_refs = refs[:ctx]
        keep_ref, send_ref, small_ref = refs[ctx:]
        terms = dot_nt(x_ref[...], w_ref[...])
        split_halves(terms, keep_ref, send_ref)
        gain = jnp.zeros((1, width), F32)
        for i in range(ctx):
            product = terms[i * part : (i + 1) * part] * normed_refs[i][...].astype(F32)
            gain = gain + jnp.sum(product, axis=0, keepdims=True)
        small_ref[0:1, :] = gain
        small_ref[1:2, :] = jnp.sum(terms, axis=0, keepdims=True)
        small_ref[4:5, :] = sums_ref[2:3, :]
        small_ref[5:6, :] = sums_ref[0:1, :]
        small_ref[6:7, :] = sums_ref[1:2, :]
        small_ref[7:8, :] = sums_ref[3:4, :]
        for k in range(ctx):
            mine = ids[0] == k
            at = slice(k * unit, (k + 1) * unit)
            small_ref[2:3, at] = jnp.where(mine, qkv_ref[:, :unit], 0.0)
            small_ref[3:4, at] = jnp.where(mine, qkv_ref[:, 2 * unit :], 0.0)
            for j in range(units // sub):
                row, col = divmod((j * ctx + k) * sub, width)
                value = jnp.where(mine, up_ref[:, j * sub : (j + 1) * sub], 0.0)
                small_ref[8 + row : 9 + row, col : col + sub] = value

    return call(
        kernel,
        [((rows // 2, width), F32), ((rows // 2, width), BF), ((small_rows, width), F32)],
        [ids, x, weight, qkv_sums, sums2, up_sums, *normed_parts],
        work=8 * rows * width,
    )


def feed_forward_hidden(ids, ln2_all, full_up, unit_bias, cot_all, dps):
    seq, width = ln2_all.shape
    units = full_up.shape[1]

    def kernel(ids, x_ref, up_ref, bias_ref, cot_ref, hidden_ref, slope_ref, *block_refs):
        forward, slope = gelu_both(dot(x_ref[...], up_ref[...]) + bias_ref[...])
        slope_ref[...] = slope
        hidden_ref[...] = forward.astype(BF)
        grad_blocks(ids, hidden_ref, cot_ref[...], *block_refs)

    return call(
        kernel,
        [((seq, units), BF), ((seq, units), F32)] + block_shapes(dps, units // dps, width, 2),
        [ids, ln2_all, full_up, unit_bias, cot_all],
        work=16 * seq * units,
    )


def feed_forward_grad(ids, slope, full_up, cot_all, full_down):
    seq, units = slope.shape
    width = cot_all.shape[1]

    def kernel(ids, slope_ref, up_ref, cot_ref, down_ref, pre_ref, sum_ref, keep_ref, send_ref):
        pre_grad = dot_nt(cot_ref[...], down_ref[...]) * slope_ref[...]
        sum_ref[...] = jnp.sum(pre_grad, axis=0, keepdims=True)
        pre_ref[...] = pre_grad.astype(BF)
        split_halves(dot_nt(pre_ref[...], up_ref[...]), keep_ref, send_ref)

    return call(
        kernel,
        [
            ((seq, units), BF),
            ((1, units), F32),
            ((seq // 2, width), F32),
            ((seq // 2, width), BF),
        ],
        [ids, slope, full_up, cot_all, full_down],
        work=12 * seq * units,
    )


def weight_blocks(ids, left, right, dps, parts, earlier=()):

    def kernel(ids, left_ref, right_ref, *block_refs):
        grad_blocks(ids, left_ref, right_ref[...], *block_refs)

    shapes = block_shapes(dps, left.shape[1] // dps, right.shape[1], parts)
    return call(kernel, shapes, [ids, left, right], earlier=earlier)


def out_blocks(ids, attn_parts, cols, dps, earlier=()):
    ctx = len(cols)
    order = ctx_order(ctx)
    rows, width = attn_parts[0].shape
    unit = cols[0][0].shape[2]

    def kernel(ids, *refs):
        *block_refs, left_ref, right_ref = refs[2 * ctx :]
        for i, r in enumerate(order):
            at = slice(i * rows, (i + 1) * rows)
            left_ref[at, :] = refs[i][...]
            right_ref[at, :] = refs[ctx + r][cols[r][1]]
        grad_blocks(ids, left_ref, right_ref[...], *block_refs)

    return call(
        kernel,
        block_shapes(dps, width // dps, unit, 1),
        [ids, *attn_parts] + [array for array, _ in cols],
        scratch=[pltpu.VMEM((ctx * rows, width), BF), pltpu.VMEM((ctx * rows, unit), BF)],
        earlier=earlier,
    )


def times_weight(x, weight, earlier=()):
    rows, width = x.shape[0], weight.shape[1]

    def kernel(ids, x_ref, w_ref, keep_ref, send_ref):
        split_halves(dot(x_ref[...], w_ref[...]), keep_ref, send_ref)

    return call(
        kernel,
        [((rows // 2, width), F32), ((rows // 2, width), BF)],
        [jnp.zeros((1,), jnp.int32), x, weight],
        earlier=earlier,
    )


def scatter_step(keep, got, earlier=()):
    rows, width = keep.shape

    def kernel(ids, keep_ref, got_ref, next_ref, send_ref):
        split_halves(keep_ref[...] + got_ref[...].astype(F32), next_ref, send_ref)

    return call(
        kernel,
        [((rows // 2, width), F32), ((rows // 2, width), BF)],
        [jnp.zeros((1,), jnp.int32), keep, got],
        earlier=earlier,
    )


def scatter_first(keep, send, earlier=()):
    for bit in list(reversed(ctx_bits(lax.axis_size("ctx"))))[:-1]:
        keep, send = scatter_step(keep, ctx_swap(send, bit), earlier)
    return keep, send


def scatter_rest(keep, send):
    return keep, ctx_swap(send, lax.axis_size("ctx") // 2)


def project_out(ids, pieces, out_parts, stream, out_bias, gain, offset):
    _, rows, unit = pieces[0][0].shape
    ctx = len(pieces)
    width = stream.shape[1]

    def kernel(ids, *refs):
        piece_refs, w_refs = refs[:ctx], refs[ctx : 2 * ctx]
        stream_ref, bias_ref, gain_ref, offset_ref = refs[2 * ctx : 2 * ctx + 4]
        attn_ref, middle_ref, normed_ref, inv_ref, act_ref = refs[2 * ctx + 4 :]
        got = [ref[i] for ref, (_, i) in zip(piece_refs, pieces)]
        for k in range(ctx):
            attn_ref[:, k * unit : (k + 1) * unit] = owned(ids, got, k)
        parts = [dot(attn_ref[...], w_refs[r][...]) for r in range(ctx)]
        for k in range(ctx):
            at = slice(k * unit, (k + 1) * unit)
            middle_ref[:, at] = stream_ref[:, at] + owned(ids, parts, k) + bias_ref[:, at]
        out, normed, inv_std = layer_norm(middle_ref[...], gain_ref[...], offset_ref[...])
        normed_ref[...] = normed
        inv_ref[...] = inv_std
        act_ref[...] = out.astype(BF)

    full = (rows, width)
    return call(
        kernel,
        [(full, BF), (full, F32), (full, F32), ((rows, 1), F32), (full, BF)],
        [ids]
        + [array for array, _ in pieces]
        + [*out_parts, stream, out_bias[None], gain[None], offset[None]],
    )


def middle_backward(ids, keep, got, normed, inv_std, gain, upstream, out_parts, earlier=()):
    rows, width = upstream.shape
    ctx = len(out_parts)
    unit = width // ctx

    def kernel(ids, keep_ref, got_ref, normed_ref, inv_ref, gain_ref, up_ref, *refs):
        w_refs = refs[:ctx]
        middle_ref, sum_ref, attn_near, attn_far, cols_near, cols_far = refs[ctx:]
        cols = []
        out_grad = keep_ref[...] + got_ref[...].astype(F32)
        normed = normed_ref[...]
        middle_grad = up_ref[...] + norm_backward(out_grad, normed, inv_ref[...], gain_ref[...])
        middle_ref[...] = middle_grad
        sum_ref[0:1, :] = jnp.sum(out_grad * normed, axis=0, keepdims=True)
        sum_ref[1:2, :] = jnp.sum(out_grad, axis=0, keepdims=True)
        sum_ref[2:3, :] = jnp.sum(middle_grad, axis=0, keepdims=True)
        sum_ref[3:4, :] = jnp.sum(up_ref[...], axis=0, keepdims=True)
        middle_bf = middle_grad.astype(BF)
        for r in range(ctx):
            owner = jnp.bitwise_xor(ids[0], r)
            value = middle_bf[:, :unit]
            for k in range(1, ctx):
                value = jnp.where(owner == k, middle_bf[:, k * unit : (k + 1) * unit], value)
            cols.append(value)
            put_piece(cols_near, cols_far, r, value)
        for r in range(ctx):
            at = pl.multiple_of(jnp.bitwise_xor(ids[0], r) * unit, unit)
            total = dot_nt(cols[0], w_refs[0][pl.ds(at, unit), :])
            for j in range(1, ctx):
                total = total + dot_nt(cols[j], w_refs[j][pl.ds(at, unit), :])
            put_piece(attn_near, attn_far, r, total.astype(BF))

    return call(
        kernel,
        [((rows, width), F32), ((4, width), F32)] + piece_shapes(ctx, rows, unit) * 2,
        [ids, keep, got, normed, inv_std, gain[None], upstream, *out_parts],
        far=[3, 6] + list(range(7, 7 + ctx)),
        earlier=earlier,
    )


def input_backward(keep, got, normed, inv_std, gain, middle_grad, earlier=()):
    rows, width = middle_grad.shape

    def kernel(ids, keep_ref, got_ref, normed_ref, inv_ref, gain_ref, mid_ref, out_ref):
        out_grad = keep_ref[...] + got_ref[...].astype(F32)
        out_ref[...] = mid_ref[...] + norm_backward(
            out_grad, normed_ref[...], inv_ref[...], gain_ref[...]
        )

    return call(
        kernel,
        [((rows, width), F32)],
        [jnp.zeros((1,), jnp.int32), keep, got, normed, inv_std, gain[None], middle_grad],
        earlier=earlier,
    )[0]


def per_device(
    layer_input,
    segment_ids,
    ln1_gain,
    ln1_bias,
    w_qkv,
    qv_bias,
    w_out,
    out_bias,
    ln2_gain,
    ln2_bias,
    w_up,
    up_bias,
    w_down,
    down_bias,
    cotangent,
):
    stream = layer_input[0]
    upstream = cotangent[0]
    seg_row = segment_ids[0]
    rows, width = stream.shape
    ctx = lax.axis_size("ctx")
    dps = lax.axis_size("dp")
    c = lax.axis_index("ctx")
    seq = rows * ctx
    unit = width // ctx
    heads = HEADS // ctx
    inv_root = 1.0 / math.sqrt(HEAD_DIM)
    ff = up_bias.shape[0]
    sub = ff // dps // ctx
    order = ctx_order(ctx)
    slots = [order.index(r) for r in range(ctx)]
    places = dp_places()

    took = [
        lax.ppermute(
            w_qkv[:, j * unit : (j + 1) * unit], "ctx", [(i, (3 * i + j) % ctx) for i in range(ctx)]
        )
        for j in range(3)
    ]
    took = jnp.stack(took)
    head_qkv = jnp.concatenate(
        [pick(took, (kind * ctx + c) % 3) for kind in range(3)] + [w_out], axis=1
    )
    normed1_out, normed1, inv_std1 = layer_norm(stream, ln1_gain, ln1_bias)
    ln1_act = normed1_out.astype(BF)
    cot_bf = upstream.astype(BF)
    w_up, w_down, ln1_act, cot_bf, normed1 = lax.optimization_barrier(
        (w_up, w_down, ln1_act, cot_bf, normed1, head_qkv)
    )[:5]

    z_count, y_count = dp_shape(dps)
    top, *lower = ctx_bits(ctx)
    first_cuts = [lambda b: b[:, : 3 * unit], lambda b: b[:, 3 * unit :]]
    first_full, out_sends, out_full, second_full = None, [], None, None
    moving = head_qkv
    unit_parts = unit_pieces(w_up, w_down, c, sub, unit)
    ln1_parts = [ln1_act]
    normed_parts = [normed1.astype(BF)]
    cot_parts = [cot_bf]
    both = travel = second = None
    for s in range(z_count):
        last = s == z_count - 1
        row = along_y(moving)
        if not last:
            moving = ring_z(moving)
        if out_sends:
            out_sends.append(ctx_swap(out_sends.pop(), top))
        if s == 0:
            ln1_parts = gather_step(ln1_parts, top)
            unit_parts = exchange_step(unit_parts, top)
        if s == 1 % z_count:
            for bit in lower:
                unit_parts = exchange_step(unit_parts, bit)
            for bit in lower:
                ln1_parts = gather_step(ln1_parts, bit)
            both = join_units(unit_parts, c, w_up.shape[0])
            normed_parts = gather_step(normed_parts, top)
        if s == 2 % z_count:
            for bit in lower:
                normed_parts = gather_step(normed_parts, bit)
        if last:
            cot_parts = gather_step(cot_parts, top)
            second = along_y(both)
            travel = ring_z(both)
        moving, row, out_sends, first_full, ln1_parts, normed_parts, cot_parts, unit_parts = (
            lax.optimization_barrier(
                (moving, row, out_sends, first_full, ln1_parts, normed_parts, cot_parts, unit_parts)
            )
        )
        if both is not None:
            both, travel, second, row = lax.optimization_barrier((both, travel, second, row))
        here = places[s * y_count : (s + 1) * y_count]
        first_full = assemble(first_full, row, here, first_cuts)
        out_sends.append(jnp.stack([b[:, 3 * unit :] for b in row]))
    full_qkv, col_out = first_full

    second_cuts = [lambda b: b[0], lambda b: b[1]]
    second_row = along_y(travel)
    travel = ring_z(travel)
    out_sends.append(ctx_swap(out_sends.pop(), top))

    ids = jnp.stack([c, lax.axis_index("dp")]).astype(jnp.int32)
    seg_blocks = seg_row.reshape(ctx, rows)
    seg = jnp.concatenate([pick(seg_blocks, c ^ r) for r in order]).astype(F32)
    pos = jnp.concatenate([(c ^ r) * rows + jnp.arange(rows, dtype=jnp.int32) for r in order])
    tokens_row = jnp.stack([pos.astype(F32), seg])
    tokens_col = tokens_row.T
    slopes = jnp.exp2(-8.0 * (c * heads + 1 + jnp.arange(heads)).astype(F32) / HEADS)

    ln1_all, qkv_heads, attn_heads, lse, attn_near, attn_far = attention_forward(
        ids, slopes, ln1_parts, full_qkv, qv_bias.reshape(2 * ctx, unit), tokens_col, tokens_row, unit
    )

    def heads_joined(got):
        return jnp.concatenate([got[r] for r in order], axis=0)

    second_full = assemble(None, second, places[:y_count], second_cuts)
    attn_near, attn_far, travel, second_row, out_sends, second_full = lax.optimization_barrier(
        (attn_near, attn_far, travel, second_row, out_sends, second_full)
    )
    pieces = trade(attn_near, attn_far)
    second_full = assemble(second_full, second_row, places[y_count : 2 * y_count], second_cuts)
    second_row = along_y(travel)
    travel = ring_z(travel)
    (out_got,) = assemble(
        None, [g[t] for g in out_sends for t in range(y_count)], places, [lambda b: b[...]]
    )
    out_parts = [col_out, out_got]
    for bit in lower:
        out_parts = gather_step(out_parts, bit)
        cot_parts = gather_step(cot_parts, bit)
    out_parts = [out_parts[slots[r]] for r in range(ctx)]
    attn, middle, normed2, inv_std2, ln2_act = project_out(
        ids, pieces, out_parts, stream, out_bias, ln2_gain, ln2_bias
    )
    ln2_parts = gather_step([ln2_act], top)
    ln2_parts, cot_parts, travel, second_row, second_full = lax.optimization_barrier(
        (ln2_parts, cot_parts, travel, second_row, second_full)
    )
    second_full = assemble(second_full, second_row, places[2 * y_count : 3 * y_count], second_cuts)
    if (z_count, y_count) == (4, 2):
        got = [travel, jnp.stack([ring_y(travel[0]), ring_z(second_row[1][1])])]
    else:
        got = along_y(travel)
    for bit in lower:
        ln2_parts = gather_step(ln2_parts, bit)
    ln2_all = jnp.concatenate(ln2_parts, axis=0)
    cot_all = jnp.concatenate(cot_parts, axis=0)
    full_up, full_down = assemble(second_full, got, places[3 * y_count :], second_cuts)
    full_up = full_up.reshape(width, dps * sub)
    unit_bias = pick(jnp.moveaxis(up_bias.reshape(dps, ctx, sub), 1, 0), c).reshape(1, dps * sub)
    hidden, slope, *grad_down = feed_forward_hidden(ids, ln2_all, full_up, unit_bias, cot_all, dps)
    pre_bf, up_bias_part, ln2_keep, ln2_send = feed_forward_grad(
        ids, slope, full_up, cot_all, full_down
    )
    ln2_keep, ln2_send = scatter_first(ln2_keep, ln2_send)
    ln2_keep, ln2_got = scatter_rest(ln2_keep, ln2_send)
    grad_up = weight_blocks(ids, ln2_all, pre_bf, dps, 2, earlier=[ln2_send])

    down, up = Reduction(grad_down), Reduction(grad_up)
    down_sent = down.step()
    middle_grad, sums2, grad_near, grad_far, col_near, col_far = middle_backward(
        ids,
        ln2_keep,
        ln2_got,
        normed2,
        inv_std2,
        ln2_gain,
        upstream,
        out_parts,
        earlier=[grad_up[0], down_sent],
    )
    grad_pieces = trade(grad_near, grad_far)
    qkv_bf, qkv_sums, *grad_qkv = attention_backward(
        ids,
        slopes,
        ln1_all,
        qkv_heads,
        attn_heads,
        grad_pieces,
        lse,
        tokens_col,
        tokens_row,
        unit,
        dps,
        earlier=[down.terms[1][0]],
    )
    qkv = Reduction(grad_qkv)
    ln1_keep, ln1_send, small = input_terms(
        ids, qkv_bf, full_qkv, normed_parts, qkv_sums, sums2, up_bias_part, sub
    )
    while down.bits:
        down.step(ln1_send)
    up.step(ln1_send)
    for bit in reversed(lower):
        small = small + ctx_swap(small, bit)
    ln1_keep, ln1_send = scatter_first(ln1_keep, ln1_send)

    ln1_keep, ln1_send, small = sync([], ln1_keep, ln1_send, small)
    ln1_keep, ln1_got = scatter_rest(ln1_keep, ln1_send)
    small_got = ctx_swap(small, top)
    cols = trade(col_near, col_far)

    cols_got, ln1_got, small_got = sync([down, up], [a for a, _ in cols], ln1_got, small_got)
    cols = [(a, i) for a, (_, i) in zip(cols_got, cols)]
    small = small + small_got
    bits = dp_bits()
    small_got = dp_swap(small, bits[0])
    attn_parts = gather_step([attn], top)
    while up.bits:
        up.step()
    input_grad = input_backward(ln1_keep, ln1_got, normed1, inv_std1, ln1_gain, middle_grad)
    result_keep, result_send = scatter_first(*times_weight(hidden, full_down, earlier=[ln1_got]))
    down_out = down.result(piece_shapes(ctx, sub, unit), column_pieces(ctx))

    attn_parts, small_got, result_keep, result_send, down_out = sync(
        [up, qkv], attn_parts, small_got, result_keep, result_send, down_out
    )
    qkv.step()
    small = small + small_got
    small_got = dp_swap(small, bits[1])
    for bit in lower:
        attn_parts = gather_step(attn_parts, bit)
    grad_out = out_blocks(ids, attn_parts, cols, dps)
    out = Reduction(grad_out)
    result_keep, result_got = scatter_rest(result_keep, result_send)
    up_rows = w_up.shape[0]
    up_out = up.result(piece_shapes(ctx, up_rows, dps * sub // ctx), column_pieces(ctx))
    up_home, down_home = trade(*up_out), trade(*down_out)

    up_got, down_got, result_got = sync(
        [qkv], [a for a, _ in up_home], [a for a, _ in down_home], result_got
    )
    up_home = [(a, i) for a, (_, i) in zip(up_got, up_home)]
    down_home = [(a, i) for a, (_, i) in zip(down_got, down_home)]
    while qkv.bits:
        qkv.step()
    out.step()
    shard_up, shard_down = units_home(
        ids, up_home, down_home, w_up.shape, w_down.shape, sub
    )
    result = add_result(middle, result_keep, result_got, down_bias)

    small_got, shard_up, shard_down, result = sync([qkv, out], small_got, shard_up, shard_down, result)
    qkv_out = qkv.result([((up_rows, unit), BF)] * 3, kind_pieces(ctx))
    while out.bits:
        out.step()
    small = small + small_got
    for bit in bits[2:]:
        small = small + dp_swap(small, bit)
    sum_out = out.result([((up_rows, unit), F32)], store_block)[0]

    shard_qkv = jnp.concatenate(
        [
            lax.ppermute(qkv_out[j], "ctx", [((3 * i + j) % ctx, i) for i in range(ctx)])
            for j in range(3)
        ],
        axis=1,
    ).astype(F32)

    return (
        result[None],
        input_grad[None],
        small[0],
        small[1],
        shard_qkv,
        small[2:4].reshape(2 * width),
        sum_out,
        small[4],
        small[5],
        small[6],
        shard_up,
        small[8:].reshape(ff),
        shard_down,
        small[7],
    )


def solution(mesh):
    tokens = P("dp", "ctx", None)
    weight = P("dp", "ctx")
    placed = (
        tokens,
        P("dp", None),
        P(),
        P(),
        weight,
        P(),
        weight,
        P(),
        P(),
        P(),
        weight,
        P(),
        weight,
        P(),
        tokens,
    )
    return jax.shard_map(
        per_device,
        mesh=mesh,
        in_specs=placed,
        out_specs=(
            tokens,
            tokens,
            P(),
            P(),
            weight,
            P(),
            weight,
            P(),
            P(),
            P(),
            weight,
            P(),
            weight,
            P(),
        ),
        check_vma=False,
    )
```

profile of v0, /device:TPU:0, one launch (start us, length us, event | category | flops | bytes accessed | tf_op | source)
XLA Modules:
  0.0 248.2 jit_solution(14398904218439503524)
XLA Ops:
  2.4 3.8 %collective-permute-start.1 = (bf16[128,256]{1,0:T(8,128)(2,1)S(1)}, bf16[128,256]{1,0:T(8,128)(2,1)S(1)}, u32[]{:S(2)}, u32[]{:S(2)}) collective-permute-start(bf16[128,256]{1,0:T(8,128)(2,1)S(1)} %get-tuple-element.483), channel_id=1, source_target_pairs={{0,1},{1,0},{2,3},{3,2},{4,5},{5,4},{6,7},{7,6},{8,9},{9,8},{10,11... | collective-permute-start | bytes 196616 | tf_op jit(solution)/shard_map/ppermute | solution.py:843
  6.2 2.2 collective-permute-start.2
  13.2 1.6 collective-permute-start.6
  14.8 1.6 collective-permute-start.3
  16.4 1.5 collective-permute-start.4
  19.2 3.3 %collective-permute-done.6 = bf16[2,2,128,256]{3,2,1,0:T(8,128)(2,1)S(1)} collective-permute-done((bf16[2,2,128,256]{3,2,1,0:T(8,128)(2,1)S(1)}, bf16[2,2,128,256]{3,2,1,0:T(8,128)(2,1)S(1)}, u32[]{:S(2)}, u32[]{:S(2)}) %collective-permute-start.6) | collective-permute-done | bytes 262176 | tf_op jit(solution)/shard_map/ppermute | solution.py:83
  23.2 2.3 collective-permute-done.5.refs_7_
  27.1 1.6 collective-permute-start.8
  29.4 2.2 collective-permute-done.10
  36.9 2.9 %collective-permute-done.13.refs_7_ = bf16[128,1024]{1,0:T(8,128)(2,1)S(1)} collective-permute-done((bf16[128,1024]{1,0:T(8,128)(2,1)}, bf16[128,1024]{1,0:T(8,128)(2,1)S(1)}, u32[]{:S(2)}, u32[]{:S(2)}) %collective-permute-start.13) | collective-permute-done | bytes 262176 | tf_op jit(solution)/shard_map/ppermute | solution.py:83
  39.8 1.6 collective-permute-start.14
  47.0 3.9 %collective-permute-done.16 = bf16[2,128,256]{2,1,0:T(8,128)(2,1)S(1)} collective-permute-done((bf16[2,128,256]{2,1,0:T(8,128)(2,1)S(1)}, bf16[2,128,256]{2,1,0:T(8,128)(2,1)S(1)}, u32[]{:S(2)}, u32[]{:S(2)}) %collective-permute-start.16) | collective-permute-done | bytes 131104 | tf_op jit(solution)/shard_map/ppermute | solution.py:83
  52.4 1.6 collective-permute-start.19
  61.9 4.5 %collective-permute-done.22 = bf16[2,128,256]{2,1,0:T(8,128)(2,1)} collective-permute-done((bf16[2,128,256]{2,1,0:T(8,128)(2,1)}, bf16[2,128,256]{2,1,0:T(8,128)(2,1)}, u32[]{:S(2)}, u32[]{:S(2)}) %collective-permute-start.22) | collective-permute-done | bytes 131104 | tf_op jit(solution)/shard_map/ppermute | solution.py:83
  66.5 6.2 %collective-permute-done.21.refs_1_ = bf16[128,1024]{1,0:T(8,128)(2,1)} collective-permute-done((bf16[128,1024]{1,0:T(8,128)(2,1)S(1)}, bf16[128,1024]{1,0:T(8,128)(2,1)}, u32[]{:S(2)}, u32[]{:S(2)}) %collective-permute-start.21) | collective-permute-done | bytes 262176 | tf_op jit(solution)/shard_map/ppermute | solution.py:175
  72.7 1.6 collective-permute-start.24
  80.7 4.3 %shard_map.258 = (bf16[512,1024]{1,0:T(8,128)(2,1)S(1)}, bf16[512,768]{1,0:T(8,128)(2,1)S(1)}, bf16[512,256]{1,0:T(8,128)(2,1)S(1)}, f32[512,4]{1,0:T(8,128)S(1)...) custom-call(s32[2]{0:T(128)S(1)} %pad_add_fusion.refs_0_, f32[4]{0:T(128)S(1)} %multiply_exponential_fusion.refs_1_, ...), custom_call_target="tpu_custom_call" | custom-call | tf_op jit(solution)/shard_map/pallas_call | solution.py:234
  85.1 1.7 collective-permute-done.24.refs_0_
  91.4 3.8 %collective-permute-done.28.refs_3_ = bf16[2,128,256]{2,1,0:T(8,128)(2,1)S(1)} collective-permute-done((bf16[2,128,256]{2,1,0:T(8,128)(2,1)S(1)}, bf16[2,128,256]{2,1,0:T(8,128)(2,1)S(1)}, u32[]{:S(2)}, u32[]{:S(2)}) %collective-permute-start.28) | collective-permute-done | bytes 131104 | tf_op jit(solution)/shard_map/ppermute | solution.py:83
  100.0 5.8 %collective-permute-done.35.refs_0_ = bf16[2,128,1024]{2,1,0:T(8,128)(2,1)S(1)} collective-permute-done((bf16[2,128,1024]{2,1,0:T(8,128)(2,1)}, bf16[2,128,1024]{2,1,0:T(8,128)(2,1)S(1)}, u32[]{:S(2)}, u32[]{:S(2)}) %collective-permute-start.35) | collective-permute-done | bytes 524320 | tf_op jit(solution)/shard_map/ppermute | solution.py:169
  111.1 5.5 %collective-permute-done.39 = bf16[128,1024]{1,0:T(8,128)(2,1)S(1)} collective-permute-done((bf16[128,1024]{1,0:T(8,128)(2,1)S(1)}, bf16[128,1024]{1,0:T(8,128)(2,1)S(1)}, u32[]{:S(2)}, u32[]{:S(2)}) %collective-permute-start.39) | collective-permute-done | bytes 262176 | tf_op jit(solution)/shard_map/ppermute | solution.py:175
  116.6 2.3 collective-permute-done.40
  119.6 5.7 %shard_map.265 = (bf16[512,1024]{1,0:T(8,128)(2,1)S(1)}, f32[512,1024]{1,0:T(8,128)S(1)}, bf16[4,128,1024]{2,1,0:T(8,128)(2,1)S(1)}, bf16[2,128,1024]{2,1,0:T(8,128)(2,1)S(1)}, bf16[2,128,1024]{2,1,0:T(8,128)(2,1)S(1)}) custom-call(s32[2]{0:T(128)S(1)} %pad_add_fusion.refs_0_, bf16[512,1024]{1,0:T(8,128)(2,1)S(1)} %constant_dynamic-update-slice_fusion.refs_1_, ...), custom_call_target="tpu_custom_call" | custom-call | tf_op jit(solution)/shard_map/pallas_call | solution.py:234
  125.3 2.9 %shard_map.267 = (bf16[512,1024]{1,0:T(8,128)(2,1)S(1)}, f32[1,1024]{1,0:T(1,128)S(1)}, f32[256,1024]{1,0:T(8,128)S(1)}, bf16[256,1024]{1,0:T(8,128)(2,1)S(1)}) custom-call(s32[2]{0:T(128)S(1)} %pad_add_fusion.refs_0_, f32[512,1024]{1,0:T(8,128)S(1)} %get-tuple-element.350.refs_1_, bf16[1024,1024]{1,0:T(8,128)(2,1)S(1)} %get-tuple-element.338.refs_2_, ...), custom_call_target="tpu_custom_call" | custom-call | tf_op jit(solution)/shard_map/pallas_call | solution.py:234
  128.3 1.6 collective-permute-start.42
  132.5 3.7 %shard_map.269 = (bf16[4,128,1024]{2,1,0:T(8,128)(2,1)S(1)}, bf16[2,128,1024]{2,1,0:T(8,128)(2,1)S(1)}, bf16[2,128,1024]{2,1,0:T(8,128)(2,1)S(1)}) custom-call(s32[2]{0:T(128)S(1)} %pad_add_fusion.refs_0_, bf16[512,1024]{1,0:T(8,128)(2,1)S(1)} %constant_dynamic-update-slice_fusion.refs_1_, bf16[512,1024]{1,0:T(8,128)(2,1)S(1)} %get-tuple-element.358.refs_2_, ...), custom_call_target="tpu_custom_call" | custom-call | tf_op jit(solution)/shard_map/pallas_call | solution.py:234
  136.2 6.9 %collective-permute-done.42.refs_2_ = bf16[2,128,1024]{2,1,0:T(8,128)(2,1)S(1)} collective-permute-done((bf16[2,128,1024]{2,1,0:T(8,128)(2,1)S(1)}, bf16[2,128,1024]{2,1,0:T(8,128)(2,1)S(1)}, u32[]{:S(2)}, u32[]{:S(2)}) %collective-permute-start.42) | collective-permute-done | bytes 524320 | tf_op jit(solution)/shard_map/ppermute | solution.py:314
  143.2 1.9 shard_map.270
  148.1 2.8 %collective-permute-done.47.refs_10_ = bf16[2,128,256]{2,1,0:T(8,128)(2,1)S(1)} collective-permute-done((bf16[2,128,256]{2,1,0:T(8,128)(2,1)S(1)}, bf16[2,128,256]{2,1,0:T(8,128)(2,1)S(1)}, u32[]{:S(2)}, u32[]{:S(2)}) %collective-permute-start.47) | collective-permute-done | bytes 131104 | tf_op jit(solution)/shard_map/ppermute | solution.py:83
  150.9 3.4 %collective-permute-done.41.refs_12_.refs_2_ = bf16[2,128,1024]{2,1,0:T(8,128)(2,1)S(1)} collective-permute-done((bf16[2,128,1024]{2,1,0:T(8,128)(2,1)S(1)}, bf16[2,128,1024]{2,1,0:T(8,128)(2,1)S(1)}, u32[]{:S(2)}, u32[]{:S(2)}) %collective-permute-start.41) | collective-permute-done | bytes 524320 | tf_op jit(solution)/shard_map/ppermute | solution.py:314
  154.3 8.7 %shard_map.271 = (bf16[512,768]{1,0:T(8,128)(2,1)S(1)}, f32[1,768]{1,0:T(1,128)S(1)}, bf16[4,128,768]{2,1,0:T(8,128)(2,1)S(1)}, bf16[4,128,768]{2,1,0:T(8,128)(2,1)S(1)}) custom-call(s32[2]{0:T(128)S(1)} %pad_add_fusion.refs_0_, f32[4]{0:T(128)S(1)} %multiply_exponential_fusion.refs_1_, bf16[512,1024]{1,0:T(8,128)(2,1)S(1)} %get-tuple-element.346.refs_2_, ...), custom_call_target="tpu_custom_call" | custom-call | tf_op jit(solution)/shard_map/pallas_call | solution.py:234
  163.0 2.0 shard_map.272
  165.1 1.6 collective-permute-start.50
  169.2 3.7 %collective-permute-done.54.refs_7_ = bf16[2,128,256]{2,1,0:T(8,128)(2,1)S(1)} collective-permute-done((bf16[2,128,256]{2,1,0:T(8,128)(2,1)S(1)}, bf16[2,128,256]{2,1,0:T(8,128)(2,1)S(1)}, u32[]{:S(2)}, u32[]{:S(2)}) %collective-permute-start.54) | collective-permute-done | bytes 131104 | tf_op jit(solution)/shard_map/ppermute | solution.py:83
  174.8 5.1 %collective-permute-done.50.refs_2_ = bf16[2,128,1024]{2,1,0:T(8,128)(2,1)S(1)} collective-permute-done((bf16[2,128,1024]{2,1,0:T(8,128)(2,1)S(1)}, bf16[2,128,1024]{2,1,0:T(8,128)(2,1)S(1)}, u32[]{:S(2)}, u32[]{:S(2)}) %collective-permute-start.50) | collective-permute-done | bytes 524320 | tf_op jit(solution)/shard_map/ppermute | solution.py:314
  182.7 1.7 collective-permute-done.49.refs_4_
  184.3 2.2 collective-permute-done.52.refs_3_
  191.6 5.0 %collective-permute-done.62.refs_2_ = bf16[128,1024]{1,0:T(8,128)(2,1)S(1)} collective-permute-done((bf16[128,1024]{1,0:T(8,128)(2,1)S(1)}, bf16[128,1024]{1,0:T(8,128)(2,1)S(1)}, u32[]{:S(2)}, u32[]{:S(2)}) %collective-permute-start.62) | collective-permute-done | bytes 262176 | tf_op jit(solution)/shard_map/ppermute | solution.py:83
  197.7 4.9 %collective-permute-done.60.refs_4_ = bf16[1,128,1024]{2,1,0:T(8,128)(2,1)S(1)} collective-permute-done((bf16[1,128,1024]{2,1,0:T(8,128)(2,1)S(1)}, bf16[1,128,1024]{2,1,0:T(8,128)(2,1)S(1)}, u32[]{:S(2)}, u32[]{:S(2)}) %collective-permute-start.60) | collective-permute-done | bytes 262176 | tf_op jit(solution)/shard_map/ppermute | solution.py:314
  205.4 3.8 %collective-permute-done.67.refs_3_ = bf16[2,128,256]{2,1,0:T(8,128)(2,1)S(1)} collective-permute-done((bf16[2,128,256]{2,1,0:T(8,128)(2,1)S(1)}, bf16[2,128,256]{2,1,0:T(8,128)(2,1)S(1)}, u32[]{:S(2)}, u32[]{:S(2)}) %collective-permute-start.67) | collective-permute-done | bytes 131104 | tf_op jit(solution)/shard_map/ppermute | solution.py:83
  211.3 2.5 %shard_map.283 = (bf16[4,128,256]{2,1,0:T(8,128)(2,1)S(1)}, bf16[4,128,256]{2,1,0:T(8,128)(2,1)S(1)}) custom-call(s32[2]{0:T(128)S(1)} %pad_add_fusion.refs_0_, bf16[128,1024]{1,0:T(8,128)(2,1)S(1)} %get-tuple-element.416.refs_1_, bf16[128,1024]{1,0:T(8,128)(2,1)S(1)} %collective-permute-done.62.refs_2_, ...), custom_call_target="tpu_custom_call" | custom-call | tf_op jit(solution)/shard_map/pallas_call | solution.py:234
  216.7 3.1 %collective-permute-done.72.refs_3_ = bf16[128,1024]{1,0:T(8,128)(2,1)S(1)} collective-permute-done((bf16[128,1024]{1,0:T(8,128)(2,1)S(1)}, bf16[128,1024]{1,0:T(8,128)(2,1)S(1)}, u32[]{:S(2)}, u32[]{:S(2)}) %collective-permute-start.72) | collective-permute-done | bytes 262176 | tf_op jit(solution)/shard_map/ppermute | solution.py:83
  219.9 2.3 collective-permute-done.76.refs_2_
  222.4 2.1 collective-permute-start.78
  225.3 1.7 shard_map.285
  227.0 5.6 %collective-permute-done.78 = f32[12,1024]{1,0:T(8,128)S(1)} collective-permute-done((f32[12,1024]{1,0:T(8,128)S(1)}, f32[12,1024]{1,0:T(8,128)S(1)}, u32[]{:S(2)}, u32[]{:S(2)}) %collective-permute-start.78) | collective-permute-done | bytes 49184 | tf_op jit(solution)/shard_map/ppermute | solution.py:314
  236.7 3.0 %collective-permute-start.83 = (bf16[1,128,256]{2,1,0:T(8,128)(2,1)S(1)}, bf16[1,128,256]{2,1,0:T(8,128)(2,1)S(1)}, u32[]{:S(2)}, u32[]{:S(2)}) collective-permute-start(bf16[1,128,256]{2,1,0:T(8,128)(2,1)S(1)} %shard_map.289), channel_id=1, source_target_pairs={{0,16},{4,20},{8,24},{12,28},{16,0},{20,4},{24,8},{28,12},{1,17},{... | collective-permute-start | bytes 196616 | tf_op jit(solution)/shard_map/ppermute | solution.py:314
  241.3 2.6 %collective-permute-start.82 = (bf16[128,256]{1,0:T(8,128)(2,1)S(1)}, bf16[128,256]{1,0:T(8,128)(2,1)S(1)}, u32[]{:S(2)}, u32[]{:S(2)}) collective-permute-start(bf16[128,256]{1,0:T(8,128)(2,1)S(1)} %get-tuple-element.448), channel_id=1, source_target_pairs={{2,0},{1,1},{0,2},{3,3},{6,4},{5,5},{4,6},{7,7},{10,8},{9,9},{8,10... | collective-permute-start | bytes 196616 | tf_op jit(solution)/shard_map/ppermute | solution.py:1063
  (334 shorter events, 90.0 us)
Async XLA Ops:
  1.7 10.4 %collective-permute-start = (bf16[128,256]{1,0:T(8,128)(2,1)S(1)}, bf16[128,256]{1,0:T(8,128)(2,1)S(1)}, u32[]{:S(2)}, u32[]{:S(2)}) collective-permute-start(bf16[128,256]{1,0:T(8,128)(2,1)S(1)} %get-tuple-element.481), channel_id=1, source_target_pairs={{0,0},{1,3},{2,2},{3,1},{4,4},{5,7},{6,6},{7,5},{8,8},{9,11},{10,1... | collective-permute-start | bytes 196616 | tf_op jit(solution)/shard_map/ppermute | solution.py:843
  2.4 9.8 %collective-permute-start.1 = (bf16[128,256]{1,0:T(8,128)(2,1)S(1)}, bf16[128,256]{1,0:T(8,128)(2,1)S(1)}, u32[]{:S(2)}, u32[]{:S(2)}) collective-permute-start(bf16[128,256]{1,0:T(8,128)(2,1)S(1)} %get-tuple-element.483), channel_id=1, source_target_pairs={{0,1},{1,0},{2,3},{3,2},{4,5},{5,4},{6,7},{7,6},{8,9},{9,8},{10,11... | collective-permute-start | bytes 196616 | tf_op jit(solution)/shard_map/ppermute | solution.py:843
  13.2 9.3 %collective-permute-start.6 = (bf16[2,2,128,256]{3,2,1,0:T(8,128)(2,1)S(1)}, bf16[2,2,128,256]{3,2,1,0:T(8,128)(2,1)S(1)}, u32[]{:S(2)}, u32[]{:S(2)}) collective-permute-start(bf16[2,2,128,256]{3,2,1,0:T(8,128)(2,1)S(1)} %pad_maximum_fusion.3), channel_id=1, source_target_pairs={{0,2},{1,3},{2,0},{3,1},{4,6},{5,7},{6,4},{7,5},{8,10},{9,11},{10,... | collective-permute-start | bytes 786440 | tf_op jit(solution)/shard_map/ppermute | solution.py:83
  14.8 10.7 %collective-permute-start.3 = (bf16[128,1024]{1,0:T(8,128)(2,1)S(1)}, bf16[128,1024]{1,0:T(8,128)(2,1)}, u32[]{:S(2)}, u32[]{:S(2)}) collective-permute-start(bf16[128,1024]{1,0:T(8,128)(2,1)S(1)} %pad_maximum_fusion.2.refs_0_), channel_id=1, source_target_pairs={{0,8},{4,12},{8,16},{12,20},{16,24},{20,28},{24,0},{28,4},{1,9},{5... | collective-permute-start | bytes 786440 | tf_op jit(solution)/shard_map/ppermute | solution.py:169
  16.4 9.1 %collective-permute-start.4 = (bf16[128,1024]{1,0:T(8,128)(2,1)S(1)}, bf16[128,1024]{1,0:T(8,128)(2,1)S(1)}, u32[]{:S(2)}, u32[]{:S(2)}) collective-permute-start(bf16[128,1024]{1,0:T(8,128)(2,1)S(1)} %pad_maximum_fusion.2.refs_0_), channel_id=1, source_target_pairs={{0,4},{4,0},{8,12},{12,8},{16,20},{20,16},{24,28},{28,24},{1,5},{5... | collective-permute-start | bytes 786440 | tf_op jit(solution)/shard_map/ppermute | solution.py:175
  27.1 12.6 %collective-permute-start.8 = (bf16[128,1024]{1,0:T(8,128)(2,1)}, bf16[128,1024]{1,0:T(8,128)(2,1)S(1)}, u32[]{:S(2)}, u32[]{:S(2)}) collective-permute-start(bf16[128,1024]{1,0:T(8,128)(2,1)} %collective-permute-done.3.refs_0_), channel_id=1, source_target_pairs={{0,8},{4,12},{8,16},{12,20},{16,24},{20,28},{24,0},{28,4},{1,9},{5... | collective-permute-start | bytes 786440 | tf_op jit(solution)/shard_map/ppermute | solution.py:169
  28.7 11.1 %collective-permute-start.9 = (bf16[128,1024]{1,0:T(8,128)(2,1)}, bf16[128,1024]{1,0:T(8,128)(2,1)S(1)}, u32[]{:S(2)}, u32[]{:S(2)}) collective-permute-start(bf16[128,1024]{1,0:T(8,128)(2,1)} %collective-permute-done.3.refs_0_), channel_id=1, source_target_pairs={{0,4},{4,0},{8,12},{12,8},{16,20},{20,16},{24,28},{28,24},{1,5},{5... | collective-permute-start | bytes 786440 | tf_op jit(solution)/shard_map/ppermute | solution.py:175
  31.6 8.1 %collective-permute-start.13 = (bf16[128,1024]{1,0:T(8,128)(2,1)}, bf16[128,1024]{1,0:T(8,128)(2,1)S(1)}, u32[]{:S(2)}, u32[]{:S(2)}) collective-permute-start(bf16[128,1024]{1,0:T(8,128)(2,1)} %convert_element_type.38.refs_6_), channel_id=1, source_target_pairs={{0,2},{1,3},{2,0},{3,1},{4,6},{5,7},{6,4},{7,5},{8,10},{9,11},{10,... | collective-permute-start | bytes 786440 | tf_op jit(solution)/shard_map/ppermute | solution.py:83
  33.0 9.9 %collective-permute-start.7 = (bf16[2,2,128,256]{3,2,1,0:T(8,128)(2,1)S(1)}, bf16[2,2,128,256]{3,2,1,0:T(8,128)(2,1)S(1)}, u32[]{:S(2)}, u32[]{:S(2)}) collective-permute-start(bf16[2,2,128,256]{3,2,1,0:T(8,128)(2,1)S(1)} %pad_maximum_fusion.4), channel_id=1, source_target_pairs={{0,1},{1,0},{2,3},{3,2},{4,5},{5,4},{6,7},{7,6},{8,9},{9,8},{10,11... | collective-permute-start | bytes 786440 | tf_op jit(solution)/shard_map/ppermute | solution.py:83
  39.8 11.2 %collective-permute-start.14 = (bf16[128,1024]{1,0:T(8,128)(2,1)S(1)}, bf16[128,1024]{1,0:T(8,128)(2,1)S(1)}, u32[]{:S(2)}, u32[]{:S(2)}) collective-permute-start(bf16[128,1024]{1,0:T(8,128)(2,1)S(1)} %collective-permute-done.8.refs_0_), channel_id=1, source_target_pairs={{0,8},{4,12},{8,16},{12,20},{16,24},{20,28},{24,0},{28,4},{1,9},{5... | collective-permute-start | bytes 786440 | tf_op jit(solution)/shard_map/ppermute | solution.py:169
  41.4 9.5 %collective-permute-start.15 = (bf16[128,1024]{1,0:T(8,128)(2,1)S(1)}, bf16[128,1024]{1,0:T(8,128)(2,1)S(1)}, u32[]{:S(2)}, u32[]{:S(2)}) collective-permute-start(bf16[128,1024]{1,0:T(8,128)(2,1)S(1)} %collective-permute-done.8.refs_0_), channel_id=1, source_target_pairs={{0,4},{4,0},{8,12},{12,8},{16,20},{20,16},{24,28},{28,24},{1,5},{5... | collective-permute-start | bytes 786440 | tf_op jit(solution)/shard_map/ppermute | solution.py:175
  52.4 20.3 %collective-permute-start.19 = (bf16[2,128,1024]{2,1,0:T(8,128)(2,1)}, bf16[2,128,1024]{2,1,0:T(8,128)(2,1)}, u32[]{:S(2)}, u32[]{:S(2)}) collective-permute-start(bf16[2,128,1024]{2,1,0:T(8,128)(2,1)} %pad_maximum_fusion.refs_0_), channel_id=1, source_target_pairs={{0,8},{4,12},{8,16},{12,20},{16,24},{20,28},{24,0},{28,4},{1,9},{5... | collective-permute-start | bytes 1572872 | tf_op jit(solution)/shard_map/ppermute | solution.py:169
  54.0 18.7 %collective-permute-start.20 = (bf16[2,128,1024]{2,1,0:T(8,128)(2,1)}, bf16[2,128,1024]{2,1,0:T(8,128)(2,1)}, u32[]{:S(2)}, u32[]{:S(2)}) collective-permute-start(bf16[2,128,1024]{2,1,0:T(8,128)(2,1)} %pad_maximum_fusion.refs_0_), channel_id=1, source_target_pairs={{0,4},{4,0},{8,12},{12,8},{16,20},{20,16},{24,28},{28,24},{1,5},{5... | collective-permute-start | bytes 1572872 | tf_op jit(solution)/shard_map/ppermute | solution.py:175
  55.2 17.5 %collective-permute-start.21 = (bf16[128,1024]{1,0:T(8,128)(2,1)S(1)}, bf16[128,1024]{1,0:T(8,128)(2,1)}, u32[]{:S(2)}, u32[]{:S(2)}) collective-permute-start(bf16[128,1024]{1,0:T(8,128)(2,1)S(1)} %collective-permute-done.14.refs_0_), channel_id=1, source_target_pairs={{0,4},{4,0},{8,12},{12,8},{16,20},{20,16},{24,28},{28,24},{1,5},{5... | collective-permute-start | bytes 786440 | tf_op jit(solution)/shard_map/ppermute | solution.py:175
  56.7 16.0 %collective-permute-start.23 = (bf16[128,1024]{1,0:T(8,128)(2,1)}, bf16[128,1024]{1,0:T(8,128)(2,1)}, u32[]{:S(2)}, u32[]{:S(2)}) collective-permute-start(bf16[128,1024]{1,0:T(8,128)(2,1)} %bitcast_convert_fusion), channel_id=1, source_target_pairs={{0,2},{1,3},{2,0},{3,1},{4,6},{5,7},{6,4},{7,5},{8,10},{9,11},{10,... | collective-permute-start | bytes 786440 | tf_op jit(solution)/shard_map/ppermute | solution.py:83
  57.9 8.5 %collective-permute-start.22 = (bf16[2,128,256]{2,1,0:T(8,128)(2,1)}, bf16[2,128,256]{2,1,0:T(8,128)(2,1)}, u32[]{:S(2)}, u32[]{:S(2)}) collective-permute-start(bf16[2,128,256]{2,1,0:T(8,128)(2,1)} %pad_maximum_fusion.12), channel_id=1, source_target_pairs={{0,2},{1,3},{2,0},{3,1},{4,6},{5,7},{6,4},{7,5},{8,10},{9,11},{10,... | collective-permute-start | bytes 393224 | tf_op jit(solution)/shard_map/ppermute | solution.py:83
  72.7 14.0 %collective-permute-start.24 = (bf16[2,128,1024]{2,1,0:T(8,128)(2,1)}, bf16[2,128,1024]{2,1,0:T(8,128)(2,1)}, u32[]{:S(2)}, u32[]{:S(2)}) collective-permute-start(bf16[2,128,1024]{2,1,0:T(8,128)(2,1)} %collective-permute-done.19.refs_0_), channel_id=1, source_target_pairs={{0,8},{4,12},{8,16},{12,20},{16,24},{20,28},{24,0},{28,4},{1,9},{5... | collective-permute-start | bytes 1572872 | tf_op jit(solution)/shard_map/ppermute | solution.py:169
  74.3 12.4 %collective-permute-start.25 = (bf16[2,128,1024]{2,1,0:T(8,128)(2,1)}, bf16[2,128,1024]{2,1,0:T(8,128)(2,1)}, u32[]{:S(2)}, u32[]{:S(2)}) collective-permute-start(bf16[2,128,1024]{2,1,0:T(8,128)(2,1)} %collective-permute-done.19.refs_0_), channel_id=1, source_target_pairs={{0,4},{4,0},{8,12},{12,8},{16,20},{20,16},{24,28},{28,24},{1,5},{5... | collective-permute-start | bytes 1572872 | tf_op jit(solution)/shard_map/ppermute | solution.py:175
  76.4 8.7 %collective-permute-start.26 = (bf16[2,128,256]{2,1,0:T(8,128)(2,1)}, bf16[2,128,256]{2,1,0:T(8,128)(2,1)}, u32[]{:S(2)}, u32[]{:S(2)}) collective-permute-start(bf16[2,128,256]{2,1,0:T(8,128)(2,1)} %pad_maximum_fusion.13), channel_id=1, source_target_pairs={{0,2},{1,3},{2,0},{3,1},{4,6},{5,7},{6,4},{7,5},{8,10},{9,11},{10,... | collective-permute-start | bytes 393224 | tf_op jit(solution)/shard_map/ppermute | solution.py:83
  79.3 12.1 %collective-permute-start.30 = (bf16[1024,256]{1,0:T(8,128)(2,1)S(1)}, bf16[1024,256]{1,0:T(8,128)(2,1)S(1)}, u32[]{:S(2)}, u32[]{:S(2)}) collective-permute-start(bf16[1024,256]{1,0:T(8,128)(2,1)S(1)} %get-tuple-element.314.refs_5_.refs_7_), channel_id=1, source_target_pairs={{0,1},{1,0},{2,3},{3,2},{4,5},{5,4},{6,7},{7,6},{8,9},{9,8},{10,11... | collective-permute-start | bytes 1572872 | tf_op jit(solution)/shard_map/ppermute | solution.py:83
  89.8 16.0 %collective-permute-start.35 = (bf16[2,128,1024]{2,1,0:T(8,128)(2,1)}, bf16[2,128,1024]{2,1,0:T(8,128)(2,1)S(1)}, u32[]{:S(2)}, u32[]{:S(2)}) collective-permute-start(bf16[2,128,1024]{2,1,0:T(8,128)(2,1)} %collective-permute-done.24.refs_0_), channel_id=1, source_target_pairs={{0,8},{4,12},{8,16},{12,20},{16,24},{20,28},{24,0},{28,4},{1,9},{5... | collective-permute-start | bytes 1572872 | tf_op jit(solution)/shard_map/ppermute | solution.py:169
  89.8 16.0 %collective-permute-start.36 = (bf16[2,128,1024]{2,1,0:T(8,128)(2,1)}, bf16[2,128,1024]{2,1,0:T(8,128)(2,1)S(1)}, u32[]{:S(2)}, u32[]{:S(2)}) collective-permute-start(bf16[2,128,1024]{2,1,0:T(8,128)(2,1)} %collective-permute-done.24.refs_0_), channel_id=1, source_target_pairs={{0,4},{4,0},{8,12},{12,8},{16,20},{20,16},{24,28},{28,24},{1,5},{5... | collective-permute-start | bytes 1572872 | tf_op jit(solution)/shard_map/ppermute | solution.py:175
  98.1 8.6 %collective-permute-start.32 = (bf16[128,1024]{1,0:T(8,128)(2,1)S(1)}, bf16[128,1024]{1,0:T(8,128)(2,1)S(1)}, u32[]{:S(2)}, u32[]{:S(2)}) collective-permute-start(bf16[128,1024]{1,0:T(8,128)(2,1)S(1)} %get-tuple-element.329), channel_id=1, source_target_pairs={{0,2},{1,3},{2,0},{3,1},{4,6},{5,7},{6,4},{7,5},{8,10},{9,11},{10,... | collective-permute-start | bytes 786440 | tf_op jit(solution)/shard_map/ppermute | solution.py:83
  106.7 12.8 %collective-permute-start.37 = (bf16[128,1024]{1,0:T(8,128)(2,1)S(1)}, bf16[128,1024]{1,0:T(8,128)(2,1)S(1)}, u32[]{:S(2)}, u32[]{:S(2)}) collective-permute-start(bf16[128,1024]{1,0:T(8,128)(2,1)S(1)} %get-tuple-element.329), channel_id=1, source_target_pairs={{0,1},{1,0},{2,3},{3,2},{4,5},{5,4},{6,7},{7,6},{8,9},{9,8},{10,11... | collective-permute-start | bytes 786440 | tf_op jit(solution)/shard_map/ppermute | solution.py:83
  107.8 8.8 %collective-permute-start.39 = (bf16[128,1024]{1,0:T(8,128)(2,1)S(1)}, bf16[128,1024]{1,0:T(8,128)(2,1)S(1)}, u32[]{:S(2)}, u32[]{:S(2)}) collective-permute-start(bf16[128,1024]{1,0:T(8,128)(2,1)S(1)} %slice_bitcast_fusion.1), channel_id=1, source_target_pairs={{0,4},{4,0},{8,12},{12,8},{16,20},{20,16},{24,28},{28,24},{1,5},{5... | collective-permute-start | bytes 786440 | tf_op jit(solution)/shard_map/ppermute | solution.py:175
  108.4 10.5 %collective-permute-start.40 = (bf16[128,1024]{1,0:T(8,128)(2,1)S(1)}, bf16[128,1024]{1,0:T(8,128)(2,1)S(1)}, u32[]{:S(2)}, u32[]{:S(2)}) collective-permute-start(bf16[128,1024]{1,0:T(8,128)(2,1)S(1)} %slice_bitcast_fusion), channel_id=1, source_target_pairs={{0,8},{4,12},{8,16},{12,20},{16,24},{20,28},{24,0},{28,4},{1,9},{5... | collective-permute-start | bytes 786440 | tf_op jit(solution)/shard_map/ppermute | solution.py:169
  108.7 10.9 %collective-permute-start.38 = (bf16[128,1024]{1,0:T(8,128)(2,1)S(1)}, bf16[128,1024]{1,0:T(8,128)(2,1)S(1)}, u32[]{:S(2)}, u32[]{:S(2)}) collective-permute-start(bf16[128,1024]{1,0:T(8,128)(2,1)S(1)} %collective-permute-done.32), channel_id=1, source_target_pairs={{0,1},{1,0},{2,3},{3,2},{4,5},{5,4},{6,7},{7,6},{8,9},{9,8},{10,11... | collective-permute-start | bytes 786440 | tf_op jit(solution)/shard_map/ppermute | solution.py:83
  128.3 14.8 %collective-permute-start.42 = (bf16[2,128,1024]{2,1,0:T(8,128)(2,1)S(1)}, bf16[2,128,1024]{2,1,0:T(8,128)(2,1)S(1)}, u32[]{:S(2)}, u32[]{:S(2)}) collective-permute-start(bf16[2,128,1024]{2,1,0:T(8,128)(2,1)S(1)} %get-tuple-element.345), channel_id=1, source_target_pairs={{0,4},{4,0},{8,12},{12,8},{16,20},{20,16},{24,28},{28,24},{1,5},{5... | collective-permute-start | bytes 1572872 | tf_op jit(solution)/shard_map/ppermute | solution.py:314
  130.3 12.9 %collective-permute-start.45 = (bf16[128,1024]{1,0:T(8,128)(2,1)S(1)}, bf16[128,1024]{1,0:T(8,128)(2,1)S(1)}, u32[]{:S(2)}, u32[]{:S(2)}) collective-permute-start(bf16[128,1024]{1,0:T(8,128)(2,1)S(1)} %get-tuple-element.355.refs_3_), channel_id=1, source_target_pairs={{0,2},{1,3},{2,0},{3,1},{4,6},{5,7},{6,4},{7,5},{8,10},{9,11},{10,... | collective-permute-start | bytes 786440 | tf_op jit(solution)/shard_map/ppermute | solution.py:83
  131.8 22.5 %collective-permute-start.41 = (bf16[2,128,1024]{2,1,0:T(8,128)(2,1)S(1)}, bf16[2,128,1024]{2,1,0:T(8,128)(2,1)S(1)}, u32[]{:S(2)}, u32[]{:S(2)}) collective-permute-start(bf16[2,128,1024]{2,1,0:T(8,128)(2,1)S(1)} %get-tuple-element.344), channel_id=1, source_target_pairs={{0,4},{4,0},{8,12},{12,8},{16,20},{20,16},{24,28},{28,24},{1,5},{5... | collective-permute-start | bytes 1572872 | tf_op jit(solution)/shard_map/ppermute | solution.py:314
  147.3 19.4 %collective-permute-start.51 = (bf16[2,128,1024]{2,1,0:T(8,128)(2,1)S(1)}, bf16[2,128,1024]{2,1,0:T(8,128)(2,1)S(1)}, u32[]{:S(2)}, u32[]{:S(2)}) collective-permute-start(bf16[2,128,1024]{2,1,0:T(8,128)(2,1)S(1)} %get-tuple-element.372), channel_id=1, source_target_pairs={{0,4},{4,0},{8,12},{12,8},{16,20},{20,16},{24,28},{28,24},{1,5},{5... | collective-permute-start | bytes 1572872 | tf_op jit(solution)/shard_map/ppermute | solution.py:314
  150.9 16.3 %collective-permute-start.43 = (bf16[2,128,1024]{2,1,0:T(8,128)(2,1)S(1)}, bf16[2,128,1024]{2,1,0:T(8,128)(2,1)S(1)}, u32[]{:S(2)}, u32[]{:S(2)}) collective-permute-start(bf16[2,128,1024]{2,1,0:T(8,128)(2,1)S(1)} %shard_map.266.refs_12_), channel_id=1, source_target_pairs={{0,8},{4,12},{8,0},{12,4},{16,24},{20,28},{24,16},{28,20},{1,9},{5... | collective-permute-start | bytes 1572872 | tf_op jit(solution)/shard_map/ppermute | solution.py:314
  165.1 14.8 %collective-permute-start.50 = (bf16[2,128,1024]{2,1,0:T(8,128)(2,1)S(1)}, bf16[2,128,1024]{2,1,0:T(8,128)(2,1)S(1)}, u32[]{:S(2)}, u32[]{:S(2)}) collective-permute-start(bf16[2,128,1024]{2,1,0:T(8,128)(2,1)S(1)} %get-tuple-element.371), channel_id=1, source_target_pairs={{0,4},{4,0},{8,12},{12,8},{16,20},{20,16},{24,28},{28,24},{1,5},{5... | collective-permute-start | bytes 1572872 | tf_op jit(solution)/shard_map/ppermute | solution.py:314
  166.8 19.7 %collective-permute-start.52 = (bf16[2,128,1024]{2,1,0:T(8,128)(2,1)S(1)}, bf16[2,128,1024]{2,1,0:T(8,128)(2,1)S(1)}, u32[]{:S(2)}, u32[]{:S(2)}) collective-permute-start(bf16[2,128,1024]{2,1,0:T(8,128)(2,1)S(1)} %shard_map.274), channel_id=1, source_target_pairs={{0,8},{4,12},{8,0},{12,4},{16,24},{20,28},{24,16},{28,20},{1,9},{5... | collective-permute-start | bytes 1572872 | tf_op jit(solution)/shard_map/ppermute | solution.py:314
  168.5 15.8 %collective-permute-start.49 = (bf16[1,128,1024]{2,1,0:T(8,128)(2,1)S(1)}, bf16[1,128,1024]{2,1,0:T(8,128)(2,1)S(1)}, u32[]{:S(2)}, u32[]{:S(2)}) collective-permute-start(bf16[1,128,1024]{2,1,0:T(8,128)(2,1)S(1)} %shard_map.273), channel_id=1, source_target_pairs={{0,16},{4,20},{8,24},{12,28},{16,0},{20,4},{24,8},{28,12},{1,17},{... | collective-permute-start | bytes 786440 | tf_op jit(solution)/shard_map/ppermute | solution.py:314
  172.9 13.6 %collective-permute-start.58 = (bf16[128,1024]{1,0:T(8,128)(2,1)S(1)}, bf16[128,1024]{1,0:T(8,128)(2,1)S(1)}, u32[]{:S(2)}, u32[]{:S(2)}) collective-permute-start(bf16[128,1024]{1,0:T(8,128)(2,1)S(1)} %get-tuple-element.379), channel_id=1, source_target_pairs={{0,2},{1,3},{2,0},{3,1},{4,6},{5,7},{6,4},{7,5},{8,10},{9,11},{10,... | collective-permute-start | bytes 786440 | tf_op jit(solution)/shard_map/ppermute | solution.py:83
  173.5 23.2 %collective-permute-start.61 = (bf16[4,128,768]{2,1,0:T(8,128)(2,1)S(1)}, bf16[4,128,768]{2,1,0:T(8,128)(2,1)S(1)}, u32[]{:S(2)}, u32[]{:S(2)}) collective-permute-start(bf16[4,128,768]{2,1,0:T(8,128)(2,1)S(1)} %get-tuple-element.385), channel_id=1, source_target_pairs={{0,4},{4,0},{8,12},{12,8},{16,20},{20,16},{24,28},{28,24},{1,5},{5... | collective-permute-start | bytes 2359304 | tf_op jit(solution)/shard_map/ppermute | solution.py:314
  187.9 8.7 %collective-permute-start.62 = (bf16[128,1024]{1,0:T(8,128)(2,1)S(1)}, bf16[128,1024]{1,0:T(8,128)(2,1)S(1)}, u32[]{:S(2)}, u32[]{:S(2)}) collective-permute-start(bf16[128,1024]{1,0:T(8,128)(2,1)S(1)} %get-tuple-element.416.refs_1_), channel_id=1, source_target_pairs={{0,2},{1,3},{2,0},{3,1},{4,6},{5,7},{6,4},{7,5},{8,10},{9,11},{10,... | collective-permute-start | bytes 786440 | tf_op jit(solution)/shard_map/ppermute | solution.py:83
  188.7 13.9 %collective-permute-start.60 = (bf16[1,128,1024]{2,1,0:T(8,128)(2,1)S(1)}, bf16[1,128,1024]{2,1,0:T(8,128)(2,1)S(1)}, u32[]{:S(2)}, u32[]{:S(2)}) collective-permute-start(bf16[1,128,1024]{2,1,0:T(8,128)(2,1)S(1)} %shard_map.276), channel_id=1, source_target_pairs={{0,16},{4,20},{8,24},{12,28},{16,0},{20,4},{24,8},{28,12},{1,17},{... | collective-permute-start | bytes 786440 | tf_op jit(solution)/shard_map/ppermute | solution.py:314
  205.2 14.5 %collective-permute-start.65 = (bf16[2,128,768]{2,1,0:T(8,128)(2,1)S(1)}, bf16[2,128,768]{2,1,0:T(8,128)(2,1)S(1)}, u32[]{:S(2)}, u32[]{:S(2)}) collective-permute-start(bf16[2,128,768]{2,1,0:T(8,128)(2,1)S(1)} %shard_map.280), channel_id=1, source_target_pairs={{0,8},{4,12},{8,0},{12,4},{16,24},{20,28},{24,16},{28,20},{1,9},{5... | collective-permute-start | bytes 1179656 | tf_op jit(solution)/shard_map/ppermute | solution.py:314
  205.3 8.5 %collective-permute-start.66 = (bf16[2,128,256]{2,1,0:T(8,128)(2,1)S(1)}, bf16[2,128,256]{2,1,0:T(8,128)(2,1)S(1)}, u32[]{:S(2)}, u32[]{:S(2)}) collective-permute-start(bf16[2,128,256]{2,1,0:T(8,128)(2,1)S(1)} %get-tuple-element.425.refs_1_), channel_id=1, source_target_pairs={{0,1},{1,0},{2,3},{3,2},{4,5},{5,4},{6,7},{7,6},{8,9},{9,8},{10,11... | collective-permute-start | bytes 393224 | tf_op jit(solution)/shard_map/ppermute | solution.py:83
  210.6 9.2 %collective-permute-start.72 = (bf16[128,1024]{1,0:T(8,128)(2,1)S(1)}, bf16[128,1024]{1,0:T(8,128)(2,1)S(1)}, u32[]{:S(2)}, u32[]{:S(2)}) collective-permute-start(bf16[128,1024]{1,0:T(8,128)(2,1)S(1)} %get-tuple-element.412), channel_id=1, source_target_pairs={{0,2},{1,3},{2,0},{3,1},{4,6},{5,7},{6,4},{7,5},{8,10},{9,11},{10,... | collective-permute-start | bytes 786440 | tf_op jit(solution)/shard_map/ppermute | solution.py:83
  213.8 8.4 %collective-permute-start.76 = (bf16[4,128,256]{2,1,0:T(8,128)(2,1)S(1)}, bf16[4,128,256]{2,1,0:T(8,128)(2,1)S(1)}, u32[]{:S(2)}, u32[]{:S(2)}) collective-permute-start(bf16[4,128,256]{2,1,0:T(8,128)(2,1)S(1)} %get-tuple-element.423), channel_id=1, source_target_pairs={{0,4},{4,0},{8,12},{12,8},{16,20},{20,16},{24,28},{28,24},{1,5},{5... | collective-permute-start | bytes 786440 | tf_op jit(solution)/shard_map/ppermute | solution.py:314
  219.8 12.8 %collective-permute-start.73 = (bf16[1,128,768]{2,1,0:T(8,128)(2,1)S(1)}, bf16[1,128,768]{2,1,0:T(8,128)(2,1)S(1)}, u32[]{:S(2)}, u32[]{:S(2)}) collective-permute-start(bf16[1,128,768]{2,1,0:T(8,128)(2,1)S(1)} %shard_map.282), channel_id=1, source_target_pairs={{0,16},{4,20},{8,24},{12,28},{16,0},{20,4},{24,8},{28,12},{1,17},{... | collective-permute-start | bytes 589832 | tf_op jit(solution)/shard_map/ppermute | solution.py:314
  222.3 10.3 %collective-permute-start.77 = (bf16[2,128,256]{2,1,0:T(8,128)(2,1)S(1)}, bf16[2,128,256]{2,1,0:T(8,128)(2,1)S(1)}, u32[]{:S(2)}, u32[]{:S(2)}) collective-permute-start(bf16[2,128,256]{2,1,0:T(8,128)(2,1)S(1)} %shard_map.284), channel_id=1, source_target_pairs={{0,8},{4,12},{8,0},{12,4},{16,24},{20,28},{24,16},{28,20},{1,9},{5... | collective-permute-start | bytes 393224 | tf_op jit(solution)/shard_map/ppermute | solution.py:314
  222.4 10.2 %collective-permute-start.78 = (f32[12,1024]{1,0:T(8,128)S(1)}, f32[12,1024]{1,0:T(8,128)S(1)}, u32[]{:S(2)}, u32[]{:S(2)}) collective-permute-start(f32[12,1024]{1,0:T(8,128)S(1)} %add.281), channel_id=1, source_target_pairs={{0,8},{4,12},{8,0},{12,4},{16,24},{20,28},{24,16},{28,20},{1,9},{5... | collective-permute-start | bytes 147464 | tf_op jit(solution)/shard_map/ppermute | solution.py:314
  233.3 10.6 %collective-permute-start.79 = (f32[12,1024]{1,0:T(8,128)}, f32[12,1024]{1,0:T(8,128)}, u32[]{:S(2)}, u32[]{:S(2)}) collective-permute-start(f32[12,1024]{1,0:T(8,128)} %add.282), channel_id=1, source_target_pairs={{0,16},{4,20},{8,24},{12,28},{16,0},{20,4},{24,8},{28,12},{1,17},{... | collective-permute-start | bytes 147464 | tf_op jit(solution)/shard_map/ppermute | solution.py:314
  236.7 10.0 %collective-permute-start.83 = (bf16[1,128,256]{2,1,0:T(8,128)(2,1)S(1)}, bf16[1,128,256]{2,1,0:T(8,128)(2,1)S(1)}, u32[]{:S(2)}, u32[]{:S(2)}) collective-permute-start(bf16[1,128,256]{2,1,0:T(8,128)(2,1)S(1)} %shard_map.289), channel_id=1, source_target_pairs={{0,16},{4,20},{8,24},{12,28},{16,0},{20,4},{24,8},{28,12},{1,17},{... | collective-permute-start | bytes 196616 | tf_op jit(solution)/shard_map/ppermute | solution.py:314
  (82 other events, 646.4 us)
where the time goes:
time: 249 us; the launch traced here: 248 us
  waiting for transfers between devices  101 us (41%)
  starting transfers between devices  65.6 us (26%)
  Pallas kernels  48.6 us (20%)
  local copies, waits for them, and re-layouts  21.4 us (9%)
  other arithmetic  9.25 us (4%)
    ppermute x46, waiting for transfers between devices, ctx_swap(): return lax.ppermute(x, 'ctx', [(i, i ^ bit) for i in range(count)])  46.3 us
    pallas_call x28, Pallas kernels, call(): pl.pallas_call(body, out_shape=[jax.ShapeDtypeStruct(shape, dtype) for sh...  40.4 us
    ppermute x17, waiting for transfers between devices, dp_swap(): return lax.ppermute(x, 'dp', [(i, i ^ bit) for i in range(count)])  33.2 us
    ppermute x46, starting transfers between devices, ctx_swap(): return lax.ppermute(x, 'ctx', [(i, i ^ bit) for i in range(count)])  22.6 us
    ppermute x17, starting transfers between devices, dp_swap(): return lax.ppermute(x, 'dp', [(i, i ^ bit) for i in range(count)])  15.7 us
    unnamed x102, local copies, waits for them, and re-layouts  13.6 us
    ppermute x8, waiting for transfers between devices, ring_y(): lax.ppermute(x, 'dp', [(i, i // y_count * y_count + (i + 1) % y_count) fo...  11.7 us
    ppermute x7, waiting for transfers between devices, ring_z(): lax.ppermute(x, 'dp', [(i, (i + y_count) % count) for i in range(count)])  9.83 us
  transfers between devices with their start and end apart: 84, of which 36 were waited for; matrix products, arithmetic and copies ran while one was open for 7% of the time, Pallas kernels for 16%

commit v1 on v0

--- a/solution.py
+++ b/solution.py
@@ -341,12 +341,25 @@
     def step(self, *earlier):
         self.size //= 2
         terms, self.first = self.first or self.terms, None
+        last = len(self.bits) == 1
 
         def write(ids, i, block, refs):
             refs[0][i] = block.astype(BF)
 
-        shape = (self.size,) + terms[0][0].shape[1:]
-        (send,) = combine(terms, self.size, self.size, [(shape, BF)], write, earlier)
+        def write_both(ids, i, block, refs):
+            if i:
+                refs[0][0] = block.astype(BF)
+            else:
+                refs[1][0] = block
+
+        block = terms[0][0].shape[1:]
+        if last and terms is self.terms:
+            outs = [((1,) + block, BF), ((1,) + block, F32)]
+            send, own = combine(terms, 0, 2, outs, write_both, earlier)
+            self.terms = [(own, 0)]
+        else:
+            outs = [((self.size,) + block, BF)]
+            (send,) = combine(terms, self.size, self.size, outs, write, earlier)
         self.terms.append((dp_swap(send, self.bits.pop(0)), 0))
         return send
 
@@ -390,20 +403,6 @@
         for k in range(ctx):
             value = block[:, k * part : (k + 1) * part].astype(BF)
             put_piece_at(*refs, jnp.bitwise_xor(ids[0], k), value)
-
-    return write
-
-
-def kind_pieces(ctx):
-
-    def write(ids, i, block, refs):
-        part = block.shape[1] // 3
-        for j in range(3):
-            kind = lax.rem((j + 3 * ctx - ids[0]) * ctx, 3)
-            value = block[:, :part]
-            for k in range(1, 3):
-                value = jnp.where(kind == k, block[:, k * part : (k + 1) * part], value)
-            refs[j][...] = value.astype(BF)
 
     return write
 
@@ -505,9 +504,9 @@
 
 
 def attention_backward(
-    ids, slopes, ln1_all, qkv, attn, pieces, lse, tokens_col, tokens_row, unit, dps, earlier=()
+    ids, slopes, qkv, attn, pieces, lse, tokens_col, tokens_row, unit, earlier=()
 ):
-    seq, width = ln1_all.shape
+    seq = qkv.shape[0]
     ctx = len(pieces)
     order = ctx_order(ctx)
     rows = seq // ctx
@@ -515,8 +514,8 @@
     heads = unit // HEAD_DIM
     inv_root = 1.0 / math.sqrt(HEAD_DIM)
 
-    def kernel(ids, slopes, x_ref, qkv_ref, attn_ref, lse_ref, col_ref, row_ref, *refs):
-        out_ref, sum_ref, *block_refs, total_ref, grad_ref = refs[ctx:]
+    def kernel(ids, slopes, qkv_ref, attn_ref, lse_ref, col_ref, row_ref, *refs):
+        out_ref, sum_ref, *kind_refs, total_ref, grad_ref = refs[ctx:]
         for i, r in enumerate(order):
             grad_ref[i * rows : (i + 1) * rows, :] = refs[r][pieces[r][1]]
         for lo in range(0, seq, tile):
@@ -544,12 +543,20 @@
         total = total_ref[...]
         out_ref[...] = total.astype(BF)
         sum_ref[...] = jnp.sum(total, axis=0, keepdims=True)
-        grad_blocks(ids, x_ref, out_ref[...], *block_refs)
-
-    return call(
-        kernel,
-        [((seq, 3 * unit), BF), ((1, 3 * unit), F32)] + block_shapes(dps, width // dps, 3 * unit, 1),
-        [ids, slopes, ln1_all, qkv, attn, lse, tokens_col, tokens_row]
+        for j in range(3):
+            slot = j
+            if ctx == 4 and j != 1:
+                slot = jnp.where(lax.rem(ids[0], 2) == 0, j, 2 - j)
+            kind = lax.rem((slot + 3 * ctx - ids[0]) * ctx, 3)
+            value = out_ref[:, :unit]
+            for k in range(1, 3):
+                value = jnp.where(kind == k, out_ref[:, k * unit : (k + 1) * unit], value)
+            kind_refs[j][...] = value
+
+    return call(
+        kernel,
+        [((seq, 3 * unit), BF), ((1, 3 * unit), F32)] + [((seq, unit), BF)] * 3,
+        [ids, slopes, qkv, attn, lse, tokens_col, tokens_row]
         + [array for array, _ in pieces],
         scalars=2,
         work=28 * tile * seq,
@@ -605,11 +612,17 @@
     )
 
 
-def feed_forward_hidden(ids, ln2_all, full_up, unit_bias, cot_all, dps):
-    seq, width = ln2_all.shape
+def feed_forward_hidden(ids, ln2_parts, full_up, unit_bias, cot_parts, dps, earlier=()):
+    ctx = len(ln2_parts)
+    rows, width = ln2_parts[0].shape
+    seq = rows * ctx
     units = full_up.shape[1]
 
-    def kernel(ids, x_ref, up_ref, bias_ref, cot_ref, hidden_ref, slope_ref, *block_refs):
+    def kernel(ids, up_ref, bias_ref, *refs):
+        x_ref, cot_ref, hidden_ref, slope_ref, *block_refs = refs[2 * ctx :]
+        for i in range(ctx):
+            x_ref[i * rows : (i + 1) * rows, :] = refs[i][...]
+            cot_ref[i * rows : (i + 1) * rows, :] = refs[ctx + i][...]
         forward, slope = gelu_both(dot(x_ref[...], up_ref[...]) + bias_ref[...])
         slope_ref[...] = slope
         hidden_ref[...] = forward.astype(BF)
@@ -617,9 +630,11 @@
 
     return call(
         kernel,
-        [((seq, units), BF), ((seq, units), F32)] + block_shapes(dps, units // dps, width, 2),
-        [ids, ln2_all, full_up, unit_bias, cot_all],
+        [((seq, width), BF), ((seq, width), BF), ((seq, units), BF), ((seq, units), F32)]
+        + block_shapes(dps, units // dps, width, 2),
+        [ids, full_up, unit_bias, *ln2_parts, *cot_parts],
         work=16 * seq * units,
+        earlier=earlier,
     )
 
 
@@ -676,6 +691,56 @@
         scratch=[pltpu.VMEM((ctx * rows, width), BF), pltpu.VMEM((ctx * rows, unit), BF)],
         earlier=earlier,
     )
+
+
+def unit_blocks(ids, left, kinds, dps):
+    seq, width = left.shape
+    unit = kinds[0].shape[1]
+    ctx = width // unit
+    rows = seq // ctx
+    bits = ctx_bits(ctx)
+
+    def kernel(ids, left_ref, *refs):
+        kind_refs, block_refs, right_ref = refs[:3], refs[3:-1], refs[-1]
+        if ctx == 4:
+            even = lax.rem(ids[0], 2) == 0
+            for i in range(ctx):
+                at = slice(i * rows, (i + 1) * rows)
+                stayed = kind_refs[0][at, :]
+                crossed = kind_refs[2][(i ^ 1) * rows : ((i ^ 1) + 1) * rows, :]
+                right_ref[at, :unit] = jnp.where(even, stayed, crossed)
+                right_ref[at, unit : 2 * unit] = kind_refs[1][
+                    (i ^ 2) * rows : ((i ^ 2) + 1) * rows, :
+                ]
+                right_ref[at, 2 * unit :] = jnp.where(even, crossed, stayed)
+        for j in range(3 if ctx != 4 else 0):
+            apart = jnp.bitwise_xor(ids[0], lax.rem(3 * ids[0] + j, ctx))
+            shift = 0
+            for i, bit in enumerate(bits):
+                shift = shift + lax.div(jnp.bitwise_and(apart, bit), bit) * (1 << i)
+            for i in range(ctx):
+                at = pl.multiple_of(jnp.bitwise_xor(shift, i) * rows, rows)
+                right_ref[i * rows : (i + 1) * rows, j * unit : (j + 1) * unit] = kind_refs[j][
+                    pl.ds(at, rows), :
+                ]
+        grad_blocks(ids, left_ref, right_ref[...], *block_refs)
+
+    return call(
+        kernel,
+        block_shapes(dps, width // dps, 3 * unit, 1),
+        [ids, left, *kinds],
+        scratch=[pltpu.VMEM((seq, 3 * unit), BF)],
+    )
+
+
+def unit_columns_home(slots, c):
+    ctx = lax.axis_size("ctx")
+    if ctx != 4:
+        return [
+            lax.ppermute(slots[j], "ctx", [((3 * i + j) % ctx, i) for i in range(ctx)])
+            for j in range(3)
+        ]
+    return [slots[0], ctx_swap(slots[1], 1), ctx_swap(slots[2], 2)]
 
 
 def times_weight(x, weight, earlier=()):
@@ -839,16 +904,32 @@
     slots = [order.index(r) for r in range(ctx)]
     places = dp_places()
 
-    took = [
-        lax.ppermute(
-            w_qkv[:, j * unit : (j + 1) * unit], "ctx", [(i, (3 * i + j) % ctx) for i in range(ctx)]
+    if ctx == 4:
+        odd = c % 2
+        trio = w_qkv.reshape(w_qkv.shape[0], 3, unit)
+        stays = lax.dynamic_index_in_dim(trio, 2 * odd, 1, keepdims=False)
+        crossed = ctx_swap(lax.dynamic_index_in_dim(trio, 2 - 2 * odd, 1, keepdims=False), 2)
+        beside = ctx_swap(trio[:, 1], 1)
+        three = jnp.stack([stays, crossed, beside])
+        held = [(0, 2, 1), (2, 0, 1), (1, 0, 2), (1, 2, 0)]
+        place = [
+            sum(jnp.where(c == k, held[k][kind], 0) for k in range(4)) for kind in range(3)
+        ]
+        head_qkv = jnp.concatenate([pick(three, at) for at in place] + [w_out], axis=1)
+    else:
+        took = [
+            lax.ppermute(
+                w_qkv[:, j * unit : (j + 1) * unit],
+                "ctx",
+                [(i, (3 * i + j) % ctx) for i in range(ctx)],
+            )
+            for j in range(3)
+        ]
+        took = jnp.stack(took)
+        head_qkv = jnp.concatenate(
+            [pick(took, (kind * ctx + c) % 3) for kind in range(3)] + [w_out], axis=1
         )
-        for j in range(3)
-    ]
-    took = jnp.stack(took)
-    head_qkv = jnp.concatenate(
-        [pick(took, (kind * ctx + c) % 3) for kind in range(3)] + [w_out], axis=1
-    )
+
     normed1_out, normed1, inv_std1 = layer_norm(stream, ln1_gain, ln1_bias)
     ln1_act = normed1_out.astype(BF)
     cot_bf = upstream.astype(BF)
@@ -952,12 +1033,12 @@
         got = along_y(travel)
     for bit in lower:
         ln2_parts = gather_step(ln2_parts, bit)
-    ln2_all = jnp.concatenate(ln2_parts, axis=0)
-    cot_all = jnp.concatenate(cot_parts, axis=0)
     full_up, full_down = assemble(second_full, got, places[3 * y_count :], second_cuts)
     full_up = full_up.reshape(width, dps * sub)
     unit_bias = pick(jnp.moveaxis(up_bias.reshape(dps, ctx, sub), 1, 0), c).reshape(1, dps * sub)
-    hidden, slope, *grad_down = feed_forward_hidden(ids, ln2_all, full_up, unit_bias, cot_all, dps)
+    ln2_all, cot_all, hidden, slope, *grad_down = feed_forward_hidden(
+        ids, ln2_parts, full_up, unit_bias, cot_parts, dps
+    )
     pre_bf, up_bias_part, ln2_keep, ln2_send = feed_forward_grad(
         ids, slope, full_up, cot_all, full_down
     )
@@ -976,13 +1057,13 @@
         ln2_gain,
         upstream,
         out_parts,
-        earlier=[grad_up[0], down_sent],
+        earlier=[grad_up[0]],
     )
     grad_pieces = trade(grad_near, grad_far)
-    qkv_bf, qkv_sums, *grad_qkv = attention_backward(
+    cols = trade(*lax.optimization_barrier((col_near, col_far, grad_pieces[2][0]))[:2])
+    qkv_bf, qkv_sums, *kinds = attention_backward(
         ids,
         slopes,
-        ln1_all,
         qkv_heads,
         attn_heads,
         grad_pieces,
@@ -990,10 +1071,13 @@
         tokens_col,
         tokens_row,
         unit,
-        dps,
-        earlier=[down.terms[1][0]],
-    )
-    qkv = Reduction(grad_qkv)
+        earlier=[down_sent, down.terms[1][0]],
+    )
+    cols_got, qkv_bf, *kinds = lax.optimization_barrier(
+        ([a for a, _ in cols], qkv_bf, *kinds)
+    )
+    cols = [(a, i) for a, (_, i) in zip(cols_got, cols)]
+    kinds = unit_columns_home(kinds, c)
     ln1_keep, ln1_send, small = input_terms(
         ids, qkv_bf, full_qkv, normed_parts, qkv_sums, sums2, up_bias_part, sub
     )
@@ -1004,13 +1088,12 @@
         small = small + ctx_swap(small, bit)
     ln1_keep, ln1_send = scatter_first(ln1_keep, ln1_send)
 
-    ln1_keep, ln1_send, small = sync([], ln1_keep, ln1_send, small)
+    ln1_keep, ln1_send, small, kinds = sync([], ln1_keep, ln1_send, small, kinds)
+    qkv = Reduction(unit_blocks(ids, ln1_all, kinds, dps))
     ln1_keep, ln1_got = scatter_rest(ln1_keep, ln1_send)
     small_got = ctx_swap(small, top)
-    cols = trade(col_near, col_far)
-
-    cols_got, ln1_got, small_got = sync([down, up], [a for a, _ in cols], ln1_got, small_got)
-    cols = [(a, i) for a, (_, i) in zip(cols_got, cols)]
+
+    ln1_got, small_got = sync([down, up], ln1_got, small_got)
     small = small + small_got
     bits = dp_bits()
     small_got = dp_swap(small, bits[0])
@@ -1019,11 +1102,12 @@
         up.step()
     input_grad = input_backward(ln1_keep, ln1_got, normed1, inv_std1, ln1_gain, middle_grad)
     result_keep, result_send = scatter_first(*times_weight(hidden, full_down, earlier=[ln1_got]))
-    down_out = down.result(piece_shapes(ctx, sub, unit), column_pieces(ctx))
-
-    attn_parts, small_got, result_keep, result_send, down_out = sync(
-        [up, qkv], attn_parts, small_got, result_keep, result_send, down_out
-    )
+    down_home = trade(*down.result(piece_shapes(ctx, sub, unit), column_pieces(ctx)))
+
+    attn_parts, small_got, result_keep, result_send, down_got = sync(
+        [up, qkv], attn_parts, small_got, result_keep, result_send, [a for a, _ in down_home]
+    )
+    down_home = [(a, i) for a, (_, i) in zip(down_got, down_home)]
     qkv.step()
     small = small + small_got
     small_got = dp_swap(small, bits[1])
@@ -1034,13 +1118,10 @@
     result_keep, result_got = scatter_rest(result_keep, result_send)
     up_rows = w_up.shape[0]
     up_out = up.result(piece_shapes(ctx, up_rows, dps * sub // ctx), column_pieces(ctx))
-    up_home, down_home = trade(*up_out), trade(*down_out)
-
-    up_got, down_got, result_got = sync(
-        [qkv], [a for a, _ in up_home], [a for a, _ in down_home], result_got
-    )
+    up_home = trade(*up_out)
+
+    up_got, result_got = sync([qkv], [a for a, _ in up_home], result_got)
     up_home = [(a, i) for a, (_, i) in zip(up_got, up_home)]
-    down_home = [(a, i) for a, (_, i) in zip(down_got, down_home)]
     while qkv.bits:
         qkv.step()
     out.step()
@@ -1050,21 +1131,13 @@
     result = add_result(middle, result_keep, result_got, down_bias)
 
     small_got, shard_up, shard_down, result = sync([qkv, out], small_got, shard_up, shard_down, result)
-    qkv_out = qkv.result([((up_rows, unit), BF)] * 3, kind_pieces(ctx))
+    shard_qkv = qkv.result([(w_qkv.shape, F32)], store_block)[0]
     while out.bits:
         out.step()
     small = small + small_got
     for bit in bits[2:]:
         small = small + dp_swap(small, bit)
     sum_out = out.result([((up_rows, unit), F32)], store_block)[0]
-
-    shard_qkv = jnp.concatenate(
-        [
-            lax.ppermute(qkv_out[j], "ctx", [((3 * i + j) % ctx, i) for i in range(ctx)])
-            for j in range(3)
-        ],
-        axis=1,
-    ).astype(F32)
 
     return (
         result[None],

time: 249 us -> 233 us (0.936)
  starting transfers between devices: 65.6 us -> 57.5 us
  local copies, waits for them, and re-layouts: 21.4 us -> 15.5 us
    ppermute x17, waiting for transfers between devices: 33.2 us -> 22.4 us  [dp_swap(): return lax.ppermute(x, 'dp', [(i, i ^ bit) for i in range(count)])]
    ppermute x6 -> x0, starting transfers between devices: 10.8 us -> none  [the longest x3 6.66 us: per_device(): lax.ppermute(w_qkv[:, j * unit:(j + 1) * unit], 'ctx', [(i, (3 * i + j) %...]
    ppermute x46 -> x50, waiting for transfers between devices: 46.3 us -> 55.5 us  [ctx_swap(): return lax.ppermute(x, 'ctx', [(i, i ^ bit) for i in range(count)])]
    unnamed x102 -> x93, local copies, waits for them, and re-layouts: 13.6 us -> 7.55 us
    pallas_call x28 -> x29, Pallas kernels: 40.4 us -> 42.3 us  [call(): pl.pallas_call(body, out_shape=[jax.ShapeDtypeStruct(shape, dtype) for sh...]
    ppermute x46 -> x50, starting transfers between devices: 22.6 us -> 23.5 us  [ctx_swap(): return lax.ppermute(x, 'ctx', [(i, i ^ bit) for i in range(count)])]
  transfers between devices with their start and end apart: 84 -> 82, of which waited for: 36 -> 34; matrix products, arithmetic and copies ran while one was open for 7% -> 6% of each run, Pallas kernels for 16% -> 18%
where the time goes in v1:
time: 233 us
  waiting for transfers between devices  100 us (43%)
  starting transfers between devices  57.5 us (25%)
  Pallas kernels  50.4 us (22%)
  local copies, waits for them, and re-layouts  15.5 us (7%)
  other arithmetic  6.96 us (3%)
    ppermute x50, waiting for transfers between devices, ctx_swap(): return lax.ppermute(x, 'ctx', [(i, i ^ bit) for i in range(count)])  55.5 us
    pallas_call x29, Pallas kernels, call(): pl.pallas_call(body, out_shape=[jax.ShapeDtypeStruct(shape, dtype) for sh...  42.3 us
    ppermute x50, starting transfers between devices, ctx_swap(): return lax.ppermute(x, 'ctx', [(i, i ^ bit) for i in range(count)])  23.5 us
    ppermute x17, waiting for transfers between devices, dp_swap(): return lax.ppermute(x, 'dp', [(i, i ^ bit) for i in range(count)])  22.4 us
    ppermute x17, starting transfers between devices, dp_swap(): return lax.ppermute(x, 'dp', [(i, i ^ bit) for i in range(count)])  16.3 us
    ppermute x8, waiting for transfers between devices, ring_y(): lax.ppermute(x, 'dp', [(i, i // y_count * y_count + (i + 1) % y_count) fo...  12.4 us
    ppermute x7, waiting for transfers between devices, ring_z(): lax.ppermute(x, 'dp', [(i, (i + y_count) % count) for i in range(count)])  9.96 us
    ppermute x8, starting transfers between devices, ring_y(): lax.ppermute(x, 'dp', [(i, i // y_count * y_count + (i + 1) % y_count) fo...  9.16 us
  transfers between devices with their start and end apart: 82, of which 34 were waited for; matrix products, arithmetic and copies ran while one was open for 6% of the time, Pallas kernels for 18%

profile of v1, /device:TPU:0, one launch (start us, length us, event | category | flops | bytes accessed | tf_op | source)
XLA Modules:
  0.0 232.7 jit_solution(12751576618043641245)
XLA Ops:
  1.9 3.0 %collective-permute-start = (bf16[128,256]{0,1:T(8,128)(2,1)S(1)}, bf16[128,256]{0,1:T(8,128)(2,1)S(1)}, u32[]{:S(2)}, u32[]{:S(2)}) collective-permute-start(bf16[128,256]{0,1:T(8,128)(2,1)S(1)} %get-tuple-element.505), channel_id=1, source_target_pairs={{0,2},{1,3},{2,0},{3,1},{4,6},{5,7},{6,4},{7,5},{8,10},{9,11},{10,... | collective-permute-start | bytes 196616 | tf_op jit(solution)/shard_map/ppermute | solution.py:83
  10.5 1.6 collective-permute-start.2
  12.0 1.5 collective-permute-start.3
  15.7 3.2 %collective-permute-done.5 = bf16[2,2,128,256]{3,2,1,0:T(8,128)(2,1)S(1)} collective-permute-done((bf16[2,2,128,256]{3,2,1,0:T(8,128)(2,1)S(1)}, bf16[2,2,128,256]{3,2,1,0:T(8,128)(2,1)S(1)}, u32[]{:S(2)}, u32[]{:S(2)}) %collective-permute-start.5) | collective-permute-done | bytes 262176 | tf_op jit(solution)/shard_map/ppermute | solution.py:83
  19.6 4.7 %collective-permute-done.4.refs_7_ = bf16[128,1024]{1,0:T(8,128)(2,1)} collective-permute-done((bf16[128,1024]{1,0:T(8,128)(2,1)S(1)}, bf16[128,1024]{1,0:T(8,128)(2,1)}, u32[]{:S(2)}, u32[]{:S(2)}) %collective-permute-start.4) | collective-permute-done | bytes 262176 | tf_op jit(solution)/shard_map/ppermute | solution.py:83
  24.8 1.8 collective-permute-start.7
  26.6 1.5 collective-permute-start.8
  28.2 2.2 collective-permute-done.9
  34.5 4.0 %collective-permute-done.12.refs_7_ = bf16[128,1024]{1,0:T(8,128)(2,1)S(1)} collective-permute-done((bf16[128,1024]{1,0:T(8,128)(2,1)}, bf16[128,1024]{1,0:T(8,128)(2,1)S(1)}, u32[]{:S(2)}, u32[]{:S(2)}) %collective-permute-start.12) | collective-permute-done | bytes 262176 | tf_op jit(solution)/shard_map/ppermute | solution.py:83
  38.5 1.6 collective-permute-start.13
  40.2 1.5 collective-permute-start.14
  45.8 3.9 %collective-permute-done.15 = bf16[2,128,256]{2,1,0:T(8,128)(2,1)S(1)} collective-permute-done((bf16[2,128,256]{2,1,0:T(8,128)(2,1)S(1)}, bf16[2,128,256]{2,1,0:T(8,128)(2,1)S(1)}, u32[]{:S(2)}, u32[]{:S(2)}) %collective-permute-start.15) | collective-permute-done | bytes 131104 | tf_op jit(solution)/shard_map/ppermute | solution.py:83
  50.5 1.6 collective-permute-start.18
  52.6 1.6 collective-permute-start.20
  59.4 4.3 %collective-permute-done.21 = bf16[2,128,256]{2,1,0:T(8,128)(2,1)} collective-permute-done((bf16[2,128,256]{2,1,0:T(8,128)(2,1)}, bf16[2,128,256]{2,1,0:T(8,128)(2,1)}, u32[]{:S(2)}, u32[]{:S(2)}) %collective-permute-start.21) | collective-permute-done | bytes 131104 | tf_op jit(solution)/shard_map/ppermute | solution.py:83
  63.7 7.1 %collective-permute-done.20.refs_1_ = bf16[128,1024]{1,0:T(8,128)(2,1)} collective-permute-done((bf16[128,1024]{1,0:T(8,128)(2,1)}, bf16[128,1024]{1,0:T(8,128)(2,1)}, u32[]{:S(2)}, u32[]{:S(2)}) %collective-permute-start.20) | collective-permute-done | bytes 262176 | tf_op jit(solution)/shard_map/ppermute | solution.py:175
  70.8 1.6 collective-permute-start.23
  78.9 4.3 %shard_map.258 = (bf16[512,1024]{1,0:T(8,128)(2,1)S(1)}, bf16[512,768]{1,0:T(8,128)(2,1)S(1)}, bf16[512,256]{1,0:T(8,128)(2,1)S(1)}, f32[512,4]{1,0:T(8,128)S(1)...) custom-call(s32[2]{0:T(128)S(1)} %pad_add_fusion.refs_0_, f32[4]{0:T(128)S(1)} %multiply_exponential_fusion.refs_1_, ...), custom_call_target="tpu_custom_call" | custom-call | tf_op jit(solution)/shard_map/pallas_call | solution.py:234
  83.1 1.7 collective-permute-done.23.refs_0_
  89.4 3.9 %collective-permute-done.27.refs_3_ = bf16[2,128,256]{2,1,0:T(8,128)(2,1)S(1)} collective-permute-done((bf16[2,128,256]{2,1,0:T(8,128)(2,1)S(1)}, bf16[2,128,256]{2,1,0:T(8,128)(2,1)S(1)}, u32[]{:S(2)}, u32[]{:S(2)}) %collective-permute-start.27) | collective-permute-done | bytes 131104 | tf_op jit(solution)/shard_map/ppermute | solution.py:83
  98.0 6.0 %collective-permute-done.34.refs_0_ = bf16[2,128,1024]{2,1,0:T(8,128)(2,1)S(1)} collective-permute-done((bf16[2,128,1024]{2,1,0:T(8,128)(2,1)}, bf16[2,128,1024]{2,1,0:T(8,128)(2,1)S(1)}, u32[]{:S(2)}, u32[]{:S(2)}) %collective-permute-start.34) | collective-permute-done | bytes 524320 | tf_op jit(solution)/shard_map/ppermute | solution.py:169
  107.3 5.3 %collective-permute-done.36 = bf16[128,1024]{1,0:T(8,128)(2,1)S(1)} collective-permute-done((bf16[128,1024]{1,0:T(8,128)(2,1)S(1)}, bf16[128,1024]{1,0:T(8,128)(2,1)S(1)}, u32[]{:S(2)}, u32[]{:S(2)}) %collective-permute-start.36) | collective-permute-done | bytes 262176 | tf_op jit(solution)/shard_map/ppermute | solution.py:175
  112.6 2.3 collective-permute-done.37
  115.5 6.1 %shard_map.265 = (bf16[512,1024]{1,0:T(8,128)(2,1)S(1)}, bf16[512,1024]{1,0:T(8,128)(2,1)S(1)}, bf16[512,1024]{1,0:T(8,128)(2,1)S(1)}, f32[512,1024]{1,0:T(8,128...) custom-call(s32[2]{0:T(128)S(1)} %pad_add_fusion.refs_0_, ...), custom_call_target="tpu_custom_call" | custom-call | tf_op jit(solution)/shard_map/pallas_call | solution.py:234
  121.6 2.9 %shard_map.267 = (bf16[512,1024]{1,0:T(8,128)(2,1)S(1)}, f32[1,1024]{1,0:T(1,128)S(1)}, f32[256,1024]{1,0:T(8,128)S(1)}, bf16[256,1024]{1,0:T(8,128)(2,1)S(1)}) custom-call(s32[2]{0:T(128)S(1)} %pad_add_fusion.refs_0_, f32[512,1024]{1,0:T(8,128)S(1)} %get-tuple-element.357.refs_1_, bf16[1024,1024]{1,0:T(8,128)(2,1)S(1)} %get-tuple-element.347.refs_1_.refs_2_, ...), custom_call_target="tpu_custom_call" | custom-call | tf_op jit(solution)/shard_map/pallas_call | solution.py:234
  124.6 1.6 collective-permute-start.41
  128.8 3.6 %shard_map.269 = (bf16[4,128,1024]{2,1,0:T(8,128)(2,1)S(1)}, bf16[2,128,1024]{2,1,0:T(8,128)(2,1)S(1)}, bf16[2,128,1024]{2,1,0:T(8,128)(2,1)S(1)}) custom-call(s32[2]{0:T(128)S(1)} %pad_add_fusion.refs_0_, bf16[512,1024]{1,0:T(8,128)(2,1)S(1)} %get-tuple-element.366.refs_1_, bf16[512,1024]{1,0:T(8,128)(2,1)S(1)} %get-tuple-element.367.refs_2_, ...), custom_call_target="tpu_custom_call" | custom-call | tf_op jit(solution)/shard_map/pallas_call | solution.py:234
  132.4 2.6 %collective-permute-done.44.refs_2_ = bf16[128,1024]{1,0:T(8,128)(2,1)S(1)} collective-permute-done((bf16[128,1024]{1,0:T(8,128)(2,1)S(1)}, bf16[128,1024]{1,0:T(8,128)(2,1)S(1)}, u32[]{:S(2)}, u32[]{:S(2)}) %collective-permute-start.44) | collective-permute-done | bytes 262176 | tf_op jit(solution)/shard_map/ppermute | solution.py:83
  135.1 1.9 shard_map.270
  137.9 4.1 %collective-permute-done.45.refs_9_ = bf16[2,128,256]{2,1,0:T(8,128)(2,1)S(1)} collective-permute-done((bf16[2,128,256]{2,1,0:T(8,128)(2,1)S(1)}, bf16[2,128,256]{2,1,0:T(8,128)(2,1)S(1)}, u32[]{:S(2)}, u32[]{:S(2)}) %collective-permute-start.45) | collective-permute-done | bytes 131104 | tf_op jit(solution)/shard_map/ppermute | solution.py:83
  144.3 6.3 %collective-permute-done.40.refs_12_.refs_2_ = bf16[2,128,1024]{2,1,0:T(8,128)(2,1)S(1)} collective-permute-done((bf16[2,128,1024]{2,1,0:T(8,128)(2,1)S(1)}, bf16[2,128,1024]{2,1,0:T(8,128)(2,1)S(1)}, u32[]{:S(2)}, u32[]{:S(2)}) %collective-permute-start.40) | collective-permute-done | bytes 524320 | tf_op jit(solution)/shard_map/ppermute | solution.py:314
  152.0 6.1 %shard_map.271 = (bf16[512,768]{1,0:T(8,128)(2,1)S(1)}, f32[1,768]{1,0:T(1,128)S(1)}, bf16[512,256]{1,0:T(8,128)(2,1)S(1)}, bf16[512,256]{1,0:T(8,128)(2,1)S(1)}, bf16[512,256]{1,0:T(8,128)(2,1)S(1)}) custom-call(s32[2]{0:T(128)S(1)} %pad_add_fusion.refs_0_, f32[4]{0:T(128)S(1)} %multiply_exponential_fusion.refs_1_, ...), custom_call_target="tpu_custom_call" | custom-call | tf_op jit(solution)/shard_map/pallas_call | solution.py:234
  158.2 2.1 shard_map.272
  160.5 1.5 collective-permute-start.52
  164.2 6.6 %collective-permute-done.58.refs_4_ = bf16[512,256]{1,0:T(8,128)(2,1)S(1)} collective-permute-done((bf16[512,256]{1,0:T(8,128)(2,1)S(1)}, bf16[512,256]{1,0:T(8,128)(2,1)S(1)}, u32[]{:S(2)}, u32[]{:S(2)}) %collective-permute-start.58) | collective-permute-done | bytes 262176 | tf_op jit(solution)/shard_map/ppermute | solution.py:83
  171.3 3.3 %shard_map.277 = (bf16[4,128,768]{2,1,0:T(8,128)(2,1)S(1)}, bf16[4,128,768]{2,1,0:T(8,128)(2,1)S(1)}) custom-call(s32[2]{0:T(128)S(1)} %pad_add_fusion.refs_0_, bf16[512,1024]{1,0:T(8,128)(2,1)S(1)} %get-tuple-element.409.refs_1_, bf16[512,256]{1,0:T(8,128)(2,1)S(1)} %get-tuple-element.410.refs_2_, bf16[512,256]{1,0:T(8,128)(2,1)S(1)} %collective-permute-done.57.refs_3_, ...), custom_call_target="tpu_custom_call" | custom-call | tf_op jit(solution)/shard_map/pallas_call | solution.py:234
  177.1 3.6 %collective-permute-done.51.refs_2_ = bf16[1,128,1024]{2,1,0:T(8,128)(2,1)S(1)} collective-permute-done((bf16[1,128,1024]{2,1,0:T(8,128)(2,1)S(1)}, bf16[1,128,1024]{2,1,0:T(8,128)(2,1)S(1)}, u32[]{:S(2)}, u32[]{:S(2)}) %collective-permute-start.51) | collective-permute-done | bytes 262176 | tf_op jit(solution)/shard_map/ppermute | solution.py:314
  180.7 2.2 collective-permute-done.54.refs_3_
  188.2 5.1 %collective-permute-done.63.refs_2_ = bf16[128,1024]{1,0:T(8,128)(2,1)S(1)} collective-permute-done((bf16[128,1024]{1,0:T(8,128)(2,1)S(1)}, bf16[128,1024]{1,0:T(8,128)(2,1)S(1)}, u32[]{:S(2)}, u32[]{:S(2)}) %collective-permute-start.63) | collective-permute-done | bytes 262176 | tf_op jit(solution)/shard_map/ppermute | solution.py:83
  193.4 2.4 %collective-permute-done.67.refs_7_ = bf16[2,128,256]{2,1,0:T(8,128)(2,1)S(1)} collective-permute-done((bf16[2,128,256]{2,1,0:T(8,128)(2,1)S(1)}, bf16[2,128,256]{2,1,0:T(8,128)(2,1)S(1)}, u32[]{:S(2)}, u32[]{:S(2)}) %collective-permute-start.67) | collective-permute-done | bytes 131104 | tf_op jit(solution)/shard_map/ppermute | solution.py:83
  196.5 3.8 %collective-permute-done.64 = f32[12,1024]{1,0:T(8,128)S(1)} collective-permute-done((f32[12,1024]{1,0:T(8,128)S(1)}, f32[12,1024]{1,0:T(8,128)S(1)}, u32[]{:S(2)}, u32[]{:S(2)}) %collective-permute-start.64) | collective-permute-done | bytes 49184 | tf_op jit(solution)/shard_map/ppermute | solution.py:314
  203.6 2.5 %shard_map.284 = (bf16[4,128,256]{2,1,0:T(8,128)(2,1)S(1)}, bf16[4,128,256]{2,1,0:T(8,128)(2,1)S(1)}) custom-call(s32[2]{0:T(128)S(1)} %pad_add_fusion.refs_0_, bf16[128,1024]{1,0:T(8,128)(2,1)S(1)} %get-tuple-element.441.refs_1_, bf16[128,1024]{1,0:T(8,128)(2,1)S(1)} %collective-permute-done.63.refs_2_, ...), custom_call_target="tpu_custom_call" | custom-call | tf_op jit(solution)/shard_map/pallas_call | solution.py:234
  209.2 3.3 %collective-permute-done.73.refs_3_ = bf16[128,1024]{1,0:T(8,128)(2,1)S(1)} collective-permute-done((bf16[128,1024]{1,0:T(8,128)(2,1)S(1)}, bf16[128,1024]{1,0:T(8,128)(2,1)S(1)}, u32[]{:S(2)}, u32[]{:S(2)}) %collective-permute-start.73) | collective-permute-done | bytes 262176 | tf_op jit(solution)/shard_map/ppermute | solution.py:83
  214.1 1.6 collective-permute-start.78
  217.1 1.6 shard_map.286
  218.7 3.5 %collective-permute-done.79 = f32[12,1024]{1,0:T(8,128)S(1)} collective-permute-done((f32[12,1024]{1,0:T(8,128)S(1)}, f32[12,1024]{1,0:T(8,128)S(1)}, u32[]{:S(2)}, u32[]{:S(2)}) %collective-permute-start.79) | collective-permute-done | bytes 49184 | tf_op jit(solution)/shard_map/ppermute | solution.py:314
  222.3 1.6 collective-permute-done.74.refs_2_
  226.8 1.5 collective-permute-start.81
  (322 shorter events, 78.9 us)
Async XLA Ops:
  9.8 9.2 %collective-permute-start.5 = (bf16[2,2,128,256]{3,2,1,0:T(8,128)(2,1)S(1)}, bf16[2,2,128,256]{3,2,1,0:T(8,128)(2,1)S(1)}, u32[]{:S(2)}, u32[]{:S(2)}) collective-permute-start(bf16[2,2,128,256]{3,2,1,0:T(8,128)(2,1)S(1)} %pad_maximum_fusion.3), channel_id=1, source_target_pairs={{0,2},{1,3},{2,0},{3,1},{4,6},{5,7},{6,4},{7,5},{8,10},{9,11},{10,... | collective-permute-start | bytes 786440 | tf_op jit(solution)/shard_map/ppermute | solution.py:83
  10.5 13.8 %collective-permute-start.2 = (bf16[128,1024]{1,0:T(8,128)(2,1)S(1)}, bf16[128,1024]{1,0:T(8,128)(2,1)}, u32[]{:S(2)}, u32[]{:S(2)}) collective-permute-start(bf16[128,1024]{1,0:T(8,128)(2,1)S(1)} %pad_maximum_fusion.2.refs_0_), channel_id=1, source_target_pairs={{0,8},{4,12},{8,16},{12,20},{16,24},{20,28},{24,0},{28,4},{1,9},{5... | collective-permute-start | bytes 786440 | tf_op jit(solution)/shard_map/ppermute | solution.py:169
  12.0 12.2 %collective-permute-start.3 = (bf16[128,1024]{1,0:T(8,128)(2,1)S(1)}, bf16[128,1024]{1,0:T(8,128)(2,1)S(1)}, u32[]{:S(2)}, u32[]{:S(2)}) collective-permute-start(bf16[128,1024]{1,0:T(8,128)(2,1)S(1)} %pad_maximum_fusion.2.refs_0_), channel_id=1, source_target_pairs={{0,4},{4,0},{8,12},{12,8},{16,20},{20,16},{24,28},{28,24},{1,5},{5... | collective-permute-start | bytes 786440 | tf_op jit(solution)/shard_map/ppermute | solution.py:175
  13.6 10.7 %collective-permute-start.4 = (bf16[128,1024]{1,0:T(8,128)(2,1)S(1)}, bf16[128,1024]{1,0:T(8,128)(2,1)}, u32[]{:S(2)}, u32[]{:S(2)}) collective-permute-start(bf16[128,1024]{1,0:T(8,128)(2,1)S(1)} %get-tuple-element.309.refs_6_), channel_id=1, source_target_pairs={{0,2},{1,3},{2,0},{3,1},{4,6},{5,7},{6,4},{7,5},{8,10},{9,11},{10,... | collective-permute-start | bytes 786440 | tf_op jit(solution)/shard_map/ppermute | solution.py:83
  24.8 13.7 %collective-permute-start.7 = (bf16[128,1024]{1,0:T(8,128)(2,1)}, bf16[128,1024]{1,0:T(8,128)(2,1)S(1)}, u32[]{:S(2)}, u32[]{:S(2)}) collective-permute-start(bf16[128,1024]{1,0:T(8,128)(2,1)} %collective-permute-done.2.refs_0_), channel_id=1, source_target_pairs={{0,8},{4,12},{8,16},{12,20},{16,24},{20,28},{24,0},{28,4},{1,9},{5... | collective-permute-start | bytes 786440 | tf_op jit(solution)/shard_map/ppermute | solution.py:169
  26.6 11.9 %collective-permute-start.8 = (bf16[128,1024]{1,0:T(8,128)(2,1)}, bf16[128,1024]{1,0:T(8,128)(2,1)S(1)}, u32[]{:S(2)}, u32[]{:S(2)}) collective-permute-start(bf16[128,1024]{1,0:T(8,128)(2,1)} %collective-permute-done.2.refs_0_), channel_id=1, source_target_pairs={{0,4},{4,0},{8,12},{12,8},{16,20},{20,16},{24,28},{28,24},{1,5},{5... | collective-permute-start | bytes 786440 | tf_op jit(solution)/shard_map/ppermute | solution.py:175
  30.4 8.1 %collective-permute-start.12 = (bf16[128,1024]{1,0:T(8,128)(2,1)}, bf16[128,1024]{1,0:T(8,128)(2,1)S(1)}, u32[]{:S(2)}, u32[]{:S(2)}) collective-permute-start(bf16[128,1024]{1,0:T(8,128)(2,1)} %convert_element_type.35.refs_6_), channel_id=1, source_target_pairs={{0,2},{1,3},{2,0},{3,1},{4,6},{5,7},{6,4},{7,5},{8,10},{9,11},{10,... | collective-permute-start | bytes 786440 | tf_op jit(solution)/shard_map/ppermute | solution.py:83
  30.7 11.0 %collective-permute-start.6 = (bf16[2,2,128,256]{3,2,1,0:T(8,128)(2,1)S(1)}, bf16[2,2,128,256]{3,2,1,0:T(8,128)(2,1)S(1)}, u32[]{:S(2)}, u32[]{:S(2)}) collective-permute-start(bf16[2,2,128,256]{3,2,1,0:T(8,128)(2,1)S(1)} %pad_maximum_fusion.4), channel_id=1, source_target_pairs={{0,1},{1,0},{2,3},{3,2},{4,5},{5,4},{6,7},{7,6},{8,9},{9,8},{10,11... | collective-permute-start | bytes 786440 | tf_op jit(solution)/shard_map/ppermute | solution.py:83
  38.5 11.2 %collective-permute-start.13 = (bf16[128,1024]{1,0:T(8,128)(2,1)S(1)}, bf16[128,1024]{1,0:T(8,128)(2,1)}, u32[]{:S(2)}, u32[]{:S(2)}) collective-permute-start(bf16[128,1024]{1,0:T(8,128)(2,1)S(1)} %collective-permute-done.7.refs_0_), channel_id=1, source_target_pairs={{0,8},{4,12},{8,16},{12,20},{16,24},{20,28},{24,0},{28,4},{1,9},{5... | collective-permute-start | bytes 786440 | tf_op jit(solution)/shard_map/ppermute | solution.py:169
  40.2 9.5 %collective-permute-start.14 = (bf16[128,1024]{1,0:T(8,128)(2,1)S(1)}, bf16[128,1024]{1,0:T(8,128)(2,1)S(1)}, u32[]{:S(2)}, u32[]{:S(2)}) collective-permute-start(bf16[128,1024]{1,0:T(8,128)(2,1)S(1)} %collective-permute-done.7.refs_0_), channel_id=1, source_target_pairs={{0,4},{4,0},{8,12},{12,8},{16,20},{20,16},{24,28},{28,24},{1,5},{5... | collective-permute-start | bytes 786440 | tf_op jit(solution)/shard_map/ppermute | solution.py:175
  50.5 20.3 %collective-permute-start.18 = (bf16[2,128,1024]{2,1,0:T(8,128)(2,1)}, bf16[2,128,1024]{2,1,0:T(8,128)(2,1)}, u32[]{:S(2)}, u32[]{:S(2)}) collective-permute-start(bf16[2,128,1024]{2,1,0:T(8,128)(2,1)} %pad_maximum_fusion.refs_0_), channel_id=1, source_target_pairs={{0,8},{4,12},{8,16},{12,20},{16,24},{20,28},{24,0},{28,4},{1,9},{5... | collective-permute-start | bytes 1572872 | tf_op jit(solution)/shard_map/ppermute | solution.py:169
  52.1 18.7 %collective-permute-start.19 = (bf16[2,128,1024]{2,1,0:T(8,128)(2,1)}, bf16[2,128,1024]{2,1,0:T(8,128)(2,1)}, u32[]{:S(2)}, u32[]{:S(2)}) collective-permute-start(bf16[2,128,1024]{2,1,0:T(8,128)(2,1)} %pad_maximum_fusion.refs_0_), channel_id=1, source_target_pairs={{0,4},{4,0},{8,12},{12,8},{16,20},{20,16},{24,28},{28,24},{1,5},{5... | collective-permute-start | bytes 1572872 | tf_op jit(solution)/shard_map/ppermute | solution.py:175
  52.6 18.2 %collective-permute-start.20 = (bf16[128,1024]{1,0:T(8,128)(2,1)}, bf16[128,1024]{1,0:T(8,128)(2,1)}, u32[]{:S(2)}, u32[]{:S(2)}) collective-permute-start(bf16[128,1024]{1,0:T(8,128)(2,1)} %collective-permute-done.13.refs_0_), channel_id=1, source_target_pairs={{0,4},{4,0},{8,12},{12,8},{16,20},{20,16},{24,28},{28,24},{1,5},{5... | collective-permute-start | bytes 786440 | tf_op jit(solution)/shard_map/ppermute | solution.py:175
  54.2 16.6 %collective-permute-start.22 = (bf16[128,1024]{1,0:T(8,128)(2,1)S(1)}, bf16[128,1024]{1,0:T(8,128)(2,1)}, u32[]{:S(2)}, u32[]{:S(2)}) collective-permute-start(bf16[128,1024]{1,0:T(8,128)(2,1)S(1)} %copy-done.5), channel_id=1, source_target_pairs={{0,2},{1,3},{2,0},{3,1},{4,6},{5,7},{6,4},{7,5},{8,10},{9,11},{10,... | collective-permute-start | bytes 786440 | tf_op jit(solution)/shard_map/ppermute | solution.py:83
  55.4 8.3 %collective-permute-start.21 = (bf16[2,128,256]{2,1,0:T(8,128)(2,1)}, bf16[2,128,256]{2,1,0:T(8,128)(2,1)}, u32[]{:S(2)}, u32[]{:S(2)}) collective-permute-start(bf16[2,128,256]{2,1,0:T(8,128)(2,1)} %pad_maximum_fusion.12), channel_id=1, source_target_pairs={{0,2},{1,3},{2,0},{3,1},{4,6},{5,7},{6,4},{7,5},{8,10},{9,11},{10,... | collective-permute-start | bytes 393224 | tf_op jit(solution)/shard_map/ppermute | solution.py:83
  70.8 14.0 %collective-permute-start.23 = (bf16[2,128,1024]{2,1,0:T(8,128)(2,1)}, bf16[2,128,1024]{2,1,0:T(8,128)(2,1)}, u32[]{:S(2)}, u32[]{:S(2)}) collective-permute-start(bf16[2,128,1024]{2,1,0:T(8,128)(2,1)} %collective-permute-done.18.refs_0_), channel_id=1, source_target_pairs={{0,8},{4,12},{8,16},{12,20},{16,24},{20,28},{24,0},{28,4},{1,9},{5... | collective-permute-start | bytes 1572872 | tf_op jit(solution)/shard_map/ppermute | solution.py:169
  72.5 12.4 %collective-permute-start.24 = (bf16[2,128,1024]{2,1,0:T(8,128)(2,1)}, bf16[2,128,1024]{2,1,0:T(8,128)(2,1)}, u32[]{:S(2)}, u32[]{:S(2)}) collective-permute-start(bf16[2,128,1024]{2,1,0:T(8,128)(2,1)} %collective-permute-done.18.refs_0_), channel_id=1, source_target_pairs={{0,4},{4,0},{8,12},{12,8},{16,20},{20,16},{24,28},{28,24},{1,5},{5... | collective-permute-start | bytes 1572872 | tf_op jit(solution)/shard_map/ppermute | solution.py:175
  75.3 7.8 %collective-permute-start.25 = (bf16[2,128,256]{2,1,0:T(8,128)(2,1)}, bf16[2,128,256]{2,1,0:T(8,128)(2,1)}, u32[]{:S(2)}, u32[]{:S(2)}) collective-permute-start(bf16[2,128,256]{2,1,0:T(8,128)(2,1)} %pad_maximum_fusion.13), channel_id=1, source_target_pairs={{0,2},{1,3},{2,0},{3,1},{4,6},{5,7},{6,4},{7,5},{8,10},{9,11},{10,... | collective-permute-start | bytes 393224 | tf_op jit(solution)/shard_map/ppermute | solution.py:83
  77.4 12.0 %collective-permute-start.29 = (bf16[1024,256]{1,0:T(8,128)(2,1)S(1)}, bf16[1024,256]{1,0:T(8,128)(2,1)S(1)}, u32[]{:S(2)}, u32[]{:S(2)}) collective-permute-start(bf16[1024,256]{1,0:T(8,128)(2,1)S(1)} %get-tuple-element.325.refs_5_.refs_7_), channel_id=1, source_target_pairs={{0,1},{1,0},{2,3},{3,2},{4,5},{5,4},{6,7},{7,6},{8,9},{9,8},{10,11... | collective-permute-start | bytes 1572872 | tf_op jit(solution)/shard_map/ppermute | solution.py:83
  88.0 16.0 %collective-permute-start.34 = (bf16[2,128,1024]{2,1,0:T(8,128)(2,1)}, bf16[2,128,1024]{2,1,0:T(8,128)(2,1)S(1)}, u32[]{:S(2)}, u32[]{:S(2)}) collective-permute-start(bf16[2,128,1024]{2,1,0:T(8,128)(2,1)} %collective-permute-done.23.refs_0_), channel_id=1, source_target_pairs={{0,8},{4,12},{8,16},{12,20},{16,24},{20,28},{24,0},{28,4},{1,9},{5... | collective-permute-start | bytes 1572872 | tf_op jit(solution)/shard_map/ppermute | solution.py:169
  88.0 16.0 %collective-permute-start.35 = (bf16[2,128,1024]{2,1,0:T(8,128)(2,1)}, bf16[2,128,1024]{2,1,0:T(8,128)(2,1)S(1)}, u32[]{:S(2)}, u32[]{:S(2)}) collective-permute-start(bf16[2,128,1024]{2,1,0:T(8,128)(2,1)} %collective-permute-done.23.refs_0_), channel_id=1, source_target_pairs={{0,4},{4,0},{8,12},{12,8},{16,20},{20,16},{24,28},{28,24},{1,5},{5... | collective-permute-start | bytes 1572872 | tf_op jit(solution)/shard_map/ppermute | solution.py:175
  96.1 8.6 %collective-permute-start.31 = (bf16[128,1024]{1,0:T(8,128)(2,1)S(1)}, bf16[128,1024]{1,0:T(8,128)(2,1)S(1)}, u32[]{:S(2)}, u32[]{:S(2)}) collective-permute-start(bf16[128,1024]{1,0:T(8,128)(2,1)S(1)} %get-tuple-element.348.refs_3_), channel_id=1, source_target_pairs={{0,2},{1,3},{2,0},{3,1},{4,6},{5,7},{6,4},{7,5},{8,10},{9,11},{10,... | collective-permute-start | bytes 786440 | tf_op jit(solution)/shard_map/ppermute | solution.py:83
  104.7 7.8 %collective-permute-start.36 = (bf16[128,1024]{1,0:T(8,128)(2,1)S(1)}, bf16[128,1024]{1,0:T(8,128)(2,1)S(1)}, u32[]{:S(2)}, u32[]{:S(2)}) collective-permute-start(bf16[128,1024]{1,0:T(8,128)(2,1)S(1)} %slice_bitcast_fusion.1), channel_id=1, source_target_pairs={{0,4},{4,0},{8,12},{12,8},{16,20},{20,16},{24,28},{28,24},{1,5},{5... | collective-permute-start | bytes 786440 | tf_op jit(solution)/shard_map/ppermute | solution.py:175
  105.3 9.5 %collective-permute-start.37 = (bf16[128,1024]{1,0:T(8,128)(2,1)S(1)}, bf16[128,1024]{1,0:T(8,128)(2,1)S(1)}, u32[]{:S(2)}, u32[]{:S(2)}) collective-permute-start(bf16[128,1024]{1,0:T(8,128)(2,1)S(1)} %slice_bitcast_fusion), channel_id=1, source_target_pairs={{0,8},{4,12},{8,16},{12,20},{16,24},{20,28},{24,0},{28,4},{1,9},{5... | collective-permute-start | bytes 786440 | tf_op jit(solution)/shard_map/ppermute | solution.py:169
  105.6 9.9 %collective-permute-start.38 = (bf16[128,1024]{1,0:T(8,128)(2,1)S(1)}, bf16[128,1024]{1,0:T(8,128)(2,1)S(1)}, u32[]{:S(2)}, u32[]{:S(2)}) collective-permute-start(bf16[128,1024]{1,0:T(8,128)(2,1)S(1)} %get-tuple-element.348.refs_3_), channel_id=1, source_target_pairs={{0,1},{1,0},{2,3},{3,2},{4,5},{5,4},{6,7},{7,6},{8,9},{9,8},{10,11... | collective-permute-start | bytes 786440 | tf_op jit(solution)/shard_map/ppermute | solution.py:83
  105.7 9.9 %collective-permute-start.39 = (bf16[128,1024]{1,0:T(8,128)(2,1)S(1)}, bf16[128,1024]{1,0:T(8,128)(2,1)S(1)}, u32[]{:S(2)}, u32[]{:S(2)}) collective-permute-start(bf16[128,1024]{1,0:T(8,128)(2,1)S(1)} %collective-permute-done.31.refs_4_), channel_id=1, source_target_pairs={{0,1},{1,0},{2,3},{3,2},{4,5},{5,4},{6,7},{7,6},{8,9},{9,8},{10,11... | collective-permute-start | bytes 786440 | tf_op jit(solution)/shard_map/ppermute | solution.py:83
  124.6 19.5 %collective-permute-start.41 = (bf16[2,128,1024]{2,1,0:T(8,128)(2,1)S(1)}, bf16[2,128,1024]{2,1,0:T(8,128)(2,1)S(1)}, u32[]{:S(2)}, u32[]{:S(2)}) collective-permute-start(bf16[2,128,1024]{2,1,0:T(8,128)(2,1)S(1)} %get-tuple-element.356), channel_id=1, source_target_pairs={{0,4},{4,0},{8,12},{12,8},{16,20},{20,16},{24,28},{28,24},{1,5},{5... | collective-permute-start | bytes 1572872 | tf_op jit(solution)/shard_map/ppermute | solution.py:314
  126.6 8.4 %collective-permute-start.44 = (bf16[128,1024]{1,0:T(8,128)(2,1)S(1)}, bf16[128,1024]{1,0:T(8,128)(2,1)S(1)}, u32[]{:S(2)}, u32[]{:S(2)}) collective-permute-start(bf16[128,1024]{1,0:T(8,128)(2,1)S(1)} %get-tuple-element.363.refs_3_), channel_id=1, source_target_pairs={{0,2},{1,3},{2,0},{3,1},{4,6},{5,7},{6,4},{7,5},{8,10},{9,11},{10,... | collective-permute-start | bytes 786440 | tf_op jit(solution)/shard_map/ppermute | solution.py:83
  127.5 23.1 %collective-permute-start.40 = (bf16[2,128,1024]{2,1,0:T(8,128)(2,1)S(1)}, bf16[2,128,1024]{2,1,0:T(8,128)(2,1)S(1)}, u32[]{:S(2)}, u32[]{:S(2)}) collective-permute-start(bf16[2,128,1024]{2,1,0:T(8,128)(2,1)S(1)} %get-tuple-element.355), channel_id=1, source_target_pairs={{0,4},{4,0},{8,12},{12,8},{16,20},{20,16},{24,28},{28,24},{1,5},{5... | collective-permute-start | bytes 1572872 | tf_op jit(solution)/shard_map/ppermute | solution.py:314
  137.9 12.8 %collective-permute-start.49 = (bf16[2,128,256]{2,1,0:T(8,128)(2,1)S(1)}, bf16[2,128,256]{2,1,0:T(8,128)(2,1)S(1)}, u32[]{:S(2)}, u32[]{:S(2)}) collective-permute-start(bf16[2,128,256]{2,1,0:T(8,128)(2,1)S(1)} %get-tuple-element.377.refs_7_), channel_id=1, source_target_pairs={{0,1},{1,0},{2,3},{3,2},{4,5},{5,4},{6,7},{7,6},{8,9},{9,8},{10,11... | collective-permute-start | bytes 393224 | tf_op jit(solution)/shard_map/ppermute | solution.py:83
  142.0 9.1 %collective-permute-start.47 = (bf16[2,128,256]{2,1,0:T(8,128)(2,1)S(1)}, bf16[2,128,256]{2,1,0:T(8,128)(2,1)S(1)}, u32[]{:S(2)}, u32[]{:S(2)}) collective-permute-start(bf16[2,128,256]{2,1,0:T(8,128)(2,1)S(1)} %get-tuple-element.373), channel_id=1, source_target_pairs={{0,2},{1,3},{2,0},{3,1},{4,6},{5,7},{6,4},{7,5},{8,10},{9,11},{10,... | collective-permute-start | bytes 393224 | tf_op jit(solution)/shard_map/ppermute | solution.py:83
  142.9 19.2 %collective-permute-start.53 = (bf16[2,128,1024]{2,1,0:T(8,128)(2,1)S(1)}, bf16[2,128,1024]{2,1,0:T(8,128)(2,1)S(1)}, u32[]{:S(2)}, u32[]{:S(2)}) collective-permute-start(bf16[2,128,1024]{2,1,0:T(8,128)(2,1)S(1)} %get-tuple-element.394), channel_id=1, source_target_pairs={{0,4},{4,0},{8,12},{12,8},{16,20},{20,16},{24,28},{28,24},{1,5},{5... | collective-permute-start | bytes 1572872 | tf_op jit(solution)/shard_map/ppermute | solution.py:314
  144.2 18.3 %collective-permute-start.42 = (bf16[2,128,1024]{2,1,0:T(8,128)(2,1)S(1)}, bf16[2,128,1024]{2,1,0:T(8,128)(2,1)S(1)}, u32[]{:S(2)}, u32[]{:S(2)}) collective-permute-start(bf16[2,128,1024]{2,1,0:T(8,128)(2,1)S(1)} %shard_map.266.refs_11_), channel_id=1, source_target_pairs={{0,8},{4,12},{8,0},{12,4},{16,24},{20,28},{24,16},{28,20},{1,9},{5... | collective-permute-start | bytes 1572872 | tf_op jit(solution)/shard_map/ppermute | solution.py:314
  160.5 15.1 %collective-permute-start.52 = (bf16[2,128,1024]{2,1,0:T(8,128)(2,1)S(1)}, bf16[2,128,1024]{2,1,0:T(8,128)(2,1)S(1)}, u32[]{:S(2)}, u32[]{:S(2)}) collective-permute-start(bf16[2,128,1024]{2,1,0:T(8,128)(2,1)S(1)} %get-tuple-element.393), channel_id=1, source_target_pairs={{0,4},{4,0},{8,12},{12,8},{16,20},{20,16},{24,28},{28,24},{1,5},{5... | collective-permute-start | bytes 1572872 | tf_op jit(solution)/shard_map/ppermute | solution.py:314
  162.5 8.3 %collective-permute-start.58 = (bf16[512,256]{1,0:T(8,128)(2,1)S(1)}, bf16[512,256]{1,0:T(8,128)(2,1)S(1)}, u32[]{:S(2)}, u32[]{:S(2)}) collective-permute-start(bf16[512,256]{1,0:T(8,128)(2,1)S(1)} %get-tuple-element.401), channel_id=1, source_target_pairs={{0,2},{1,3},{2,0},{3,1},{4,6},{5,7},{6,4},{7,5},{8,10},{9,11},{10,... | collective-permute-start | bytes 786440 | tf_op jit(solution)/shard_map/ppermute | solution.py:83
  163.3 19.6 %collective-permute-start.54 = (bf16[2,128,1024]{2,1,0:T(8,128)(2,1)S(1)}, bf16[2,128,1024]{2,1,0:T(8,128)(2,1)S(1)}, u32[]{:S(2)}, u32[]{:S(2)}) collective-permute-start(bf16[2,128,1024]{2,1,0:T(8,128)(2,1)S(1)} %shard_map.274), channel_id=1, source_target_pairs={{0,8},{4,12},{8,0},{12,4},{16,24},{20,28},{24,16},{28,20},{1,9},{5... | collective-permute-start | bytes 1572872 | tf_op jit(solution)/shard_map/ppermute | solution.py:314
  163.5 17.2 %collective-permute-start.51 = (bf16[1,128,1024]{2,1,0:T(8,128)(2,1)S(1)}, bf16[1,128,1024]{2,1,0:T(8,128)(2,1)S(1)}, u32[]{:S(2)}, u32[]{:S(2)}) collective-permute-start(bf16[1,128,1024]{2,1,0:T(8,128)(2,1)S(1)} %get-tuple-element.392), channel_id=1, source_target_pairs={{0,16},{4,20},{8,24},{12,28},{16,0},{20,4},{24,8},{28,12},{1,17},{... | collective-permute-start | bytes 786440 | tf_op jit(solution)/shard_map/ppermute | solution.py:314
  170.8 12.1 %collective-permute-start.59 = (bf16[128,1024]{1,0:T(8,128)(2,1)S(1)}, bf16[128,1024]{1,0:T(8,128)(2,1)S(1)}, u32[]{:S(2)}, u32[]{:S(2)}) collective-permute-start(bf16[128,1024]{1,0:T(8,128)(2,1)S(1)} %get-tuple-element.402), channel_id=1, source_target_pairs={{0,2},{1,3},{2,0},{3,1},{4,6},{5,7},{6,4},{7,5},{8,10},{9,11},{10,... | collective-permute-start | bytes 786440 | tf_op jit(solution)/shard_map/ppermute | solution.py:83
  174.6 26.0 %collective-permute-start.62 = (bf16[4,128,768]{2,1,0:T(8,128)(2,1)S(1)}, bf16[4,128,768]{2,1,0:T(8,128)(2,1)S(1)}, u32[]{:S(2)}, u32[]{:S(2)}) collective-permute-start(bf16[4,128,768]{2,1,0:T(8,128)(2,1)S(1)} %get-tuple-element.414), channel_id=1, source_target_pairs={{0,4},{4,0},{8,12},{12,8},{16,20},{20,16},{24,28},{28,24},{1,5},{5... | collective-permute-start | bytes 2359304 | tf_op jit(solution)/shard_map/ppermute | solution.py:314
  184.1 11.6 %collective-permute-start.65 = (bf16[256,1024]{1,0:T(8,128)(2,1)S(1)}, bf16[256,1024]{1,0:T(8,128)(2,1)S(1)}, u32[]{:S(2)}, u32[]{:S(2)}) collective-permute-start(bf16[256,1024]{1,0:T(8,128)(2,1)S(1)} %get-tuple-element.420), channel_id=1, source_target_pairs={{0,1},{1,0},{2,3},{3,2},{4,5},{5,4},{6,7},{7,6},{8,9},{9,8},{10,11... | collective-permute-start | bytes 1572872 | tf_op jit(solution)/shard_map/ppermute | solution.py:83
  184.2 9.2 %collective-permute-start.63 = (bf16[128,1024]{1,0:T(8,128)(2,1)S(1)}, bf16[128,1024]{1,0:T(8,128)(2,1)S(1)}, u32[]{:S(2)}, u32[]{:S(2)}) collective-permute-start(bf16[128,1024]{1,0:T(8,128)(2,1)S(1)} %get-tuple-element.441.refs_1_), channel_id=1, source_target_pairs={{0,2},{1,3},{2,0},{3,1},{4,6},{5,7},{6,4},{7,5},{8,10},{9,11},{10,... | collective-permute-start | bytes 786440 | tf_op jit(solution)/shard_map/ppermute | solution.py:83
  185.8 9.9 %collective-permute-start.67 = (bf16[2,128,256]{2,1,0:T(8,128)(2,1)S(1)}, bf16[2,128,256]{2,1,0:T(8,128)(2,1)S(1)}, u32[]{:S(2)}, u32[]{:S(2)}) collective-permute-start(bf16[2,128,256]{2,1,0:T(8,128)(2,1)S(1)} %get-tuple-element.426), channel_id=1, source_target_pairs={{0,2},{1,3},{2,0},{3,1},{4,6},{5,7},{6,4},{7,5},{8,10},{9,11},{10,... | collective-permute-start | bytes 393224 | tf_op jit(solution)/shard_map/ppermute | solution.py:83
  187.0 13.7 %collective-permute-start.61 = (bf16[1,128,1024]{2,1,0:T(8,128)(2,1)S(1)}, bf16[1,128,1024]{2,1,0:T(8,128)(2,1)S(1)}, u32[]{:S(2)}, u32[]{:S(2)}) collective-permute-start(bf16[1,128,1024]{2,1,0:T(8,128)(2,1)S(1)} %get-tuple-element.408), channel_id=1, source_target_pairs={{0,16},{4,20},{8,24},{12,28},{16,0},{20,4},{24,8},{28,12},{1,17},{... | collective-permute-start | bytes 786440 | tf_op jit(solution)/shard_map/ppermute | solution.py:314
  201.2 11.3 %collective-permute-start.69 = (bf16[2,128,768]{2,1,0:T(8,128)(2,1)S(1)}, bf16[2,128,768]{2,1,0:T(8,128)(2,1)S(1)}, u32[]{:S(2)}, u32[]{:S(2)}) collective-permute-start(bf16[2,128,768]{2,1,0:T(8,128)(2,1)S(1)} %shard_map.281), channel_id=1, source_target_pairs={{0,8},{4,12},{8,0},{12,4},{16,24},{20,28},{24,16},{28,20},{1,9},{5... | collective-permute-start | bytes 1179656 | tf_op jit(solution)/shard_map/ppermute | solution.py:314
  202.7 9.9 %collective-permute-start.73 = (bf16[128,1024]{1,0:T(8,128)(2,1)S(1)}, bf16[128,1024]{1,0:T(8,128)(2,1)S(1)}, u32[]{:S(2)}, u32[]{:S(2)}) collective-permute-start(bf16[128,1024]{1,0:T(8,128)(2,1)S(1)} %get-tuple-element.435), channel_id=1, source_target_pairs={{0,2},{1,3},{2,0},{3,1},{4,6},{5,7},{6,4},{7,5},{8,10},{9,11},{10,... | collective-permute-start | bytes 786440 | tf_op jit(solution)/shard_map/ppermute | solution.py:83
  206.1 7.9 %collective-permute-start.77 = (bf16[4,128,256]{2,1,0:T(8,128)(2,1)S(1)}, bf16[4,128,256]{2,1,0:T(8,128)(2,1)S(1)}, u32[]{:S(2)}, u32[]{:S(2)}) collective-permute-start(bf16[4,128,256]{2,1,0:T(8,128)(2,1)S(1)} %get-tuple-element.448), channel_id=1, source_target_pairs={{0,4},{4,0},{8,12},{12,8},{16,20},{20,16},{24,28},{28,24},{1,5},{5... | collective-permute-start | bytes 786440 | tf_op jit(solution)/shard_map/ppermute | solution.py:314
  212.7 11.2 %collective-permute-start.74 = (bf16[1,128,768]{2,1,0:T(8,128)(2,1)S(1)}, bf16[1,128,768]{2,1,0:T(8,128)(2,1)S(1)}, u32[]{:S(2)}, u32[]{:S(2)}) collective-permute-start(bf16[1,128,768]{2,1,0:T(8,128)(2,1)S(1)} %get-tuple-element.440), channel_id=1, source_target_pairs={{0,16},{4,20},{8,24},{12,28},{16,0},{20,4},{24,8},{28,12},{1,17},{... | collective-permute-start | bytes 589832 | tf_op jit(solution)/shard_map/ppermute | solution.py:314
  214.1 9.9 %collective-permute-start.78 = (bf16[2,128,256]{2,1,0:T(8,128)(2,1)S(1)}, bf16[2,128,256]{2,1,0:T(8,128)(2,1)S(1)}, u32[]{:S(2)}, u32[]{:S(2)}) collective-permute-start(bf16[2,128,256]{2,1,0:T(8,128)(2,1)S(1)} %shard_map.285), channel_id=1, source_target_pairs={{0,8},{4,12},{8,0},{12,4},{16,24},{20,28},{24,16},{28,20},{1,9},{5... | collective-permute-start | bytes 393224 | tf_op jit(solution)/shard_map/ppermute | solution.py:314
  (78 other events, 636.8 us)

commit v2 on v1

--- a/solution.py
+++ b/solution.py
@@ -116,10 +116,12 @@
     return pieces
 
 
-def trade(near, far):
+def trade(near, far, *earlier):
     count = 2 * near.shape[0]
     if count == 4:
         got = ctx_swap(far, 2)
+        if earlier:
+            got = after(got, *earlier)
         return [(near, 0), (ctx_swap(near, 1), 1), (got, 0), (ctx_swap(got, 1), 1)]
     pieces = ctx_exchange([*near, *far])
     return [(piece[None], 0) for piece in pieces]
@@ -906,10 +908,13 @@
 
     if ctx == 4:
         odd = c % 2
-        trio = w_qkv.reshape(w_qkv.shape[0], 3, unit)
-        stays = lax.dynamic_index_in_dim(trio, 2 * odd, 1, keepdims=False)
-        crossed = ctx_swap(lax.dynamic_index_in_dim(trio, 2 - 2 * odd, 1, keepdims=False), 2)
-        beside = ctx_swap(trio[:, 1], 1)
+
+        def third(at):
+            return lax.dynamic_slice_in_dim(w_qkv, at * unit, unit, 1)
+
+        stays = third(2 * odd)
+        crossed = ctx_swap(third(2 - 2 * odd), 2)
+        beside = ctx_swap(w_qkv[:, unit : 2 * unit], 1)
         three = jnp.stack([stays, crossed, beside])
         held = [(0, 2, 1), (2, 0, 1), (1, 0, 2), (1, 2, 0)]
         place = [
@@ -1118,7 +1123,7 @@
     result_keep, result_got = scatter_rest(result_keep, result_send)
     up_rows = w_up.shape[0]
     up_out = up.result(piece_shapes(ctx, up_rows, dps * sub // ctx), column_pieces(ctx))
-    up_home = trade(*up_out)
+    up_home = trade(*up_out, grad_out[0])
 
     up_got, result_got = sync([qkv], [a for a, _ in up_home], result_got)
     up_home = [(a, i) for a, (_, i) in zip(up_got, up_home)]

time: 233 us -> 233 us (level)
    unnamed x93 -> x92, local copies, waits for them, and re-layouts: 7.55 us -> 6.37 us
  transfers between devices with their start and end apart: 82 -> 82, of which waited for: 34 -> 33; matrix products, arithmetic and copies ran while one was open for 6% -> 6% of each run, Pallas kernels for 18% -> 18%
where the time goes in v2:
time: 233 us; the launch traced here: 232 us
  waiting for transfers between devices  100 us (43%)
  starting transfers between devices  57.5 us (25%)
  Pallas kernels  50.4 us (22%)
  local copies, waits for them, and re-layouts  15 us (6%)
  other arithmetic  6.96 us (3%)
    ppermute x50, waiting for transfers between devices, ctx_swap(): return lax.ppermute(x, 'ctx', [(i, i ^ bit) for i in range(count)])  55.5 us
    pallas_call x29, Pallas kernels, call(): pl.pallas_call(body, out_shape=[jax.ShapeDtypeStruct(shape, dtype) for sh...  42.3 us
    ppermute x50, starting transfers between devices, ctx_swap(): return lax.ppermute(x, 'ctx', [(i, i ^ bit) for i in range(count)])  23.6 us
    ppermute x17, waiting for transfers between devices, dp_swap(): return lax.ppermute(x, 'dp', [(i, i ^ bit) for i in range(count)])  22.4 us
    ppermute x17, starting transfers between devices, dp_swap(): return lax.ppermute(x, 'dp', [(i, i ^ bit) for i in range(count)])  16.2 us
    ppermute x8, waiting for transfers between devices, ring_y(): lax.ppermute(x, 'dp', [(i, i // y_count * y_count + (i + 1) % y_count) fo...  12.4 us
    ppermute x7, waiting for transfers between devices, ring_z(): lax.ppermute(x, 'dp', [(i, (i + y_count) % count) for i in range(count)])  9.95 us
    ppermute x8, starting transfers between devices, ring_y(): lax.ppermute(x, 'dp', [(i, i // y_count * y_count + (i + 1) % y_count) fo...  9.17 us
  transfers between devices with their start and end apart: 82, of which 33 were waited for; matrix products, arithmetic and copies ran while one was open for 6% of the time, Pallas kernels for 18%

profile of v2, /device:TPU:0, one launch (start us, length us, event | category | flops | bytes accessed | tf_op | source)
XLA Modules:
  0.0 232.1 jit_solution(13835147914085541867)
XLA Ops:
  1.7 3.0 %collective-permute-start = (bf16[128,256]{1,0:T(8,128)(2,1)S(1)}, bf16[128,256]{1,0:T(8,128)(2,1)S(1)}, u32[]{:S(2)}, u32[]{:S(2)}) collective-permute-start(bf16[128,256]{1,0:T(8,128)(2,1)S(1)} %get-tuple-element.507), channel_id=1, source_target_pairs={{0,2},{1,3},{2,0},{3,1},{4,6},{5,7},{6,4},{7,5},{8,10},{9,11},{10,... | collective-permute-start | bytes 196616 | tf_op jit(solution)/shard_map/ppermute | solution.py:83
  9.9 1.6 collective-permute-start.2
  11.5 1.5 collective-permute-start.3
  15.2 3.2 %collective-permute-done.5 = bf16[2,2,128,256]{3,2,1,0:T(8,128)(2,1)S(1)} collective-permute-done((bf16[2,2,128,256]{3,2,1,0:T(8,128)(2,1)S(1)}, bf16[2,2,128,256]{3,2,1,0:T(8,128)(2,1)S(1)}, u32[]{:S(2)}, u32[]{:S(2)}) %collective-permute-start.5) | collective-permute-done | bytes 262176 | tf_op jit(solution)/shard_map/ppermute | solution.py:83
  19.1 4.7 %collective-permute-done.4.refs_7_ = bf16[128,1024]{1,0:T(8,128)(2,1)} collective-permute-done((bf16[128,1024]{1,0:T(8,128)(2,1)S(1)}, bf16[128,1024]{1,0:T(8,128)(2,1)}, u32[]{:S(2)}, u32[]{:S(2)}) %collective-permute-start.4) | collective-permute-done | bytes 262176 | tf_op jit(solution)/shard_map/ppermute | solution.py:83
  24.2 1.8 collective-permute-start.7
  26.1 1.5 collective-permute-start.8
  27.6 2.2 collective-permute-done.9
  34.0 4.0 %collective-permute-done.12.refs_7_ = bf16[128,1024]{1,0:T(8,128)(2,1)S(1)} collective-permute-done((bf16[128,1024]{1,0:T(8,128)(2,1)}, bf16[128,1024]{1,0:T(8,128)(2,1)S(1)}, u32[]{:S(2)}, u32[]{:S(2)}) %collective-permute-start.12) | collective-permute-done | bytes 262176 | tf_op jit(solution)/shard_map/ppermute | solution.py:83
  38.0 1.6 collective-permute-start.13
  39.6 1.5 collective-permute-start.14
  45.3 3.9 %collective-permute-done.15 = bf16[2,128,256]{2,1,0:T(8,128)(2,1)S(1)} collective-permute-done((bf16[2,128,256]{2,1,0:T(8,128)(2,1)S(1)}, bf16[2,128,256]{2,1,0:T(8,128)(2,1)S(1)}, u32[]{:S(2)}, u32[]{:S(2)}) %collective-permute-start.15) | collective-permute-done | bytes 131104 | tf_op jit(solution)/shard_map/ppermute | solution.py:83
  50.0 1.6 collective-permute-start.18
  52.1 1.6 collective-permute-start.20
  58.9 4.3 %collective-permute-done.21 = bf16[2,128,256]{2,1,0:T(8,128)(2,1)} collective-permute-done((bf16[2,128,256]{2,1,0:T(8,128)(2,1)}, bf16[2,128,256]{2,1,0:T(8,128)(2,1)}, u32[]{:S(2)}, u32[]{:S(2)}) %collective-permute-start.21) | collective-permute-done | bytes 131104 | tf_op jit(solution)/shard_map/ppermute | solution.py:83
  63.2 7.1 %collective-permute-done.20.refs_1_ = bf16[128,1024]{1,0:T(8,128)(2,1)} collective-permute-done((bf16[128,1024]{1,0:T(8,128)(2,1)}, bf16[128,1024]{1,0:T(8,128)(2,1)}, u32[]{:S(2)}, u32[]{:S(2)}) %collective-permute-start.20) | collective-permute-done | bytes 262176 | tf_op jit(solution)/shard_map/ppermute | solution.py:177
  70.3 1.6 collective-permute-start.23
  78.3 4.3 %shard_map.258 = (bf16[512,1024]{1,0:T(8,128)(2,1)S(1)}, bf16[512,768]{1,0:T(8,128)(2,1)S(1)}, bf16[512,256]{1,0:T(8,128)(2,1)S(1)}, f32[512,4]{1,0:T(8,128)S(1)...) custom-call(s32[2]{0:T(128)S(1)} %pad_add_fusion.refs_0_, f32[4]{0:T(128)S(1)} %multiply_exponential_fusion.refs_1_, ...), custom_call_target="tpu_custom_call" | custom-call | tf_op jit(solution)/shard_map/pallas_call | solution.py:236
  82.6 1.7 collective-permute-done.23.refs_0_
  88.9 3.8 %collective-permute-done.27.refs_3_ = bf16[2,128,256]{2,1,0:T(8,128)(2,1)S(1)} collective-permute-done((bf16[2,128,256]{2,1,0:T(8,128)(2,1)S(1)}, bf16[2,128,256]{2,1,0:T(8,128)(2,1)S(1)}, u32[]{:S(2)}, u32[]{:S(2)}) %collective-permute-start.27) | collective-permute-done | bytes 131104 | tf_op jit(solution)/shard_map/ppermute | solution.py:83
  97.5 6.0 %collective-permute-done.34.refs_0_ = bf16[2,128,1024]{2,1,0:T(8,128)(2,1)S(1)} collective-permute-done((bf16[2,128,1024]{2,1,0:T(8,128)(2,1)}, bf16[2,128,1024]{2,1,0:T(8,128)(2,1)S(1)}, u32[]{:S(2)}, u32[]{:S(2)}) %collective-permute-start.34) | collective-permute-done | bytes 524320 | tf_op jit(solution)/shard_map/ppermute | solution.py:171
  106.8 5.3 %collective-permute-done.36 = bf16[128,1024]{1,0:T(8,128)(2,1)S(1)} collective-permute-done((bf16[128,1024]{1,0:T(8,128)(2,1)S(1)}, bf16[128,1024]{1,0:T(8,128)(2,1)S(1)}, u32[]{:S(2)}, u32[]{:S(2)}) %collective-permute-start.36) | collective-permute-done | bytes 262176 | tf_op jit(solution)/shard_map/ppermute | solution.py:177
  112.0 2.3 collective-permute-done.37
  115.0 6.1 %shard_map.265 = (bf16[512,1024]{1,0:T(8,128)(2,1)S(1)}, bf16[512,1024]{1,0:T(8,128)(2,1)S(1)}, bf16[512,1024]{1,0:T(8,128)(2,1)S(1)}, f32[512,1024]{1,0:T(8,128...) custom-call(s32[2]{0:T(128)S(1)} %pad_add_fusion.refs_0_, ...), custom_call_target="tpu_custom_call" | custom-call | tf_op jit(solution)/shard_map/pallas_call | solution.py:236
  121.1 2.9 %shard_map.267 = (bf16[512,1024]{1,0:T(8,128)(2,1)S(1)}, f32[1,1024]{1,0:T(1,128)S(1)}, f32[256,1024]{1,0:T(8,128)S(1)}, bf16[256,1024]{1,0:T(8,128)(2,1)S(1)}) custom-call(s32[2]{0:T(128)S(1)} %pad_add_fusion.refs_0_, f32[512,1024]{1,0:T(8,128)S(1)} %get-tuple-element.358.refs_1_, bf16[1024,1024]{1,0:T(8,128)(2,1)S(1)} %get-tuple-element.348.refs_1_.refs_2_, ...), custom_call_target="tpu_custom_call" | custom-call | tf_op jit(solution)/shard_map/pallas_call | solution.py:236
  124.1 1.6 collective-permute-start.41
  128.2 3.6 %shard_map.269 = (bf16[4,128,1024]{2,1,0:T(8,128)(2,1)S(1)}, bf16[2,128,1024]{2,1,0:T(8,128)(2,1)S(1)}, bf16[2,128,1024]{2,1,0:T(8,128)(2,1)S(1)}) custom-call(s32[2]{0:T(128)S(1)} %pad_add_fusion.refs_0_, bf16[512,1024]{1,0:T(8,128)(2,1)S(1)} %get-tuple-element.367.refs_1_, bf16[512,1024]{1,0:T(8,128)(2,1)S(1)} %get-tuple-element.368.refs_2_, ...), custom_call_target="tpu_custom_call" | custom-call | tf_op jit(solution)/shard_map/pallas_call | solution.py:236
  131.9 2.6 %collective-permute-done.44.refs_2_ = bf16[128,1024]{1,0:T(8,128)(2,1)S(1)} collective-permute-done((bf16[128,1024]{1,0:T(8,128)(2,1)S(1)}, bf16[128,1024]{1,0:T(8,128)(2,1)S(1)}, u32[]{:S(2)}, u32[]{:S(2)}) %collective-permute-start.44) | collective-permute-done | bytes 262176 | tf_op jit(solution)/shard_map/ppermute | solution.py:83
  134.5 1.9 shard_map.270
  137.4 4.1 %collective-permute-done.45.refs_9_ = bf16[2,128,256]{2,1,0:T(8,128)(2,1)S(1)} collective-permute-done((bf16[2,128,256]{2,1,0:T(8,128)(2,1)S(1)}, bf16[2,128,256]{2,1,0:T(8,128)(2,1)S(1)}, u32[]{:S(2)}, u32[]{:S(2)}) %collective-permute-start.45) | collective-permute-done | bytes 131104 | tf_op jit(solution)/shard_map/ppermute | solution.py:83
  143.8 6.3 %collective-permute-done.40.refs_12_.refs_2_ = bf16[2,128,1024]{2,1,0:T(8,128)(2,1)S(1)} collective-permute-done((bf16[2,128,1024]{2,1,0:T(8,128)(2,1)S(1)}, bf16[2,128,1024]{2,1,0:T(8,128)(2,1)S(1)}, u32[]{:S(2)}, u32[]{:S(2)}) %collective-permute-start.40) | collective-permute-done | bytes 524320 | tf_op jit(solution)/shard_map/ppermute | solution.py:316
  151.4 6.1 %shard_map.271 = (bf16[512,768]{1,0:T(8,128)(2,1)S(1)}, f32[1,768]{1,0:T(1,128)S(1)}, bf16[512,256]{1,0:T(8,128)(2,1)S(1)}, bf16[512,256]{1,0:T(8,128)(2,1)S(1)}, bf16[512,256]{1,0:T(8,128)(2,1)S(1)}) custom-call(s32[2]{0:T(128)S(1)} %pad_add_fusion.refs_0_, f32[4]{0:T(128)S(1)} %multiply_exponential_fusion.refs_1_, ...), custom_call_target="tpu_custom_call" | custom-call | tf_op jit(solution)/shard_map/pallas_call | solution.py:236
  157.6 2.1 shard_map.272
  159.9 1.5 collective-permute-start.52
  163.6 6.6 %collective-permute-done.58.refs_4_ = bf16[512,256]{1,0:T(8,128)(2,1)S(1)} collective-permute-done((bf16[512,256]{1,0:T(8,128)(2,1)S(1)}, bf16[512,256]{1,0:T(8,128)(2,1)S(1)}, u32[]{:S(2)}, u32[]{:S(2)}) %collective-permute-start.58) | collective-permute-done | bytes 262176 | tf_op jit(solution)/shard_map/ppermute | solution.py:83
  170.8 3.3 %shard_map.277 = (bf16[4,128,768]{2,1,0:T(8,128)(2,1)S(1)}, bf16[4,128,768]{2,1,0:T(8,128)(2,1)S(1)}) custom-call(s32[2]{0:T(128)S(1)} %pad_add_fusion.refs_0_, bf16[512,1024]{1,0:T(8,128)(2,1)S(1)} %get-tuple-element.410.refs_1_, bf16[512,256]{1,0:T(8,128)(2,1)S(1)} %get-tuple-element.411.refs_2_, bf16[512,256]{1,0:T(8,128)(2,1)S(1)} %collective-permute-done.57.refs_3_, ...), custom_call_target="tpu_custom_call" | custom-call | tf_op jit(solution)/shard_map/pallas_call | solution.py:236
  176.5 3.6 %collective-permute-done.51.refs_2_ = bf16[1,128,1024]{2,1,0:T(8,128)(2,1)S(1)} collective-permute-done((bf16[1,128,1024]{2,1,0:T(8,128)(2,1)S(1)}, bf16[1,128,1024]{2,1,0:T(8,128)(2,1)S(1)}, u32[]{:S(2)}, u32[]{:S(2)}) %collective-permute-start.51) | collective-permute-done | bytes 262176 | tf_op jit(solution)/shard_map/ppermute | solution.py:316
  180.1 2.2 collective-permute-done.54.refs_3_
  187.7 5.1 %collective-permute-done.63.refs_2_ = bf16[128,1024]{1,0:T(8,128)(2,1)S(1)} collective-permute-done((bf16[128,1024]{1,0:T(8,128)(2,1)S(1)}, bf16[128,1024]{1,0:T(8,128)(2,1)S(1)}, u32[]{:S(2)}, u32[]{:S(2)}) %collective-permute-start.63) | collective-permute-done | bytes 262176 | tf_op jit(solution)/shard_map/ppermute | solution.py:83
  192.8 2.4 %collective-permute-done.67.refs_7_ = bf16[2,128,256]{2,1,0:T(8,128)(2,1)S(1)} collective-permute-done((bf16[2,128,256]{2,1,0:T(8,128)(2,1)S(1)}, bf16[2,128,256]{2,1,0:T(8,128)(2,1)S(1)}, u32[]{:S(2)}, u32[]{:S(2)}) %collective-permute-start.67) | collective-permute-done | bytes 131104 | tf_op jit(solution)/shard_map/ppermute | solution.py:83
  196.0 3.8 %collective-permute-done.64 = f32[12,1024]{1,0:T(8,128)S(1)} collective-permute-done((f32[12,1024]{1,0:T(8,128)S(1)}, f32[12,1024]{1,0:T(8,128)S(1)}, u32[]{:S(2)}, u32[]{:S(2)}) %collective-permute-start.64) | collective-permute-done | bytes 49184 | tf_op jit(solution)/shard_map/ppermute | solution.py:316
  203.0 2.5 %shard_map.283 = (bf16[4,128,256]{2,1,0:T(8,128)(2,1)S(1)}, bf16[4,128,256]{2,1,0:T(8,128)(2,1)S(1)}) custom-call(s32[2]{0:T(128)S(1)} %pad_add_fusion.refs_0_, bf16[128,1024]{1,0:T(8,128)(2,1)S(1)} %get-tuple-element.436.refs_1_, bf16[128,1024]{1,0:T(8,128)(2,1)S(1)} %collective-permute-done.63.refs_2_, ...), custom_call_target="tpu_custom_call" | custom-call | tf_op jit(solution)/shard_map/pallas_call | solution.py:236
  207.6 4.5 %collective-permute-done.75.refs_3_ = bf16[128,1024]{1,0:T(8,128)(2,1)S(1)} collective-permute-done((bf16[128,1024]{1,0:T(8,128)(2,1)S(1)}, bf16[128,1024]{1,0:T(8,128)(2,1)S(1)}, u32[]{:S(2)}, u32[]{:S(2)}) %collective-permute-start.75) | collective-permute-done | bytes 262176 | tf_op jit(solution)/shard_map/ppermute | solution.py:83
  213.5 1.6 collective-permute-start.78
  216.5 1.6 shard_map.286
  218.2 3.5 %collective-permute-done.79 = f32[12,1024]{1,0:T(8,128)S(1)} collective-permute-done((f32[12,1024]{1,0:T(8,128)S(1)}, f32[12,1024]{1,0:T(8,128)S(1)}, u32[]{:S(2)}, u32[]{:S(2)}) %collective-permute-start.79) | collective-permute-done | bytes 49184 | tf_op jit(solution)/shard_map/ppermute | solution.py:316
  221.7 1.6 collective-permute-done.76.refs_2_
  226.2 1.5 collective-permute-start.81
  (318 shorter events, 77.3 us)
Async XLA Ops:
  9.2 9.2 %collective-permute-start.5 = (bf16[2,2,128,256]{3,2,1,0:T(8,128)(2,1)S(1)}, bf16[2,2,128,256]{3,2,1,0:T(8,128)(2,1)S(1)}, u32[]{:S(2)}, u32[]{:S(2)}) collective-permute-start(bf16[2,2,128,256]{3,2,1,0:T(8,128)(2,1)S(1)} %pad_maximum_fusion.3), channel_id=1, source_target_pairs={{0,2},{1,3},{2,0},{3,1},{4,6},{5,7},{6,4},{7,5},{8,10},{9,11},{10,... | collective-permute-start | bytes 786440 | tf_op jit(solution)/shard_map/ppermute | solution.py:83
  9.9 13.8 %collective-permute-start.2 = (bf16[128,1024]{1,0:T(8,128)(2,1)S(1)}, bf16[128,1024]{1,0:T(8,128)(2,1)}, u32[]{:S(2)}, u32[]{:S(2)}) collective-permute-start(bf16[128,1024]{1,0:T(8,128)(2,1)S(1)} %pad_maximum_fusion.2.refs_0_), channel_id=1, source_target_pairs={{0,8},{4,12},{8,16},{12,20},{16,24},{20,28},{24,0},{28,4},{1,9},{5... | collective-permute-start | bytes 786440 | tf_op jit(solution)/shard_map/ppermute | solution.py:171
  11.5 12.2 %collective-permute-start.3 = (bf16[128,1024]{1,0:T(8,128)(2,1)S(1)}, bf16[128,1024]{1,0:T(8,128)(2,1)S(1)}, u32[]{:S(2)}, u32[]{:S(2)}) collective-permute-start(bf16[128,1024]{1,0:T(8,128)(2,1)S(1)} %pad_maximum_fusion.2.refs_0_), channel_id=1, source_target_pairs={{0,4},{4,0},{8,12},{12,8},{16,20},{20,16},{24,28},{28,24},{1,5},{5... | collective-permute-start | bytes 786440 | tf_op jit(solution)/shard_map/ppermute | solution.py:177
  13.0 10.7 %collective-permute-start.4 = (bf16[128,1024]{1,0:T(8,128)(2,1)S(1)}, bf16[128,1024]{1,0:T(8,128)(2,1)}, u32[]{:S(2)}, u32[]{:S(2)}) collective-permute-start(bf16[128,1024]{1,0:T(8,128)(2,1)S(1)} %get-tuple-element.310.refs_6_), channel_id=1, source_target_pairs={{0,2},{1,3},{2,0},{3,1},{4,6},{5,7},{6,4},{7,5},{8,10},{9,11},{10,... | collective-permute-start | bytes 786440 | tf_op jit(solution)/shard_map/ppermute | solution.py:83
  24.2 13.7 %collective-permute-start.7 = (bf16[128,1024]{1,0:T(8,128)(2,1)}, bf16[128,1024]{1,0:T(8,128)(2,1)S(1)}, u32[]{:S(2)}, u32[]{:S(2)}) collective-permute-start(bf16[128,1024]{1,0:T(8,128)(2,1)} %collective-permute-done.2.refs_0_), channel_id=1, source_target_pairs={{0,8},{4,12},{8,16},{12,20},{16,24},{20,28},{24,0},{28,4},{1,9},{5... | collective-permute-start | bytes 786440 | tf_op jit(solution)/shard_map/ppermute | solution.py:171
  26.1 11.9 %collective-permute-start.8 = (bf16[128,1024]{1,0:T(8,128)(2,1)}, bf16[128,1024]{1,0:T(8,128)(2,1)S(1)}, u32[]{:S(2)}, u32[]{:S(2)}) collective-permute-start(bf16[128,1024]{1,0:T(8,128)(2,1)} %collective-permute-done.2.refs_0_), channel_id=1, source_target_pairs={{0,4},{4,0},{8,12},{12,8},{16,20},{20,16},{24,28},{28,24},{1,5},{5... | collective-permute-start | bytes 786440 | tf_op jit(solution)/shard_map/ppermute | solution.py:177
  29.8 8.1 %collective-permute-start.12 = (bf16[128,1024]{1,0:T(8,128)(2,1)}, bf16[128,1024]{1,0:T(8,128)(2,1)S(1)}, u32[]{:S(2)}, u32[]{:S(2)}) collective-permute-start(bf16[128,1024]{1,0:T(8,128)(2,1)} %convert_element_type.35.refs_6_), channel_id=1, source_target_pairs={{0,2},{1,3},{2,0},{3,1},{4,6},{5,7},{6,4},{7,5},{8,10},{9,11},{10,... | collective-permute-start | bytes 786440 | tf_op jit(solution)/shard_map/ppermute | solution.py:83
  30.1 11.0 %collective-permute-start.6 = (bf16[2,2,128,256]{3,2,1,0:T(8,128)(2,1)S(1)}, bf16[2,2,128,256]{3,2,1,0:T(8,128)(2,1)S(1)}, u32[]{:S(2)}, u32[]{:S(2)}) collective-permute-start(bf16[2,2,128,256]{3,2,1,0:T(8,128)(2,1)S(1)} %pad_maximum_fusion.4), channel_id=1, source_target_pairs={{0,1},{1,0},{2,3},{3,2},{4,5},{5,4},{6,7},{7,6},{8,9},{9,8},{10,11... | collective-permute-start | bytes 786440 | tf_op jit(solution)/shard_map/ppermute | solution.py:83
  38.0 11.2 %collective-permute-start.13 = (bf16[128,1024]{1,0:T(8,128)(2,1)S(1)}, bf16[128,1024]{1,0:T(8,128)(2,1)}, u32[]{:S(2)}, u32[]{:S(2)}) collective-permute-start(bf16[128,1024]{1,0:T(8,128)(2,1)S(1)} %collective-permute-done.7.refs_0_), channel_id=1, source_target_pairs={{0,8},{4,12},{8,16},{12,20},{16,24},{20,28},{24,0},{28,4},{1,9},{5... | collective-permute-start | bytes 786440 | tf_op jit(solution)/shard_map/ppermute | solution.py:171
  39.6 9.5 %collective-permute-start.14 = (bf16[128,1024]{1,0:T(8,128)(2,1)S(1)}, bf16[128,1024]{1,0:T(8,128)(2,1)S(1)}, u32[]{:S(2)}, u32[]{:S(2)}) collective-permute-start(bf16[128,1024]{1,0:T(8,128)(2,1)S(1)} %collective-permute-done.7.refs_0_), channel_id=1, source_target_pairs={{0,4},{4,0},{8,12},{12,8},{16,20},{20,16},{24,28},{28,24},{1,5},{5... | collective-permute-start | bytes 786440 | tf_op jit(solution)/shard_map/ppermute | solution.py:177
  50.0 20.3 %collective-permute-start.18 = (bf16[2,128,1024]{2,1,0:T(8,128)(2,1)}, bf16[2,128,1024]{2,1,0:T(8,128)(2,1)}, u32[]{:S(2)}, u32[]{:S(2)}) collective-permute-start(bf16[2,128,1024]{2,1,0:T(8,128)(2,1)} %pad_maximum_fusion.refs_0_), channel_id=1, source_target_pairs={{0,8},{4,12},{8,16},{12,20},{16,24},{20,28},{24,0},{28,4},{1,9},{5... | collective-permute-start | bytes 1572872 | tf_op jit(solution)/shard_map/ppermute | solution.py:171
  51.6 18.7 %collective-permute-start.19 = (bf16[2,128,1024]{2,1,0:T(8,128)(2,1)}, bf16[2,128,1024]{2,1,0:T(8,128)(2,1)}, u32[]{:S(2)}, u32[]{:S(2)}) collective-permute-start(bf16[2,128,1024]{2,1,0:T(8,128)(2,1)} %pad_maximum_fusion.refs_0_), channel_id=1, source_target_pairs={{0,4},{4,0},{8,12},{12,8},{16,20},{20,16},{24,28},{28,24},{1,5},{5... | collective-permute-start | bytes 1572872 | tf_op jit(solution)/shard_map/ppermute | solution.py:177
  52.1 18.2 %collective-permute-start.20 = (bf16[128,1024]{1,0:T(8,128)(2,1)}, bf16[128,1024]{1,0:T(8,128)(2,1)}, u32[]{:S(2)}, u32[]{:S(2)}) collective-permute-start(bf16[128,1024]{1,0:T(8,128)(2,1)} %collective-permute-done.13.refs_0_), channel_id=1, source_target_pairs={{0,4},{4,0},{8,12},{12,8},{16,20},{20,16},{24,28},{28,24},{1,5},{5... | collective-permute-start | bytes 786440 | tf_op jit(solution)/shard_map/ppermute | solution.py:177
  53.7 16.6 %collective-permute-start.22 = (bf16[128,1024]{1,0:T(8,128)(2,1)S(1)}, bf16[128,1024]{1,0:T(8,128)(2,1)}, u32[]{:S(2)}, u32[]{:S(2)}) collective-permute-start(bf16[128,1024]{1,0:T(8,128)(2,1)S(1)} %copy-done.5), channel_id=1, source_target_pairs={{0,2},{1,3},{2,0},{3,1},{4,6},{5,7},{6,4},{7,5},{8,10},{9,11},{10,... | collective-permute-start | bytes 786440 | tf_op jit(solution)/shard_map/ppermute | solution.py:83
  54.9 8.3 %collective-permute-start.21 = (bf16[2,128,256]{2,1,0:T(8,128)(2,1)}, bf16[2,128,256]{2,1,0:T(8,128)(2,1)}, u32[]{:S(2)}, u32[]{:S(2)}) collective-permute-start(bf16[2,128,256]{2,1,0:T(8,128)(2,1)} %pad_maximum_fusion.12), channel_id=1, source_target_pairs={{0,2},{1,3},{2,0},{3,1},{4,6},{5,7},{6,4},{7,5},{8,10},{9,11},{10,... | collective-permute-start | bytes 393224 | tf_op jit(solution)/shard_map/ppermute | solution.py:83
  70.3 14.0 %collective-permute-start.23 = (bf16[2,128,1024]{2,1,0:T(8,128)(2,1)}, bf16[2,128,1024]{2,1,0:T(8,128)(2,1)}, u32[]{:S(2)}, u32[]{:S(2)}) collective-permute-start(bf16[2,128,1024]{2,1,0:T(8,128)(2,1)} %collective-permute-done.18.refs_0_), channel_id=1, source_target_pairs={{0,8},{4,12},{8,16},{12,20},{16,24},{20,28},{24,0},{28,4},{1,9},{5... | collective-permute-start | bytes 1572872 | tf_op jit(solution)/shard_map/ppermute | solution.py:171
  71.9 12.4 %collective-permute-start.24 = (bf16[2,128,1024]{2,1,0:T(8,128)(2,1)}, bf16[2,128,1024]{2,1,0:T(8,128)(2,1)}, u32[]{:S(2)}, u32[]{:S(2)}) collective-permute-start(bf16[2,128,1024]{2,1,0:T(8,128)(2,1)} %collective-permute-done.18.refs_0_), channel_id=1, source_target_pairs={{0,4},{4,0},{8,12},{12,8},{16,20},{20,16},{24,28},{28,24},{1,5},{5... | collective-permute-start | bytes 1572872 | tf_op jit(solution)/shard_map/ppermute | solution.py:177
  74.8 7.8 %collective-permute-start.25 = (bf16[2,128,256]{2,1,0:T(8,128)(2,1)}, bf16[2,128,256]{2,1,0:T(8,128)(2,1)}, u32[]{:S(2)}, u32[]{:S(2)}) collective-permute-start(bf16[2,128,256]{2,1,0:T(8,128)(2,1)} %pad_maximum_fusion.13), channel_id=1, source_target_pairs={{0,2},{1,3},{2,0},{3,1},{4,6},{5,7},{6,4},{7,5},{8,10},{9,11},{10,... | collective-permute-start | bytes 393224 | tf_op jit(solution)/shard_map/ppermute | solution.py:83
  76.9 12.0 %collective-permute-start.29 = (bf16[1024,256]{1,0:T(8,128)(2,1)S(1)}, bf16[1024,256]{1,0:T(8,128)(2,1)S(1)}, u32[]{:S(2)}, u32[]{:S(2)}) collective-permute-start(bf16[1024,256]{1,0:T(8,128)(2,1)S(1)} %get-tuple-element.326.refs_5_.refs_7_), channel_id=1, source_target_pairs={{0,1},{1,0},{2,3},{3,2},{4,5},{5,4},{6,7},{7,6},{8,9},{9,8},{10,11... | collective-permute-start | bytes 1572872 | tf_op jit(solution)/shard_map/ppermute | solution.py:83
  87.4 16.0 %collective-permute-start.34 = (bf16[2,128,1024]{2,1,0:T(8,128)(2,1)}, bf16[2,128,1024]{2,1,0:T(8,128)(2,1)S(1)}, u32[]{:S(2)}, u32[]{:S(2)}) collective-permute-start(bf16[2,128,1024]{2,1,0:T(8,128)(2,1)} %collective-permute-done.23.refs_0_), channel_id=1, source_target_pairs={{0,8},{4,12},{8,16},{12,20},{16,24},{20,28},{24,0},{28,4},{1,9},{5... | collective-permute-start | bytes 1572872 | tf_op jit(solution)/shard_map/ppermute | solution.py:171
  87.4 16.0 %collective-permute-start.35 = (bf16[2,128,1024]{2,1,0:T(8,128)(2,1)}, bf16[2,128,1024]{2,1,0:T(8,128)(2,1)S(1)}, u32[]{:S(2)}, u32[]{:S(2)}) collective-permute-start(bf16[2,128,1024]{2,1,0:T(8,128)(2,1)} %collective-permute-done.23.refs_0_), channel_id=1, source_target_pairs={{0,4},{4,0},{8,12},{12,8},{16,20},{20,16},{24,28},{28,24},{1,5},{5... | collective-permute-start | bytes 1572872 | tf_op jit(solution)/shard_map/ppermute | solution.py:177
  95.5 8.6 %collective-permute-start.31 = (bf16[128,1024]{1,0:T(8,128)(2,1)S(1)}, bf16[128,1024]{1,0:T(8,128)(2,1)S(1)}, u32[]{:S(2)}, u32[]{:S(2)}) collective-permute-start(bf16[128,1024]{1,0:T(8,128)(2,1)S(1)} %get-tuple-element.349.refs_3_), channel_id=1, source_target_pairs={{0,2},{1,3},{2,0},{3,1},{4,6},{5,7},{6,4},{7,5},{8,10},{9,11},{10,... | collective-permute-start | bytes 786440 | tf_op jit(solution)/shard_map/ppermute | solution.py:83
  104.2 7.8 %collective-permute-start.36 = (bf16[128,1024]{1,0:T(8,128)(2,1)S(1)}, bf16[128,1024]{1,0:T(8,128)(2,1)S(1)}, u32[]{:S(2)}, u32[]{:S(2)}) collective-permute-start(bf16[128,1024]{1,0:T(8,128)(2,1)S(1)} %slice_bitcast_fusion.1), channel_id=1, source_target_pairs={{0,4},{4,0},{8,12},{12,8},{16,20},{20,16},{24,28},{28,24},{1,5},{5... | collective-permute-start | bytes 786440 | tf_op jit(solution)/shard_map/ppermute | solution.py:177
  104.8 9.5 %collective-permute-start.37 = (bf16[128,1024]{1,0:T(8,128)(2,1)S(1)}, bf16[128,1024]{1,0:T(8,128)(2,1)S(1)}, u32[]{:S(2)}, u32[]{:S(2)}) collective-permute-start(bf16[128,1024]{1,0:T(8,128)(2,1)S(1)} %slice_bitcast_fusion), channel_id=1, source_target_pairs={{0,8},{4,12},{8,16},{12,20},{16,24},{20,28},{24,0},{28,4},{1,9},{5... | collective-permute-start | bytes 786440 | tf_op jit(solution)/shard_map/ppermute | solution.py:171
  105.0 9.9 %collective-permute-start.38 = (bf16[128,1024]{1,0:T(8,128)(2,1)S(1)}, bf16[128,1024]{1,0:T(8,128)(2,1)S(1)}, u32[]{:S(2)}, u32[]{:S(2)}) collective-permute-start(bf16[128,1024]{1,0:T(8,128)(2,1)S(1)} %get-tuple-element.349.refs_3_), channel_id=1, source_target_pairs={{0,1},{1,0},{2,3},{3,2},{4,5},{5,4},{6,7},{7,6},{8,9},{9,8},{10,11... | collective-permute-start | bytes 786440 | tf_op jit(solution)/shard_map/ppermute | solution.py:83
  105.1 9.9 %collective-permute-start.39 = (bf16[128,1024]{1,0:T(8,128)(2,1)S(1)}, bf16[128,1024]{1,0:T(8,128)(2,1)S(1)}, u32[]{:S(2)}, u32[]{:S(2)}) collective-permute-start(bf16[128,1024]{1,0:T(8,128)(2,1)S(1)} %collective-permute-done.31.refs_4_), channel_id=1, source_target_pairs={{0,1},{1,0},{2,3},{3,2},{4,5},{5,4},{6,7},{7,6},{8,9},{9,8},{10,11... | collective-permute-start | bytes 786440 | tf_op jit(solution)/shard_map/ppermute | solution.py:83
  124.1 19.5 %collective-permute-start.41 = (bf16[2,128,1024]{2,1,0:T(8,128)(2,1)S(1)}, bf16[2,128,1024]{2,1,0:T(8,128)(2,1)S(1)}, u32[]{:S(2)}, u32[]{:S(2)}) collective-permute-start(bf16[2,128,1024]{2,1,0:T(8,128)(2,1)S(1)} %get-tuple-element.357), channel_id=1, source_target_pairs={{0,4},{4,0},{8,12},{12,8},{16,20},{20,16},{24,28},{28,24},{1,5},{5... | collective-permute-start | bytes 1572872 | tf_op jit(solution)/shard_map/ppermute | solution.py:316
  126.1 8.4 %collective-permute-start.44 = (bf16[128,1024]{1,0:T(8,128)(2,1)S(1)}, bf16[128,1024]{1,0:T(8,128)(2,1)S(1)}, u32[]{:S(2)}, u32[]{:S(2)}) collective-permute-start(bf16[128,1024]{1,0:T(8,128)(2,1)S(1)} %get-tuple-element.364.refs_3_), channel_id=1, source_target_pairs={{0,2},{1,3},{2,0},{3,1},{4,6},{5,7},{6,4},{7,5},{8,10},{9,11},{10,... | collective-permute-start | bytes 786440 | tf_op jit(solution)/shard_map/ppermute | solution.py:83
  127.0 23.1 %collective-permute-start.40 = (bf16[2,128,1024]{2,1,0:T(8,128)(2,1)S(1)}, bf16[2,128,1024]{2,1,0:T(8,128)(2,1)S(1)}, u32[]{:S(2)}, u32[]{:S(2)}) collective-permute-start(bf16[2,128,1024]{2,1,0:T(8,128)(2,1)S(1)} %get-tuple-element.356), channel_id=1, source_target_pairs={{0,4},{4,0},{8,12},{12,8},{16,20},{20,16},{24,28},{28,24},{1,5},{5... | collective-permute-start | bytes 1572872 | tf_op jit(solution)/shard_map/ppermute | solution.py:316
  137.4 12.7 %collective-permute-start.49 = (bf16[2,128,256]{2,1,0:T(8,128)(2,1)S(1)}, bf16[2,128,256]{2,1,0:T(8,128)(2,1)S(1)}, u32[]{:S(2)}, u32[]{:S(2)}) collective-permute-start(bf16[2,128,256]{2,1,0:T(8,128)(2,1)S(1)} %get-tuple-element.378.refs_7_), channel_id=1, source_target_pairs={{0,1},{1,0},{2,3},{3,2},{4,5},{5,4},{6,7},{7,6},{8,9},{9,8},{10,11... | collective-permute-start | bytes 393224 | tf_op jit(solution)/shard_map/ppermute | solution.py:83
  141.5 9.1 %collective-permute-start.47 = (bf16[2,128,256]{2,1,0:T(8,128)(2,1)S(1)}, bf16[2,128,256]{2,1,0:T(8,128)(2,1)S(1)}, u32[]{:S(2)}, u32[]{:S(2)}) collective-permute-start(bf16[2,128,256]{2,1,0:T(8,128)(2,1)S(1)} %get-tuple-element.374), channel_id=1, source_target_pairs={{0,2},{1,3},{2,0},{3,1},{4,6},{5,7},{6,4},{7,5},{8,10},{9,11},{10,... | collective-permute-start | bytes 393224 | tf_op jit(solution)/shard_map/ppermute | solution.py:83
  142.3 19.2 %collective-permute-start.53 = (bf16[2,128,1024]{2,1,0:T(8,128)(2,1)S(1)}, bf16[2,128,1024]{2,1,0:T(8,128)(2,1)S(1)}, u32[]{:S(2)}, u32[]{:S(2)}) collective-permute-start(bf16[2,128,1024]{2,1,0:T(8,128)(2,1)S(1)} %get-tuple-element.395), channel_id=1, source_target_pairs={{0,4},{4,0},{8,12},{12,8},{16,20},{20,16},{24,28},{28,24},{1,5},{5... | collective-permute-start | bytes 1572872 | tf_op jit(solution)/shard_map/ppermute | solution.py:316
  143.7 18.3 %collective-permute-start.42 = (bf16[2,128,1024]{2,1,0:T(8,128)(2,1)S(1)}, bf16[2,128,1024]{2,1,0:T(8,128)(2,1)S(1)}, u32[]{:S(2)}, u32[]{:S(2)}) collective-permute-start(bf16[2,128,1024]{2,1,0:T(8,128)(2,1)S(1)} %shard_map.266.refs_11_), channel_id=1, source_target_pairs={{0,8},{4,12},{8,0},{12,4},{16,24},{20,28},{24,16},{28,20},{1,9},{5... | collective-permute-start | bytes 1572872 | tf_op jit(solution)/shard_map/ppermute | solution.py:316
  159.9 15.1 %collective-permute-start.52 = (bf16[2,128,1024]{2,1,0:T(8,128)(2,1)S(1)}, bf16[2,128,1024]{2,1,0:T(8,128)(2,1)S(1)}, u32[]{:S(2)}, u32[]{:S(2)}) collective-permute-start(bf16[2,128,1024]{2,1,0:T(8,128)(2,1)S(1)} %get-tuple-element.394), channel_id=1, source_target_pairs={{0,4},{4,0},{8,12},{12,8},{16,20},{20,16},{24,28},{28,24},{1,5},{5... | collective-permute-start | bytes 1572872 | tf_op jit(solution)/shard_map/ppermute | solution.py:316
  162.0 8.3 %collective-permute-start.58 = (bf16[512,256]{1,0:T(8,128)(2,1)S(1)}, bf16[512,256]{1,0:T(8,128)(2,1)S(1)}, u32[]{:S(2)}, u32[]{:S(2)}) collective-permute-start(bf16[512,256]{1,0:T(8,128)(2,1)S(1)} %get-tuple-element.402), channel_id=1, source_target_pairs={{0,2},{1,3},{2,0},{3,1},{4,6},{5,7},{6,4},{7,5},{8,10},{9,11},{10,... | collective-permute-start | bytes 786440 | tf_op jit(solution)/shard_map/ppermute | solution.py:83
  162.7 19.6 %collective-permute-start.54 = (bf16[2,128,1024]{2,1,0:T(8,128)(2,1)S(1)}, bf16[2,128,1024]{2,1,0:T(8,128)(2,1)S(1)}, u32[]{:S(2)}, u32[]{:S(2)}) collective-permute-start(bf16[2,128,1024]{2,1,0:T(8,128)(2,1)S(1)} %shard_map.274), channel_id=1, source_target_pairs={{0,8},{4,12},{8,0},{12,4},{16,24},{20,28},{24,16},{28,20},{1,9},{5... | collective-permute-start | bytes 1572872 | tf_op jit(solution)/shard_map/ppermute | solution.py:316
  163.0 17.1 %collective-permute-start.51 = (bf16[1,128,1024]{2,1,0:T(8,128)(2,1)S(1)}, bf16[1,128,1024]{2,1,0:T(8,128)(2,1)S(1)}, u32[]{:S(2)}, u32[]{:S(2)}) collective-permute-start(bf16[1,128,1024]{2,1,0:T(8,128)(2,1)S(1)} %get-tuple-element.393), channel_id=1, source_target_pairs={{0,16},{4,20},{8,24},{12,28},{16,0},{20,4},{24,8},{28,12},{1,17},{... | collective-permute-start | bytes 786440 | tf_op jit(solution)/shard_map/ppermute | solution.py:316
  170.2 12.1 %collective-permute-start.59 = (bf16[128,1024]{1,0:T(8,128)(2,1)S(1)}, bf16[128,1024]{1,0:T(8,128)(2,1)S(1)}, u32[]{:S(2)}, u32[]{:S(2)}) collective-permute-start(bf16[128,1024]{1,0:T(8,128)(2,1)S(1)} %get-tuple-element.403), channel_id=1, source_target_pairs={{0,2},{1,3},{2,0},{3,1},{4,6},{5,7},{6,4},{7,5},{8,10},{9,11},{10,... | collective-permute-start | bytes 786440 | tf_op jit(solution)/shard_map/ppermute | solution.py:83
  174.1 26.0 %collective-permute-start.62 = (bf16[4,128,768]{2,1,0:T(8,128)(2,1)S(1)}, bf16[4,128,768]{2,1,0:T(8,128)(2,1)S(1)}, u32[]{:S(2)}, u32[]{:S(2)}) collective-permute-start(bf16[4,128,768]{2,1,0:T(8,128)(2,1)S(1)} %get-tuple-element.415), channel_id=1, source_target_pairs={{0,4},{4,0},{8,12},{12,8},{16,20},{20,16},{24,28},{28,24},{1,5},{5... | collective-permute-start | bytes 2359304 | tf_op jit(solution)/shard_map/ppermute | solution.py:316
  183.6 11.6 %collective-permute-start.65 = (bf16[256,1024]{1,0:T(8,128)(2,1)S(1)}, bf16[256,1024]{1,0:T(8,128)(2,1)S(1)}, u32[]{:S(2)}, u32[]{:S(2)}) collective-permute-start(bf16[256,1024]{1,0:T(8,128)(2,1)S(1)} %get-tuple-element.421), channel_id=1, source_target_pairs={{0,1},{1,0},{2,3},{3,2},{4,5},{5,4},{6,7},{7,6},{8,9},{9,8},{10,11... | collective-permute-start | bytes 1572872 | tf_op jit(solution)/shard_map/ppermute | solution.py:83
  183.7 9.2 %collective-permute-start.63 = (bf16[128,1024]{1,0:T(8,128)(2,1)S(1)}, bf16[128,1024]{1,0:T(8,128)(2,1)S(1)}, u32[]{:S(2)}, u32[]{:S(2)}) collective-permute-start(bf16[128,1024]{1,0:T(8,128)(2,1)S(1)} %get-tuple-element.436.refs_1_), channel_id=1, source_target_pairs={{0,2},{1,3},{2,0},{3,1},{4,6},{5,7},{6,4},{7,5},{8,10},{9,11},{10,... | collective-permute-start | bytes 786440 | tf_op jit(solution)/shard_map/ppermute | solution.py:83
  185.3 9.9 %collective-permute-start.67 = (bf16[2,128,256]{2,1,0:T(8,128)(2,1)S(1)}, bf16[2,128,256]{2,1,0:T(8,128)(2,1)S(1)}, u32[]{:S(2)}, u32[]{:S(2)}) collective-permute-start(bf16[2,128,256]{2,1,0:T(8,128)(2,1)S(1)} %get-tuple-element.427), channel_id=1, source_target_pairs={{0,2},{1,3},{2,0},{3,1},{4,6},{5,7},{6,4},{7,5},{8,10},{9,11},{10,... | collective-permute-start | bytes 393224 | tf_op jit(solution)/shard_map/ppermute | solution.py:83
  186.4 13.7 %collective-permute-start.61 = (bf16[1,128,1024]{2,1,0:T(8,128)(2,1)S(1)}, bf16[1,128,1024]{2,1,0:T(8,128)(2,1)S(1)}, u32[]{:S(2)}, u32[]{:S(2)}) collective-permute-start(bf16[1,128,1024]{2,1,0:T(8,128)(2,1)S(1)} %get-tuple-element.409), channel_id=1, source_target_pairs={{0,16},{4,20},{8,24},{12,28},{16,0},{20,4},{24,8},{28,12},{1,17},{... | collective-permute-start | bytes 786440 | tf_op jit(solution)/shard_map/ppermute | solution.py:316
  200.7 11.3 %collective-permute-start.69 = (bf16[2,128,768]{2,1,0:T(8,128)(2,1)S(1)}, bf16[2,128,768]{2,1,0:T(8,128)(2,1)S(1)}, u32[]{:S(2)}, u32[]{:S(2)}) collective-permute-start(bf16[2,128,768]{2,1,0:T(8,128)(2,1)S(1)} %shard_map.281), channel_id=1, source_target_pairs={{0,8},{4,12},{8,0},{12,4},{16,24},{20,28},{24,16},{28,20},{1,9},{5... | collective-permute-start | bytes 1179656 | tf_op jit(solution)/shard_map/ppermute | solution.py:316
  202.1 9.9 %collective-permute-start.75 = (bf16[128,1024]{1,0:T(8,128)(2,1)S(1)}, bf16[128,1024]{1,0:T(8,128)(2,1)S(1)}, u32[]{:S(2)}, u32[]{:S(2)}) collective-permute-start(bf16[128,1024]{1,0:T(8,128)(2,1)S(1)} %get-tuple-element.444), channel_id=1, source_target_pairs={{0,2},{1,3},{2,0},{3,1},{4,6},{5,7},{6,4},{7,5},{8,10},{9,11},{10,... | collective-permute-start | bytes 786440 | tf_op jit(solution)/shard_map/ppermute | solution.py:83
  205.6 7.9 %collective-permute-start.77 = (bf16[4,128,256]{2,1,0:T(8,128)(2,1)S(1)}, bf16[4,128,256]{2,1,0:T(8,128)(2,1)S(1)}, u32[]{:S(2)}, u32[]{:S(2)}) collective-permute-start(bf16[4,128,256]{2,1,0:T(8,128)(2,1)S(1)} %get-tuple-element.450), channel_id=1, source_target_pairs={{0,4},{4,0},{8,12},{12,8},{16,20},{20,16},{24,28},{28,24},{1,5},{5... | collective-permute-start | bytes 786440 | tf_op jit(solution)/shard_map/ppermute | solution.py:316
  212.2 11.2 %collective-permute-start.76 = (bf16[1,128,768]{2,1,0:T(8,128)(2,1)S(1)}, bf16[1,128,768]{2,1,0:T(8,128)(2,1)S(1)}, u32[]{:S(2)}, u32[]{:S(2)}) collective-permute-start(bf16[1,128,768]{2,1,0:T(8,128)(2,1)S(1)} %get-tuple-element.449), channel_id=1, source_target_pairs={{0,16},{4,20},{8,24},{12,28},{16,0},{20,4},{24,8},{28,12},{1,17},{... | collective-permute-start | bytes 589832 | tf_op jit(solution)/shard_map/ppermute | solution.py:316
  213.5 9.9 %collective-permute-start.78 = (bf16[2,128,256]{2,1,0:T(8,128)(2,1)S(1)}, bf16[2,128,256]{2,1,0:T(8,128)(2,1)S(1)}, u32[]{:S(2)}, u32[]{:S(2)}) collective-permute-start(bf16[2,128,256]{2,1,0:T(8,128)(2,1)S(1)} %shard_map.285), channel_id=1, source_target_pairs={{0,8},{4,12},{8,0},{12,4},{16,24},{20,28},{24,16},{28,20},{1,9},{5... | collective-permute-start | bytes 393224 | tf_op jit(solution)/shard_map/ppermute | solution.py:316
  (78 other events, 637.6 us)
